TPU v7x, 128 devices: a whole 4x4x4 slice. The times are simulated.
128 devices in a mesh: face: 16 (over x, z), rep: 8 (over y, core).
Axes of the slice: x: 4, y: 4, z: 4, core: 2. Of those that a mesh axis runs over, the one named last changes fastest.
Arguments:
- fields: bfloat16 [8, 32, 32, 32, 256], P('rep', 'face'), may hold values from -6 to 6
- out_grad: bfloat16 [8, 32, 32, 32, 256], P('rep', 'face'), may hold values from -6 to 6
- kernel: bfloat16 [7, 7, 256], replicated, may hold values from -0.875 to 0.875
- ln_gain: float32 [256], replicated, may hold values from 0.1 to 1.9
- ln_shift: float32 [256], replicated, may hold values from -3 to 3
- w_in: bfloat16 [256, 1024], replicated, may hold values from -0.375 to 0.375
- w_out: bfloat16 [1024, 256], replicated, may hold values from -0.1875 to 0.1875
- edge_tile: int32 [32, 4], replicated, may hold values from 0 to 31, as said below
- edge_code: int32 [32, 4], replicated, may hold values from 0 to 7, as said below
- corner_tile: int32 [32, 4], replicated, may hold values from 0 to 31, as said below
- corner_code: int32 [32, 4], replicated, may hold values from 0 to 7, as said below
Outputs:
- result: bfloat16 [8, 32, 32, 32, 256], P('rep', 'face')
- grad_input: bfloat16 [8, 32, 32, 32, 256], P('rep', 'face')
- grad_kernel: float32 [7, 7, 256], replicated
- grad_gain: float32 [256], replicated
- grad_shift: float32 [256], replicated
- grad_win: float32 [256, 1024], replicated
- grad_wout: float32 [1024, 256], replicated
Inputs may be any that keep to these rules, and one draw needn't show every extreme that they name: `edge_tile`: the tiles form 32/4 faces of 4 slabs each, numbered face-major (tile = 4 face + slab). The north and south neighbours of a slab inside a face are the slabs beside it in the same face. The first slab's north neighbour is the last slab of the face given by a permutation of faces. Every slab's east neighbour is the same slab of the face given by a second permutation, and its west neighbour is given by the inverse. Which faces are paired is redrawn with the seed. `edge_code`: code % 4 names the neighbour's edge and is (e + 2) % 4 for edge e. code // 4 is 1 where the direction along the edge is reversed, which happens only across face seams and is the same from both sides of a seam. `corner_tile`: the top-left and top-right corners are owned by the north neighbour of the west and east neighbours; the bottom-right and bottom-left corners by their south neighbours. `corner_code`: code % 4 names the owner's corner and is (k + 2) % 4 for corner k. code // 4 is 1 where the block is transposed, which happens only where the corner lies across an east or west face seam that reverses.
All inputs are finite; a program needn't handle non-finite values.
Results may differ from a plain program's by a relative error of at most 0.0056.
Values may be sent and summed in bfloat16 or wider, within the bound.
No kernel may reach another device: no remote copies, remote signals or barrier semaphores. Data moves between devices by JAX's collectives and lax.ppermute only.
A program may use at most 128 MiB of HBM per device.

v0:
```python
import math

import jax
import jax.numpy as jnp
from jax import lax
from jax.sharding import PartitionSpec as P


def for_sending(array):
    return jax.tree.map(lambda a: a.astype(jnp.bfloat16) if a.dtype == jnp.float32 else a, array)


def bands_of(patches):
    edge_bands = jnp.stack([jnp.rot90(patches, e, axes=(1, 2))[:, 0:3] for e in range(4)], axis=1)
    corner_blocks = jnp.stack(
        [jnp.rot90(patches, e, axes=(1, 2))[:, 0:3, 0:3] for e in range(4)], axis=1
    )
    return (edge_bands, corner_blocks)


def edge_pieces(fetched, code_table):
    is_flipped = (code_table // 4)[:, :, None, None, None] == 1
    return jnp.where(is_flipped, fetched[:, :, :, ::-1], fetched)[:, :, ::-1]


def corner_pieces(fetched, code_table):
    is_transposed = (code_table // 4)[:, :, None, None, None] == 1
    return jnp.where(is_transposed, jnp.swapaxes(fetched, 2, 3), fetched)[:, :, ::-1, ::-1]


def edge_return(rim_bands, code_table):
    is_flipped = (code_table // 4)[:, :, None, None, None] == 1
    restored = rim_bands[:, :, ::-1]
    return jnp.where(is_flipped, restored[:, :, :, ::-1], restored)


def corner_return(rim_bands, code_table):
    is_transposed = (code_table // 4)[:, :, None, None, None] == 1
    restored = rim_bands[:, :, ::-1, ::-1]
    return jnp.where(is_transposed, jnp.swapaxes(restored, 2, 3), restored)


def assemble(patches, edge_halo, corner_halo):
    extent = patches.shape[1]
    padded = jnp.zeros((patches.shape[0], extent + 6, extent + 6, patches.shape[3]), patches.dtype)
    padded = padded.at[:, 3 : extent + 3, 3 : extent + 3].set(patches)
    for e in range(4):
        turned = jnp.rot90(padded, e, axes=(1, 2))
        turned = turned.at[:, 0:3, 3 : extent + 3].set(edge_halo[:, e])
        turned = turned.at[:, 0:3, 0:3].set(corner_halo[:, e])
        padded = jnp.rot90(turned, -e, axes=(1, 2))
    return padded


def split_rims(grad_padded):
    extent = grad_padded.shape[1] - 6
    edge_rims = []
    corner_rims = []
    for e in range(4):
        turned = jnp.rot90(grad_padded, e, axes=(1, 2))
        edge_rims.append(turned[:, 0:3, 3 : extent + 3])
        corner_rims.append(turned[:, 0:3, 0:3])
    interior = grad_padded[:, 3 : extent + 3, 3 : extent + 3]
    return (jnp.stack(edge_rims, axis=1), jnp.stack(corner_rims, axis=1), interior)


def place_rims(running, edge_grads, corner_grads):
    for e in range(4):
        turned = jnp.rot90(running, e, axes=(1, 2))
        turned = turned.at[:, 0:3].add(edge_grads[:, e])
        turned = turned.at[:, 0:3, 0:3].add(corner_grads[:, e])
        running = jnp.rot90(turned, -e, axes=(1, 2))
    return running


def depthwise(padded, kernel):
    extent = padded.shape[1] - 6
    widened = padded.astype(jnp.float32)
    kernel_f = kernel.astype(jnp.float32)
    running = jnp.zeros((padded.shape[0], extent, extent, padded.shape[3]), jnp.float32)
    for a in range(7):
        for b in range(7):
            running = running + kernel_f[a, b] * widened[:, a : a + extent, b : b + extent]
    return running


def kernel_grad(padded, grad_z):
    extent = grad_z.shape[1]
    widened = padded.astype(jnp.float32)
    pieces = []
    for a in range(7):
        for b in range(7):
            pieces.append(
                jnp.sum(grad_z * widened[:, a : a + extent, b : b + extent], axis=(0, 1, 2))
            )
    return jnp.stack(pieces, axis=0).reshape(7, 7, grad_z.shape[3])


def input_grad(grad_z, kernel):
    extent = grad_z.shape[1]
    kernel_f = kernel.astype(jnp.float32)
    padded_grad = jnp.pad(grad_z, ((0, 0), (6, 6), (6, 6), (0, 0)))
    running = jnp.zeros((grad_z.shape[0], extent + 6, extent + 6, grad_z.shape[3]), jnp.float32)
    for a in range(7):
        for b in range(7):
            running = (
                running
                + kernel_f[a, b] * padded_grad[:, 6 - a : 12 - a + extent, 6 - b : 12 - b + extent]
            )
    return running


def gelu_parts(hidden):
    normal_cdf = 0.5 * (1.0 + jax.scipy.special.erf(hidden / math.sqrt(2.0)))
    normal_pdf = jnp.exp(-0.5 * hidden * hidden) / math.sqrt(2.0 * math.pi)
    return (hidden * normal_cdf, normal_cdf + hidden * normal_pdf)


def block(padded, patches, cotangent, kernel, ln_gain, ln_shift, w_in, w_out):
    z_field = depthwise(padded, kernel)
    channels = z_field.shape[3]
    flat_z = z_field.reshape(-1, channels)
    average = jnp.mean(flat_z, axis=1, keepdims=True)
    centered = flat_z - average
    variance = jnp.mean(centered * centered, axis=1, keepdims=True)
    inv_std = lax.rsqrt(variance + 1e-06)
    normed = centered * inv_std
    zn_rows = (normed * ln_gain + ln_shift).astype(jnp.bfloat16)
    hidden = jnp.dot(zn_rows, w_in, preferred_element_type=jnp.float32)
    activ, gelu_slope = gelu_parts(hidden)
    activated = activ.astype(jnp.bfloat16)
    branch_out = jnp.dot(activated, w_out, preferred_element_type=jnp.float32)
    outcome = (patches.reshape(-1, channels).astype(jnp.float32) + branch_out).astype(jnp.bfloat16)
    cot_rows = cotangent.reshape(-1, channels)
    grad_wout = jnp.dot(activated.T, cot_rows, preferred_element_type=jnp.float32)
    grad_act = jnp.dot(cot_rows, w_out.T, preferred_element_type=jnp.float32)
    grad_hidden = (grad_act * gelu_slope).astype(jnp.bfloat16)
    grad_win = jnp.dot(zn_rows.T, grad_hidden, preferred_element_type=jnp.float32)
    grad_normed = jnp.dot(grad_hidden, w_in.T, preferred_element_type=jnp.float32)
    grad_gain = jnp.sum(grad_normed * normed, axis=0)
    grad_shift = jnp.sum(grad_normed, axis=0)
    scaled = grad_normed * ln_gain
    grad_z = inv_std * (
        scaled
        - jnp.mean(scaled, axis=1, keepdims=True)
        - normed * jnp.mean(scaled * normed, axis=1, keepdims=True)
    )
    grad_z = grad_z.reshape(z_field.shape)
    grads = (kernel_grad(padded, grad_z), grad_gain, grad_shift, grad_win, grad_wout)
    return (outcome.reshape(patches.shape), input_grad(grad_z, kernel), grads)


def own_rows(int_table, offset, tile_count):
    return lax.dynamic_slice_in_dim(int_table, offset, tile_count, 0)


def body(
    fields,
    out_grad,
    kernel,
    ln_gain,
    ln_shift,
    w_in,
    w_out,
    edge_tile,
    edge_code,
    corner_tile,
    corner_code,
):
    patches = fields[0]
    cotangent = out_grad[0]
    tile_count = patches.shape[0]
    extent = patches.shape[1]
    offset = lax.axis_index("face") * tile_count
    edge_bands, corner_blocks = bands_of(patches)
    all_edges, all_corners = (
        lax.all_gather(for_sending(edge_bands), "face", axis=0, tiled=True).astype(
            edge_bands.dtype
        ),
        lax.all_gather(for_sending(corner_blocks), "face", axis=0, tiled=True).astype(
            corner_blocks.dtype
        ),
    )
    my_edge_tile = own_rows(edge_tile, offset, tile_count)
    my_edge_code = own_rows(edge_code, offset, tile_count)
    my_corner_tile = own_rows(corner_tile, offset, tile_count)
    my_corner_code = own_rows(corner_code, offset, tile_count)
    edge_src = my_edge_tile * 4 + my_edge_code % 4
    corner_src = my_corner_tile * 4 + my_corner_code % 4
    fetched_edge = jnp.take(all_edges.reshape((-1,) + edge_bands.shape[2:]), edge_src, axis=0)
    fetched_corner = jnp.take(
        all_corners.reshape((-1,) + corner_blocks.shape[2:]), corner_src, axis=0
    )
    padded = assemble(
        patches,
        edge_pieces(fetched_edge, my_edge_code),
        corner_pieces(fetched_corner, my_corner_code),
    )
    outcome, grad_padded, grads = block(
        padded, patches, cotangent, kernel, ln_gain, ln_shift, w_in, w_out
    )
    edge_rims, corner_rims, interior = split_rims(grad_padded)
    back_edge = edge_return(edge_rims, my_edge_code).reshape(tile_count * 4, -1)
    back_corner = corner_return(corner_rims, my_corner_code).reshape(tile_count * 4, -1)
    edge_width = back_edge.shape[1]
    src_edge = edge_src.reshape(-1)
    src_corner = corner_src.reshape(-1)
    slot_ids = jnp.arange(tile_count * 4 * lax.axis_size("face"), dtype=jnp.int32)
    pick_edge = (src_edge[None, :] == slot_ids[:, None]).astype(jnp.float32)
    pick_corner = (src_corner[None, :] == slot_ids[:, None]).astype(jnp.float32)
    received = lax.psum_scatter(
        jnp.concatenate(
            [
                jnp.dot(pick_edge, back_edge, precision=lax.Precision.HIGHEST),
                jnp.dot(pick_corner, back_corner, precision=lax.Precision.HIGHEST),
            ],
            axis=1,
        ).astype(jnp.bfloat16),
        "face",
        scatter_dimension=0,
        tiled=True,
    ).astype(jnp.float32)
    edge_got = received[:, :edge_width]
    corner_got = received[:, edge_width:]
    edge_sums = edge_got.reshape(edge_rims.shape)
    corner_sums = corner_got.reshape(corner_rims.shape)
    running = place_rims(interior + cotangent.astype(jnp.float32), edge_sums, corner_sums)
    summed = lax.psum((grads[0], grads[1], grads[2], grads[3], grads[4]), ("face", "rep"))
    norm_scale = 1.0 / math.sqrt(
        lax.axis_size("rep") * lax.axis_size("face") * tile_count * extent * extent
    )
    return (
        outcome[None],
        running.astype(jnp.bfloat16)[None],
        summed[0] * norm_scale,
        summed[1] * norm_scale,
        summed[2] * norm_scale,
        summed[3] * norm_scale,
        summed[4] * norm_scale,
    )


def solution(mesh):
    return jax.shard_map(
        body,
        mesh=mesh,
        in_specs=(
            P("rep", "face", None, None, None),
            P("rep", "face", None, None, None),
            P(),
            P(),
            P(),
            P(),
            P(),
            P(),
            P(),
            P(),
            P(),
        ),
        out_specs=(
            P("rep", "face", None, None, None),
            P("rep", "face", None, None, None),
            P(),
            P(),
            P(),
            P(),
            P(),
        ),
        check_vma=False,
    )
```

profile of v0, /device:TPU:1, one launch (start us, length us, event | category | flops | bytes accessed | tf_op | source)
XLA Modules:
  0.0 518.2 jit_solution(10431707495431030444)
XLA Ops:
  7.2 1.9 copy.513
  9.2 1.8 rev.98
  11.5 1.0 slice_bitcast_fusion.4
  18.9 24.5 %all_gather.7 = bf16[32,4,3,3,256]{4,2,3,0,1:T(4,128)(2,1)S(1)} all-gather(bf16[2,4,3,3,256]{4,2,3,0,1:T(4,128)(2,1)S(1)} %pad_maximum_fusion.4), channel_id=1, replica_groups=mesh['face'=16,'rep'=8] {'face'}, dimensions={0}, use_global_device_ids=true | all-gather | bytes 626688 | tf_op jit(solution)/shard_map/all_gather | solution.py:180
  43.4 1.2 copy.425
  44.7 1.7 gather_fusion.1
  52.2 27.5 %all-gather.2.cloned.1.call-done = bf16[32,4,3,32,256]{4,3,2,1,0:T(8,128)(2,1)} async-done(((bf16[2,4,3,32,256]{4,3,2,1,0:T(8,128)(2,1)}), bf16[32,4,3,32,256]{4,3,2,1,0:T(8,128)(2,1)}) %all-gather.2.cloned.1.call-update) | async-done | bytes 6291472 | tf_op jit(solution)/shard_map/all_gather | solution.py:177
  79.7 3.5 gather_fusion
  83.2 1.5 broadcast_select_fusion.1
  84.7 1.7 rev.99
  86.5 1.1 broadcast_select_fusion
  88.8 2.1 bitcast_select_fusion.1
  90.8 2.8 scatter.31
  93.8 1.3 reverse_bitcast_fusion.2
  95.1 1.2 rev.100
  96.8 2.8 bitcast_select_fusion.3
  99.6 2.9 scatter.35
  102.5 1.4 scatter.36
  103.9 5.3 %rev.101 = bf16[2,38,38,256]{3,1,2,0:T(8,128)(2,1)S(1)} reverse(bf16[2,38,38,256]{3,1,2,0:T(8,128)(2,1)} %bitcast.270), dimensions={1} | reverse | bytes 2957312 | tf_op jit(solution)/shard_map/jit(rot90)/jit(_flip)/rev | solution.py:48
  109.2 2.0 bitcast_select_fusion
  111.2 2.8 scatter.39
  114.2 4.0 rev.102
  118.2 5.3 %rev.103 = bf16[2,38,38,256]{3,2,1,0:T(8,128)(2,1)S(1)} reverse(bf16[2,38,38,256]{3,2,1,0:T(8,128)(2,1)} %bitcast.271), dimensions={2} | reverse | bytes 2957312 | tf_op jit(solution)/shard_map/jit(rot90)/jit(_flip)/rev | solution.py:48
  123.5 1.9 bitcast_select_fusion.2
  125.4 1.5 scatter.41
  127.2 4.0 rev.104
  131.6 1.6 convert_bitcast_fusion
  133.6 16.2 %fusion.124 = (f32[2,32,32]{1,2,0:T(8,128)S(1)}, f32[2,32,32,256]{3,1,2,0:T(8,128)S(1)}) fusion(f32[2,38,38,256]{3,1,2,0:T(8,128)S(1)} %convert_bitcast_fusion, f32[256]{0:T(256)S(1)} %bitcast.325, f32[256]{0:T(256)S(1)} %bitcast.323, f32[256]{0:T(256)S(1)} %bitcast.321, f32[256]{0:T(256)S(1)} %bitcast.319, f32[256]{0:T(256)S(1)} %bitcast.317, ...), kind=kLoop, calls=%fused_computation.319 | loop fusion | flops 51378176 | bytes 104915968 | tf_op jit(solution)/shard_map/reduce_sum | solution.py:123
  149.8 1.2 copy.355
  152.9 3.9 multiply_convert_fusion
  156.8 4.5 fusion.5
  161.3 2.3 fusion.135
  163.5 2.5 multiply_reduce_fusion
  166.1 1.4 subtract_multiply_fusion
  167.5 1.4 copy-done.4
  169.0 23.0 %fusion.99 = f32[2,38,38,256]{3,2,1,0:T(8,128)S(1)} fusion(f32[2,32,32,256]{3,2,1,0:T(8,128)S(1)} %bitcast.257, f32[256]{0:T(256)S(1)} %bitcast.326, f32[256]{0:T(256)S(1)} %bitcast.324, f32[256]{0:T(256)S(1)} %bitcast.322, f32[256]{0:T(256)S(1)} %bitcast.320, f32[256]{0:T(256)S(1)} %bitcast.318, f32[256]{0:T(256)S(1)} %bitcast.316, f32[256]{0:T(256)S(1)} %bitcast.314, ...), kind=kLoop, calls=%fused_computation.156 | loop fusion | flops 71714816 | bytes 5104640 | tf_op jit(solution)/shard_map/add | solution.py:107
  192.0 2.6 copy.512
  194.6 3.8 rev.105
  199.2 1.1 slice_bitcast_fusion
  201.1 1.0 slice.1558
  202.3 4.7 fusion.136
  209.6 7.1 %convolution_convert_fusion = bf16[128,24576]{1,0:T(8,128)(2,1)} fusion(f32[8,24576]{1,0:T(8,128)S(1)} %reshape.818, s32[8]{0:T(128)S(1)} %copy-done.78), kind=kOutput, calls=%fused_computation.51 | convolution fusion | flops 305136640 | bytes 7077920 | tf_op jit(solution)/shard_map/dot_general | solution.py:214
  216.6 6.1 %pad_maximum_fusion = bf16[128,26880]{1,0:T(8,128)(2,1)} fusion(bf16[128,2304]{1,0:T(8,128)(2,1)S(1)} %convolution_convert_fusion.1, bf16[128,24576]{1,0:T(8,128)(2,1)} %convolution_convert_fusion), kind=kLoop, calls=%fused_computation.61 | loop fusion | flops 13762560 | bytes 13762560 | tf_op jit(solution)/shard_map/concatenate | solution.py:212
  224.7 6.2 %multiply_reduce_fusion.37 = (f32[256]{0:T(256)S(1)}, f32[256]{0:T(256)S(1)}, f32[256]{0:T(256)S(1)}, f32[256]{0:T(256)S(1)}, f32[256]{0:T(256)S(1)}, /*index=5*...) fusion(f32[2,38,38,256]{3,1,2,0:T(8,128)S(1)} %copy-done.3, ...), kind=kLoop, calls=%fused_computation.204 | loop fusion | flops 13628160 | bytes 29373440 | tf_op jit(solution)/shard_map/reduce_sum | solution.py:94
  230.9 6.1 %multiply_reduce_fusion.19 = (f32[256]{0:T(256)S(1)}, f32[256]{0:T(256)S(1)}, f32[256]{0:T(256)S(1)}, f32[256]{0:T(256)S(1)}, f32[256]{0:T(256)S(1)}, /*index=5*...) fusion(f32[2,38,38,256]{3,1,2,0:T(8,128)S(1)} %copy-done.3, ...), kind=kLoop, calls=%fused_computation.186 | loop fusion | flops 18869760 | bytes 39864320 | tf_op jit(solution)/shard_map/reduce_sum | solution.py:94
  237.0 6.1 %multiply_reduce_fusion.1 = (f32[256]{0:T(256)S(1)}, f32[256]{0:T(256)S(1)}, f32[256]{0:T(256)S(1)}, f32[256]{0:T(256)S(1)}, f32[256]{0:T(256)S(1)}, /*index=5*/...) fusion(f32[2,38,38,256]{3,1,2,0:T(8,128)S(1)} %copy-done.3, ...), kind=kLoop, calls=%fused_computation.168 | loop fusion | flops 18869760 | bytes 39864320 | tf_op jit(solution)/shard_map/reduce_sum | solution.py:94
  243.3 66.0 %all-reduce.3 = (f32[7,7,256]{2,1,0:T(8,128)S(1)}, f32[256]{0:T(256)S(1)}, f32[256]{0:T(256)S(1)}) all-reduce(f32[7,7,256]{2,1,0:T(8,128)S(1)} %reshape.830, f32[256]{0:T(256)S(1)} %copy-done.76, f32[256]{0:T(256)S(1)} %copy-done.77), channel_id=1, replica_groups=mesh['face'=16,'rep'=8] {'face','rep'}, use_global_device_ids=true, to_apply=%region_55.56 | all-reduce | flops 13056 | bytes 104448 | tf_op jit(solution)/shard_map/psum | solution.py:228
  311.1 2.6 slice_add_fusion
  314.7 3.3 fusion.103
  318.0 40.8 %all-reduce.10.cloned.1.call-done = (f32[256,1024]{1,0:T(8,128)}, f32[1024,256]{1,0:T(8,128)}) async-done(((f32[256,1024]{1,0:T(8,128)}, f32[1024,256]{1,0:T(8,128)}), (f32[256,1024]{1,0:T(8,128)}, f32[1024,256]{1,0:T(8,128)})) %all-reduce.10.cloned.1.call-update) | async-done | bytes 2097168 | tf_op jit(solution)/shard_map/psum | solution.py:228
  358.7 2.4 broadcast_multiply_fusion.1
  361.1 1.0 broadcast_multiply_fusion
  362.2 126.0 %all-reduce.8.cloned.1.call-done = bf16[128,26880]{1,0:T(8,128)(2,1)} async-done(((bf16[128,26880]{1,0:T(8,128)(2,1)}), bf16[128,26880]{1,0:T(8,128)(2,1)}) %all-reduce.8.cloned.1.call-update) | async-done | bytes 6881296
  488.2 1.1 dynamic-slice_convert_fusion
  490.0 2.0 rev.109
  493.2 1.1 fusion.107
  494.4 1.6 scatter-add.30
  496.2 1.5 rev.110
  498.5 1.5 scatter-add.35
  500.0 2.4 rev.111
  502.5 1.1 rev.112
  503.8 3.9 scatter-add.36
  507.7 1.4 scatter-add.39
  509.1 2.3 fusion.105
  (277 shorter events, 28.2 us)
Async XLA Ops:
  7.2 145.7 %copy-start = (bf16[256,1024]{1,0:T(8,128)(2,1)S(1)}, bf16[256,1024]{1,0:T(8,128)(2,1)}, u32[]{:S(2)}) copy-start(bf16[256,1024]{1,0:T(8,128)(2,1)} %param.50) | copy-start | bytes 1572868
  7.2 72.5 %all-gather.2.cloned.1.call-start = ((), (), s32[]{:S(2)}) async-start(), calls=%async_computation | async-start | bytes 6684672 | tf_op jit(solution)/shard_map/all_gather | solution.py:177
  11.0 2.9 copy-start.71
  11.0 2.9 copy-start.72
  11.0 4.9 copy-start.73
  11.0 5.0 copy-start.74
  13.8 344.9 %all-reduce.10.cloned.1.call-start = ((), (), s32[]{:S(2)}) async-start(), calls=%async_computation.2 | async-start | bytes 4194304 | tf_op jit(solution)/shard_map/psum | solution.py:228
  16.1 30.4 %copy-start.66 = (pred[2,4]{0,1:T(4,128)(4,1)}, pred[2,4]{0,1:T(4,128)(4,1)S(1)}, u32[]{:S(2)}) copy-start(pred[2,4]{0,1:T(4,128)(4,1)S(1)} %get-tuple-element.346) | copy-start | bytes 28
  18.1 31.4 %copy-start.80 = (s32[4]{0:T(128)S(1)}, s32[4]{0:T(128)}, u32[]{:S(2)}) copy-start(s32[4]{0:T(128)} %constant.474.clone.1) | copy-start | bytes 52
  18.1 32.1 %copy-start.16 = (bf16[7,7,256]{2,1,0:T(8,128)(2,1)S(1)}, bf16[7,7,256]{2,1,0:T(8,128)(2,1)}, u32[]{:S(2)}) copy-start(bf16[7,7,256]{2,1,0:T(8,128)(2,1)} %param.47) | copy-start | bytes 75268
  87.6 6.0 %copy-start.18 = (bf16[2,3,3,256]{3,1,2,0:T(4,128)(2,1)S(1)}, bf16[2,3,3,256]{3,1,2,0:T(4,128)(2,1)}, u32[]{:S(2)}) copy-start(bf16[2,3,3,256]{3,1,2,0:T(4,128)(2,1)} %copy.349) | copy-start | bytes 27652
  95.1 7.4 %copy-start.17 = (bf16[2,1,3,3,256]{4,3,2,0,1:T(4,128)(2,1)S(1)}, bf16[2,1,3,3,256]{4,3,2,0,1:T(4,128)(2,1)}, u32[]{:S(2)}) copy-start(bf16[2,1,3,3,256]{4,3,2,0,1:T(4,128)(2,1)} %slice.1249) | copy-start | bytes 27652
  118.2 5.3 %copy-start.14 = (bf16[2,1,3,32,256]{4,3,2,1,0:T(8,128)(2,1)S(1)}, bf16[2,1,3,32,256]{4,3,2,1,0:T(8,128)(2,1)}, u32[]{:S(2)}) copy-start(bf16[2,1,3,32,256]{4,3,2,1,0:T(8,128)(2,1)} %get-tuple-element.287) | copy-start | bytes 294916
  131.2 2.1 copy-start.23
  131.2 2.1 copy-start.24
  131.2 2.1 copy-start.25
  131.2 2.1 copy-start.26
  131.3 2.1 copy-start.27
  131.3 2.1 copy-start.28
  131.3 2.1 copy-start.29
  131.3 2.1 copy-start.30
  131.3 2.1 copy-start.31
  131.3 2.1 copy-start.32
  131.3 2.1 copy-start.33
  131.3 2.1 copy-start.34
  131.3 2.1 copy-start.35
  131.3 2.1 copy-start.36
  131.4 2.1 copy-start.37
  131.4 2.1 copy-start.38
  131.4 2.1 copy-start.39
  131.4 2.1 copy-start.40
  131.4 2.1 copy-start.41
  131.4 2.1 copy-start.42
  131.4 2.1 copy-start.43
  131.4 2.1 copy-start.44
  131.4 2.1 copy-start.45
  131.4 2.1 copy-start.46
  131.5 2.1 copy-start.47
  131.5 2.1 copy-start.48
  131.5 2.1 copy-start.49
  131.5 2.1 copy-start.50
  131.5 2.1 copy-start.51
  133.2 16.6 %copy-start.2 = (f32[2,38,38,256]{3,1,2,0:T(8,128)}, f32[2,38,38,256]{3,1,2,0:T(8,128)S(1)}, u32[]{:S(2)}) copy-start(f32[2,38,38,256]{3,1,2,0:T(8,128)S(1)} %convert_bitcast_fusion) | copy-start | bytes 8871940
  152.9 3.9 copy-start.11
  152.9 3.9 copy-start.81
  166.0 2.9 copy-start.58
  166.0 2.9 copy-start.59
  166.0 2.9 copy-start.60
  166.0 2.9 copy-start.61
  166.1 2.9 copy-start.62
  166.1 2.9 copy-start.63
  166.1 2.9 copy-start.64
  166.1 2.9 copy-start.65
  192.0 6.5 %copy-start.6 = (f32[2,38,38,256]{3,2,1,0:T(8,128)}, f32[2,38,38,256]{3,2,1,0:T(8,128)S(1)}, u32[]{:S(2)}) copy-start(f32[2,38,38,256]{3,2,1,0:T(8,128)S(1)} %fusion.99) | copy-start | bytes 8871940
  202.3 5.3 %copy-start.67 = (pred[2,4]{0,1:T(4,128)(4,1)S(1)}, pred[2,4]{0,1:T(4,128)(4,1)}, u32[]{:S(2)}) copy-start(pred[2,4]{0,1:T(4,128)(4,1)} %copy-done.66) | copy-start | bytes 28
  208.5 279.7 %all-reduce.8.cloned.1.call-start = ((), (), s32[]{:S(2)}) async-start(), calls=%async_computation.1 | async-start | bytes 13762560
  224.7 6.2 %copy-start.5 = (f32[2048,256]{1,0:T(8,128)S(1)}, f32[2048,256]{1,0:T(8,128)}, u32[]{:S(2)}) copy-start(f32[2048,256]{1,0:T(8,128)} %copy-done.4) | copy-start | bytes 6291460
  236.9 6.3 %copy-start.76 = (f32[256]{0:T(256)S(1)}, f32[256]{0:T(256)}, u32[]{:S(2)}) copy-start(f32[256]{0:T(256)} %get-tuple-element.260) | copy-start | bytes 3076
  237.0 6.3 %copy-start.77 = (f32[256]{0:T(256)S(1)}, f32[256]{0:T(256)}, u32[]{:S(2)}) copy-start(f32[256]{0:T(256)} %get-tuple-element.263) | copy-start | bytes 3076
  311.1 3.3 copy-start.7
  311.1 3.6 copy-start.10
  358.7 2.4 copy-start.12
  492.1 2.3 copy-start.8
  502.5 8.9 %copy-start.1 = (bf16[256,1024]{1,0:T(8,128)(2,1)S(1)}, bf16[256,1024]{1,0:T(8,128)(2,1)}, u32[]{:S(2)}) copy-start(bf16[256,1024]{1,0:T(8,128)(2,1)} %param.50) | copy-start | bytes 1572868
  (22 other events, 35.2 us)
Sparse Core Ops, SparseCore 0:
  14.0 65.7 all-gather.1
  208.6 150.0 all-reduce.9
  362.2 125.9 all-reduce.7
where the time goes:
time: 523 us; the launch traced here: 518 us
  waiting for transfers between devices  194 us (37%)
  local copies, waits for them, and re-layouts  94.8 us (18%)
  other arithmetic  93.2 us (18%)
  blocking collectives  90.5 us (17%)
  matrix products  28.8 us (6%)
  between operations  16.3 us (3%)
    unnamed x4, waiting for transfers between devices  126 us
    psum x1, blocking collectives, body(): lax.psum((grads[0], grads[1], grads[2], grads[3], grads[4]), ('face', 're...  66 us
    psum x1, waiting for transfers between devices, body(): lax.psum((grads[0], grads[1], grads[2], grads[3], grads[4]), ('face', 're...  40.8 us
    all_gather x1, waiting for transfers between devices, body(): lax.all_gather(for_sending(edge_bands), 'face', axis=0, tiled=True)  27.5 us
    all_gather x1, blocking collectives, body(): lax.all_gather(for_sending(corner_blocks), 'face', axis=0, tiled=True)  24.5 us
    add x1, other arithmetic, input_grad(): running + kernel_f[a, b] * padded_grad[:, 6 - a:12 - a + extent, 6 - b:12...  23 us
    reduce_sum x3, other arithmetic, kernel_grad(): jnp.sum(grad_z * widened[:, a:a + extent, b:b + extent], axis=(0, 1, 2))  18.4 us
    reduce_sum x1, other arithmetic, block(): average = jnp.mean(flat_z, axis=1, keepdims=True)  16.2 us
  transfers between devices with their start and end apart: 3, of which 3 were waited for; matrix products, arithmetic and copies ran while one was open for 11% of the time, Pallas kernels for 0%

commit v1 on v0

--- a/solution.py
+++ b/solution.py
@@ -150,8 +150,44 @@
     return (outcome.reshape(patches.shape), input_grad(grad_z, kernel), grads)
 
 
-def own_rows(int_table, offset, tile_count):
-    return lax.dynamic_slice_in_dim(int_table, offset, tile_count, 0)
+def chunked(bands, corners):
+    parts = lax.axis_size("face")
+    tiles, channels = bands.shape[0], bands.shape[-1]
+    span = bands.shape[3] // parts
+    band_part = bands.reshape(tiles * 4, 3, parts, span, channels)
+    band_part = band_part.transpose(2, 0, 3, 1, 4).reshape(parts, tiles * 4, span * 3 * channels)
+    corner_part = corners.reshape(tiles * 4, 9, channels).transpose(1, 0, 2)
+    corner_part = jnp.pad(corner_part, ((0, parts - 9), (0, 0), (0, channels)))
+    return jnp.concatenate([band_part, corner_part], axis=2)
+
+
+def unchunked(parts_array, tiles):
+    parts, _, width = parts_array.shape
+    channels = width // 8
+    span = 6 // 3
+    band_part = parts_array[:, :, : 6 * channels].reshape(parts, tiles * 4, span, 3, channels)
+    bands = band_part.transpose(1, 3, 0, 2, 4).reshape(tiles, 4, 3, parts * span, channels)
+    corners = parts_array[:9, :, 6 * channels : 7 * channels].transpose(1, 0, 2)
+    return bands, corners.reshape(tiles, 4, 3, 3, channels)
+
+
+def swap_face(array):
+    return lax.all_to_all(array, "face", 0, 0, tiled=True)
+
+
+def routed(bands, corners, pick_edge, pick_corner):
+    tiles = bands.shape[0]
+    sent = swap_face(chunked(bands.astype(jnp.bfloat16), corners.astype(jnp.bfloat16)))
+    width = sent.shape[2] * 6 // 8
+    rows = sent.reshape(-1, sent.shape[2])
+    chosen = jnp.concatenate(
+        [
+            jnp.dot(pick_edge, rows[:, :width], preferred_element_type=jnp.float32),
+            jnp.dot(pick_corner, rows[:, width:], preferred_element_type=jnp.float32),
+        ],
+        axis=1,
+    ).astype(jnp.bfloat16)
+    return unchunked(swap_face(chosen.reshape(sent.shape)), tiles)
 
 
 def body(
@@ -171,26 +207,20 @@
     cotangent = out_grad[0]
     tile_count = patches.shape[0]
     extent = patches.shape[1]
+    channels = patches.shape[-1]
+    faces = lax.axis_size("face")
+    reps = lax.axis_size("rep")
     offset = lax.axis_index("face") * tile_count
+    slot_ids = jnp.arange(tile_count * 4 * faces, dtype=jnp.int32)
+    edge_src = (edge_tile * 4 + edge_code % 4).reshape(-1)
+    corner_src = (corner_tile * 4 + corner_code % 4).reshape(-1)
+    pick_edge = (edge_src[:, None] == slot_ids[None, :]).astype(jnp.bfloat16)
+    pick_corner = (corner_src[:, None] == slot_ids[None, :]).astype(jnp.bfloat16)
+    my_edge_code = lax.dynamic_slice_in_dim(edge_code, offset, tile_count, 0)
+    my_corner_code = lax.dynamic_slice_in_dim(corner_code, offset, tile_count, 0)
+
     edge_bands, corner_blocks = bands_of(patches)
-    all_edges, all_corners = (
-        lax.all_gather(for_sending(edge_bands), "face", axis=0, tiled=True).astype(
-            edge_bands.dtype
-        ),
-        lax.all_gather(for_sending(corner_blocks), "face", axis=0, tiled=True).astype(
-            corner_blocks.dtype
-        ),
-    )
-    my_edge_tile = own_rows(edge_tile, offset, tile_count)
-    my_edge_code = own_rows(edge_code, offset, tile_count)
-    my_corner_tile = own_rows(corner_tile, offset, tile_count)
-    my_corner_code = own_rows(corner_code, offset, tile_count)
-    edge_src = my_edge_tile * 4 + my_edge_code % 4
-    corner_src = my_corner_tile * 4 + my_corner_code % 4
-    fetched_edge = jnp.take(all_edges.reshape((-1,) + edge_bands.shape[2:]), edge_src, axis=0)
-    fetched_corner = jnp.take(
-        all_corners.reshape((-1,) + corner_blocks.shape[2:]), corner_src, axis=0
-    )
+    fetched_edge, fetched_corner = routed(edge_bands, corner_blocks, pick_edge, pick_corner)
     padded = assemble(
         patches,
         edge_pieces(fetched_edge, my_edge_code),
@@ -200,43 +230,50 @@
         padded, patches, cotangent, kernel, ln_gain, ln_shift, w_in, w_out
     )
     edge_rims, corner_rims, interior = split_rims(grad_padded)
-    back_edge = edge_return(edge_rims, my_edge_code).reshape(tile_count * 4, -1)
-    back_corner = corner_return(corner_rims, my_corner_code).reshape(tile_count * 4, -1)
-    edge_width = back_edge.shape[1]
-    src_edge = edge_src.reshape(-1)
-    src_corner = corner_src.reshape(-1)
-    slot_ids = jnp.arange(tile_count * 4 * lax.axis_size("face"), dtype=jnp.int32)
-    pick_edge = (src_edge[None, :] == slot_ids[:, None]).astype(jnp.float32)
-    pick_corner = (src_corner[None, :] == slot_ids[:, None]).astype(jnp.float32)
-    received = lax.psum_scatter(
-        jnp.concatenate(
-            [
-                jnp.dot(pick_edge, back_edge, precision=lax.Precision.HIGHEST),
-                jnp.dot(pick_corner, back_corner, precision=lax.Precision.HIGHEST),
-            ],
-            axis=1,
-        ).astype(jnp.bfloat16),
-        "face",
-        scatter_dimension=0,
-        tiled=True,
-    ).astype(jnp.float32)
-    edge_got = received[:, :edge_width]
-    corner_got = received[:, edge_width:]
-    edge_sums = edge_got.reshape(edge_rims.shape)
-    corner_sums = corner_got.reshape(corner_rims.shape)
-    running = place_rims(interior + cotangent.astype(jnp.float32), edge_sums, corner_sums)
-    summed = lax.psum((grads[0], grads[1], grads[2], grads[3], grads[4]), ("face", "rep"))
-    norm_scale = 1.0 / math.sqrt(
-        lax.axis_size("rep") * lax.axis_size("face") * tile_count * extent * extent
-    )
+    edge_sums, corner_sums = routed(
+        edge_return(edge_rims, my_edge_code),
+        corner_return(corner_rims, my_corner_code),
+        pick_edge.T,
+        pick_corner.T,
+    )
+    running = place_rims(
+        interior + cotangent.astype(jnp.float32),
+        edge_sums.astype(jnp.float32),
+        corner_sums.astype(jnp.float32),
+    )
+    norm_scale = 1.0 / math.sqrt(reps * faces * tile_count * extent * extent)
+
+    devices = faces * reps
+    both = ("face", "rep")
+    wide = jnp.concatenate(
+        [grads[3].reshape(devices, -1, channels), grads[4].reshape(devices, -1, channels)], axis=1
+    ).astype(jnp.bfloat16)
+    wide = lax.all_to_all(wide, both, 0, 0, tiled=True)
+    wide = jnp.sum(wide.astype(jnp.float32), axis=0, keepdims=True) * norm_scale
+    wide = jnp.broadcast_to(wide.astype(jnp.bfloat16), (devices,) + wide.shape[1:])
+    wide = lax.all_to_all(wide, both, 0, 0, tiled=True).astype(jnp.float32)
+    half = wide.shape[1] // 2
+    grad_win = wide[:, :half].reshape(grads[3].shape)
+    grad_wout = wide[:, half:].reshape(grads[4].shape)
+
+    small = jnp.concatenate(
+        [grads[0].reshape(-1, channels), grads[1][None], grads[2][None]], axis=0
+    )
+    count = small.shape[0]
+    small = jnp.pad(small, ((0, -count % 16), (0, 0))).astype(jnp.bfloat16)
+    for axis, size in (("face", faces), ("rep", reps)):
+        small = jnp.broadcast_to(small.astype(jnp.bfloat16)[None], (size,) + small.shape)
+        small = lax.all_to_all(small, axis, 0, 0, tiled=True)
+        small = jnp.sum(small.astype(jnp.float32), axis=0)
+    small = small * norm_scale
     return (
         outcome[None],
         running.astype(jnp.bfloat16)[None],
-        summed[0] * norm_scale,
-        summed[1] * norm_scale,
-        summed[2] * norm_scale,
-        summed[3] * norm_scale,
-        summed[4] * norm_scale,
+        small[: count - 2].reshape(kernel.shape),
+        small[count - 2],
+        small[count - 1],
+        grad_win,
+        grad_wout,
     )
 
 

time: 523 us -> 384 us (0.73)
  waiting for transfers between devices: 194 us -> 37.7 us
  blocking collectives: 90.5 us -> 0 us
  other arithmetic: 93.2 us -> 154 us
  starting transfers between devices: 0.12 us -> 51.1 us
  between operations: 16.3 us -> 3.52 us
  local copies, waits for them, and re-layouts: 94.8 us -> 106 us
    unnamed x4 -> x0, waiting for transfers between devices: 126 us -> none
    psum x1 -> x0, blocking collectives: 66 us -> none  [body(): lax.psum((grads[0], grads[1], grads[2], grads[3], grads[4]), ('face', 're...]
    all_to_all x0 -> x8, starting transfers between devices: none -> 51.1 us  [the longest x4 22.4 us: swap_face(): return lax.all_to_all(array, 'face', 0, 0, tiled=True)]
    psum x1 -> x0, waiting for transfers between devices: 40.8 us -> none  [body(): lax.psum((grads[0], grads[1], grads[2], grads[3], grads[4]), ('face', 're...]
    add x1, other arithmetic: 23 us -> 63 us  [input_grad(): running + kernel_f[a, b] * padded_grad[:, 6 - a:12 - a + extent, 6 - b:12...]
    all_to_all x0 -> x8, waiting for transfers between devices: none -> 37.7 us  [the longest x4 21.7 us: swap_face(): return lax.all_to_all(array, 'face', 0, 0, tiled=True)]
    all_gather x1 -> x0, waiting for transfers between devices: 27.5 us -> none  [body(): lax.all_gather(for_sending(edge_bands), 'face', axis=0, tiled=True)]
    all_gather x1 -> x0, blocking collectives: 24.5 us -> none  [body(): lax.all_gather(for_sending(corner_blocks), 'face', axis=0, tiled=True)]
  transfers between devices with their start and end apart: 3 -> 8, of which waited for: 3 -> 6; matrix products, arithmetic and copies ran while one was open for 11% -> 16% of each run, Pallas kernels for 0% -> 0%
where the time goes in v1:
time: 384 us; the launch traced here: 378 us
  other arithmetic  154 us (40%)
  local copies, waits for them, and re-layouts  106 us (28%)
  starting transfers between devices  51.1 us (13%)
  waiting for transfers between devices  37.7 us (10%)
  matrix products  25.2 us (7%)
    add x1, other arithmetic, input_grad(): running + kernel_f[a, b] * padded_grad[:, 6 - a:12 - a + extent, 6 - b:12...  63 us
    transpose x1, other arithmetic, split_rims(): turned = jnp.rot90(grad_padded, e, axes=(1, 2))  23.3 us
    all_to_all x4, starting transfers between devices, swap_face(): return lax.all_to_all(array, 'face', 0, 0, tiled=True)  22.4 us
    all_to_all x4, waiting for transfers between devices, swap_face(): return lax.all_to_all(array, 'face', 0, 0, tiled=True)  21.7 us
    reduce_sum x3, other arithmetic, kernel_grad(): jnp.sum(grad_z * widened[:, a:a + extent, b:b + extent], axis=(0, 1, 2))  20.3 us
    reduce_sum x1, other arithmetic, block(): average = jnp.mean(flat_z, axis=1, keepdims=True)  16.2 us
    all_to_all x2, starting transfers between devices, body(): small = lax.all_to_all(small, axis, 0, 0, tiled=True)  16.1 us
    rev x3, local copies, waits for them, and re-layouts, assemble(): turned = jnp.rot90(padded, e, axes=(1, 2))  11.8 us
  transfers between devices with their start and end apart: 8, of which 6 were waited for; matrix products, arithmetic and copies ran while one was open for 16% of the time, Pallas kernels for 0%

profile of v1, /device:TPU:1, one launch (start us, length us, event | category | flops | bytes accessed | tf_op | source)
XLA Modules:
  0.0 377.9 jit_solution(16620778768918316759)
XLA Ops:
  2.5 1.8 copy.892
  4.5 1.8 rev.98
  11.2 8.4 %all-to-all-start = ((bf16[16,8,2048]{2,1,0:T(8,128)(2,1)}), bf16[16,8,2048]{2,1,0:T(8,128)(2,1)S(1)}, u32[]{:S(2)}, u32[]{:S(2)}) async-start(bf16[16,8,2048]{2,1,0:T(8,128)(2,1)} %fusion.123), calls=%async_computation | async-start | bytes 1048576 | tf_op jit(solution)/shard_map/all_to_all | solution.py:175
  22.2 7.8 %all-to-all-done = bf16[16,8,2048]{2,1,0:T(8,128)(2,1)S(1)} async-done(((bf16[16,8,2048]{2,1,0:T(8,128)(2,1)}), bf16[16,8,2048]{2,1,0:T(8,128)(2,1)S(1)}, u32[]{:S(2)}, u32[]{:S(2)}) %all-to-all-start) | async-done | bytes 524320 | tf_op jit(solution)/shard_map/all_to_all | solution.py:175
  31.4 4.7 %all-to-all-start.1 = ((bf16[16,8,2048]{2,1,0:T(8,128)(2,1)}), bf16[16,8,2048]{2,1,0:T(8,128)(2,1)}, u32[]{:S(2)}, u32[]{:S(2)}) async-start(bf16[16,8,2048]{2,1,0:T(8,128)(2,1)} %pad_maximum_fusion.3), calls=%async_computation.1 | async-start | bytes 1048576 | tf_op jit(solution)/shard_map/all_to_all | solution.py:175
  39.1 6.2 %all-to-all-done.1 = bf16[16,8,2048]{2,1,0:T(8,128)(2,1)} async-done(((bf16[16,8,2048]{2,1,0:T(8,128)(2,1)}), bf16[16,8,2048]{2,1,0:T(8,128)(2,1)}, u32[]{:S(2)}, u32[]{:S(2)}) %all-to-all-start.1) | async-done | bytes 524320 | tf_op jit(solution)/shard_map/all_to_all | solution.py:175
  48.6 1.4 slice_bitcast_fusion.8
  50.0 1.4 reshape.857
  53.0 1.3 slice.1282
  58.2 2.1 bitcast_select_fusion.1
  60.3 2.8 scatter.31
  63.3 1.3 reverse_bitcast_fusion.5
  66.5 2.8 bitcast_select_fusion.3
  69.3 2.9 scatter.35
  72.3 1.4 scatter.36
  73.7 5.3 %rev.101 = bf16[2,38,38,256]{3,1,2,0:T(8,128)(2,1)S(1)} reverse(bf16[2,38,38,256]{3,1,2,0:T(8,128)(2,1)} %bitcast.283), dimensions={1} | reverse | bytes 2957312 | tf_op jit(solution)/shard_map/jit(rot90)/jit(_flip)/rev | solution.py:48
  79.0 2.0 bitcast_select_fusion
  81.0 2.8 scatter.39
  84.0 4.0 %rev.102 = bf16[2,38,38,256]{3,1,2,0:T(8,128)(2,1)} reverse(bf16[2,38,38,256]{3,1,2,0:T(8,128)(2,1)S(1)} %scatter.40), dimensions={1,2} | reverse | bytes 2957312 | tf_op jit(solution)/shard_map/jit(rot90)/jit(_flip)/rev | solution.py:51
  88.0 5.3 %rev.103 = bf16[2,38,38,256]{3,2,1,0:T(8,128)(2,1)S(1)} reverse(bf16[2,38,38,256]{3,2,1,0:T(8,128)(2,1)} %bitcast.284), dimensions={2} | reverse | bytes 2957312 | tf_op jit(solution)/shard_map/jit(rot90)/jit(_flip)/rev | solution.py:48
  93.3 1.9 bitcast_select_fusion.2
  95.3 1.6 scatter.41
  97.0 4.0 %rev.104 = bf16[2,38,38,256]{3,2,1,0:T(8,128)(2,1)} reverse(bf16[2,38,38,256]{3,2,1,0:T(8,128)(2,1)S(1)} %scatter.44), dimensions={2} | reverse | bytes 2957312 | tf_op jit(solution)/shard_map/jit(rot90)/jit(_flip)/rev | solution.py:51
  101.4 1.6 convert_bitcast_fusion
  103.5 16.2 %fusion.152 = (f32[2,32,32]{1,2,0:T(8,128)S(1)}, f32[2,32,32,256]{3,1,2,0:T(8,128)S(1)}) fusion(f32[2,38,38,256]{3,1,2,0:T(8,128)S(1)} %convert_bitcast_fusion, f32[256]{0:T(256)S(1)} %bitcast.346, f32[256]{0:T(256)S(1)} %bitcast.343, f32[256]{0:T(256)S(1)} %bitcast.340, f32[256]{0:T(256)S(1)} %bitcast.337, f32[256]{0:T(256)S(1)} %bitcast.334, ...), kind=kLoop, calls=%fused_computation.352 | loop fusion | flops 51378176 | bytes 104915968 | tf_op jit(solution)/shard_map/reduce_sum | solution.py:123
  122.9 1.3 fusion.162
  124.6 4.4 %fusion.5 = bf16[2048,1024]{0,1:T(8,128)(2,1)S(1)} fusion(f32[2048,1024]{0,1:T(8,128)S(1)} %fusion.162, bf16[2048,256]{1,0:T(8,128)(2,1)S(1)} %bitcast.302, bf16[1024,256]{1,0:T(8,128)(2,1)S(1)} %copy-done.84), kind=kOutput, calls=%fused_computation.55 | convolution fusion | flops 1094713344 | bytes 14155776 | tf_op jit(solution)/shard_map/dot_general | solution.py:136
  129.0 2.8 multiply_reduce_fusion
  131.8 3.4 subtract_multiply_fusion
  135.3 1.3 copy-done.4
  136.6 5.1 %multiply_reduce_fusion.37 = (bf16[256]{0:T(256)(128)(2,1)S(1)}, bf16[256]{0:T(256)(128)(2,1)S(1)}, bf16[256]{0:T(256)(128)(2,1)S(1)}, bf16[256]{0:T(256)(128)(2...) fusion(f32[2,38,38,256]{3,1,2,0:T(8,128)S(1)} %copy-done.3, ...), kind=kLoop, calls=%fused_computation.213 | loop fusion | flops 13628160 | bytes 29366784 | tf_op jit(solution)/shard_map/reduce_sum | solution.py:94
  141.7 7.3 %multiply_reduce_fusion.19 = (bf16[256]{0:T(256)(128)(2,1)S(1)}, bf16[256]{0:T(256)(128)(2,1)S(1)}, bf16[256]{0:T(256)(128)(2,1)S(1)}, bf16[256]{0:T(256)(128)(2...) fusion(f32[2,38,38,256]{3,1,2,0:T(8,128)S(1)} %copy-done.3, ...), kind=kLoop, calls=%fused_computation.195 | loop fusion | flops 18869760 | bytes 39855104 | tf_op jit(solution)/shard_map/reduce_sum | solution.py:94
  149.1 8.0 %multiply_reduce_fusion.1 = (bf16[256]{0:T(256)(128)(2,1)S(1)}, bf16[256]{0:T(256)(128)(2,1)S(1)}, bf16[256]{0:T(256)(128)(2,1)S(1)}, bf16[256]{0:T(256)(128)(2,...) fusion(f32[2,38,38,256]{3,1,2,0:T(8,128)S(1)} %copy-done.3, ...), kind=kLoop, calls=%fused_computation.177 | loop fusion | flops 18869760 | bytes 41952256 | tf_op jit(solution)/shard_map/reduce_sum | solution.py:94
  157.2 63.0 %fusion.107 = f32[2,38,38,256]{3,1,2,0:T(8,128)S(1)} fusion(f32[2,32,32,256]{3,1,2,0:T(8,128)} %get-tuple-element.302, f32[256]{0:T(256)S(1)} %bitcast.347, f32[256]{0:T(256)S(1)} %bitcast.344, f32[256]{0:T(256)S(1)} %bitcast.341, f32[256]{0:T(256)S(1)} %bitcast.338, f32[256]{0:T(256)S(1)} %bitcast.335, f32[256]{0:T(256)S(1)} %bitcast.332, ...), kind=kLoop, calls=%fused_computation.160 | loop fusion | flops 71714816 | bytes 5104640 | tf_op jit(solution)/shard_map/add | solution.py:107
  220.3 23.3 %fusion.173 = f32[2,38,38,256]{3,2,1,0:T(8,128)S(1)} fusion(f32[256]{0:T(256)S(1)} %bitcast.348, f32[256]{0:T(256)S(1)} %bitcast.345, f32[256]{0:T(256)S(1)} %bitcast.342, f32[256]{0:T(256)S(1)} %bitcast.339, f32[256]{0:T(256)S(1)} %bitcast.336, f32[256]{0:T(256)S(1)} %bitcast.333, f32[256]{0:T(256)S(1)} %bitcast.330, f32[256]{0:T(256)S(1)} %bitcast.327, ...), kind=kLoop, calls=%fused_computation.363 | loop fusion | flops 71714816 | bytes 5104640 | tf_op jit(solution)/shard_map/jit(rot90)/transpose | solution.py:60
  244.9 5.5 %fusion.112 = bf16[2048,256]{1,0:T(8,128)(2,1)} fusion(bf16[1024,256]{1,0:T(8,128)(2,1)S(1)} %copy-done.85, f32[2048,1024]{0,1:T(8,128)} %copy-done.8, bf16[2048,256]{1,0:T(8,128)(2,1)S(1)} %bitcast.288), kind=kOutput, calls=%fused_computation.167 | convolution fusion | flops 1085800448 | bytes 11010048 | tf_op jit(solution)/shard_map/dot_general | solution.py:132
  254.2 3.8 %all-to-all-start.2 = ((bf16[16,8,2048]{2,1,0:T(8,128)(2,1)}), bf16[16,8,2048]{2,1,0:T(8,128)(2,1)S(1)}, u32[]{:S(2)}, u32[]{:S(2)}) async-start(bf16[16,8,2048]{2,1,0:T(8,128)(2,1)} %fusion.124), calls=%async_computation.2 | async-start | bytes 1048576 | tf_op jit(solution)/shard_map/all_to_all | solution.py:175
  258.0 5.1 %fusion.116 = bf16[128,8,256]{2,1,0:T(8,128)(2,1)} fusion(bf16[2048,256,1]{1,0,2:T(8,128)(2,1)S(1)} %bitcast.303, f32[2048,1024]{0,1:T(8,128)} %copy-done.8), kind=kOutput, calls=%fused_computation.233 | convolution fusion | flops 1084489728 | bytes 9961472 | tf_op jit(solution)/shard_map/dot_general | solution.py:135
  263.9 4.3 %convolution_convert_fusion.2 = bf16[256,1024]{1,0:T(8,128)(2,1)} fusion(bf16[2048,256]{1,0:T(8,128)(2,1)S(1)} %copy-done.10, bf16[2048,1024]{0,1:T(8,128)(2,1)} %copy-done.86), kind=kOutput, calls=%fused_computation.234 | convolution fusion | flops 1074003968 | bytes 5767168 | tf_op jit(solution)/shard_map/dot_general | solution.py:138
  269.0 6.7 %all-to-all-start.4 = ((bf16[16,64,256]{2,1,0:T(8,128)(2,1)}), bf16[16,64,256]{2,1,0:T(8,128)(2,1)S(1)}, u32[]{:S(2)}, u32[]{:S(2)}) async-start(bf16[16,64,256]{2,1,0:T(8,128)(2,1)} %broadcast_in_dim.47), calls=%async_computation.4 | async-start | bytes 1048576 | tf_op jit(solution)/shard_map/all_to_all | solution.py:266
  275.7 2.8 slice_add_fusion
  278.6 2.1 reshape.880
  280.7 2.2 pad_maximum_fusion
  285.5 9.4 %all-to-all-start.5 = ((bf16[8,64,256]{2,1,0:T(8,128)(2,1)}), bf16[8,64,256]{2,1,0:T(8,128)(2,1)S(1)}, u32[]{:S(2)}, u32[]{:S(2)}) async-start(bf16[8,64,256]{2,1,0:T(8,128)(2,1)} %broadcast_in_dim.48), calls=%async_computation.5 | async-start | bytes 524288 | tf_op jit(solution)/shard_map/all_to_all | solution.py:266
  294.9 1.7 pad_maximum_fusion.4
  296.6 4.8 %all-to-all-done.5 = bf16[8,64,256]{2,1,0:T(8,128)(2,1)S(1)} async-done(((bf16[8,64,256]{2,1,0:T(8,128)(2,1)}), bf16[8,64,256]{2,1,0:T(8,128)(2,1)S(1)}, u32[]{:S(2)}, u32[]{:S(2)}) %all-to-all-start.5) | async-done | bytes 262176 | tf_op jit(solution)/shard_map/all_to_all | solution.py:266
  301.4 5.4 %all-to-all-start.3 = ((bf16[16,8,2048]{2,1,0:T(8,128)(2,1)}), bf16[16,8,2048]{2,1,0:T(8,128)(2,1)S(1)}, u32[]{:S(2)}, u32[]{:S(2)}) async-start(bf16[16,8,2048]{2,1,0:T(8,128)(2,1)} %pad_maximum_fusion.4), calls=%async_computation.3 | async-start | bytes 1048576 | tf_op jit(solution)/shard_map/all_to_all | solution.py:175
  308.1 7.7 %all-to-all-done.3 = bf16[16,8,2048]{2,1,0:T(8,128)(2,1)S(1)} async-done(((bf16[16,8,2048]{2,1,0:T(8,128)(2,1)}), bf16[16,8,2048]{2,1,0:T(8,128)(2,1)S(1)}, u32[]{:S(2)}, u32[]{:S(2)}) %all-to-all-start.3) | async-done | bytes 524320 | tf_op jit(solution)/shard_map/all_to_all | solution.py:175
  315.8 7.9 %all-to-all-start.6 = ((bf16[128,16,256]{2,1,0:T(8,128)(2,1)}), bf16[128,16,256]{2,1,0:T(8,128)(2,1)}, u32[]{:S(2)}, u32[]{:S(2)}) async-start(bf16[128,16,256]{2,1,0:T(8,128)(2,1)} %pad_maximum_fusion), calls=%async_computation.6 | async-start | bytes 2097152 | tf_op jit(solution)/shard_map/all_to_all | solution.py:251
  323.8 1.3 copy.893
  325.1 1.7 reshape.885
  327.7 1.6 scatter-add.26
  329.6 1.5 reverse_bitcast_fusion.1
  331.8 10.8 %all-to-all-done.6 = bf16[128,16,256]{2,1,0:T(8,128)(2,1)} async-done(((bf16[128,16,256]{2,1,0:T(8,128)(2,1)}), bf16[128,16,256]{2,1,0:T(8,128)(2,1)}, u32[]{:S(2)}, u32[]{:S(2)}) %all-to-all-start.6) | async-done | bytes 1048608 | tf_op jit(solution)/shard_map/all_to_all | solution.py:251
  342.6 1.4 convert_reduce_fusion
  345.1 4.7 %all-to-all-start.7 = ((bf16[128,16,256]{2,1,0:T(8,128)(2,1)}), bf16[128,16,256]{2,1,0:T(8,128)(2,1)S(1)}, u32[]{:S(2)}, u32[]{:S(2)}) async-start(bf16[128,16,256]{2,1,0:T(8,128)(2,1)} %broadcast_in_dim.49), calls=%async_computation.7 | async-start | bytes 2097152 | tf_op jit(solution)/shard_map/all_to_all | solution.py:254
  349.8 1.6 scatter-add.31
  352.5 3.9 %rev.110 = f32[2,32,32,256]{3,1,2,0:T(8,128)} reverse(f32[2,32,32,256]{3,1,2,0:T(8,128)} %bitcast.119), dimensions={1} | reverse | bytes 4194304 | tf_op jit(solution)/shard_map/jit(rot90)/jit(_flip)/rev | solution.py:69
  356.9 4.1 %scatter-add.34 = f32[2,32,32,256]{3,1,2,0:T(8,128)} dynamic-update-slice(f32[2,32,32,256]{3,1,2,0:T(8,128)} %rev.110, f32[2,3,32,256]{3,1,2,0:T(4,128)S(1)} %fusion.127, s32[]{:T(128)} %constant.448.clone.1, s32[]{:T(128)} %constant.448.clone.1, s32[]{:T(128)} %constant.448.clone.1, s32[]{:T(128)} %constant.448.clone.1) | dynamic-update-slice | bytes 393220 | tf_op jit(solution)/shard_map/scatter-add | solution.py:70
  361.0 1.5 scatter-add.35
  362.5 3.9 %rev.111 = f32[2,32,32,256]{3,1,2,0:T(8,128)} reverse(f32[2,32,32,256]{3,1,2,0:T(8,128)} %scatter-add.35), dimensions={1,2} | reverse | bytes 4194304 | tf_op jit(solution)/shard_map/jit(rot90)/jit(_flip)/rev | solution.py:72
  367.3 2.5 rev.112
  370.2 1.8 rev.113
  372.0 2.8 copy.788
  (367 shorter events, 47.1 us)
Async XLA Ops:
  0.6 122.2 %copy-start = (bf16[256,1024]{1,0:T(8,128)(2,1)S(1)}, bf16[256,1024]{1,0:T(8,128)(2,1)}, u32[]{:S(2)}) copy-start(bf16[256,1024]{1,0:T(8,128)(2,1)} %param.50) | copy-start | bytes 1572868
  0.6 3.8 %copy-start.11 = (bf16[1,2,32,32,256]{4,3,2,1,0:T(8,128)(2,1)S(1)}, bf16[1,2,32,32,256]{4,3,2,1,0:T(8,128)(2,1)}, u32[]{:S(2)}) copy-start(bf16[1,2,32,32,256]{4,3,2,1,0:T(8,128)(2,1)} %param.45) | copy-start | bytes 3145732
  8.6 11.1 %copy-start.70 = (s32[32,4]{0,1:T(4,128)S(1)}, s32[32,4]{0,1:T(4,128)}, u32[]{:S(2)}) copy-start(s32[32,4]{0,1:T(4,128)} %param.53) | copy-start | bytes 1540
  8.6 11.1 %copy-start.71 = (s32[32,4]{0,1:T(4,128)S(1)}, s32[32,4]{0,1:T(4,128)}, u32[]{:S(2)}) copy-start(s32[32,4]{0,1:T(4,128)} %param.55) | copy-start | bytes 1540
  8.6 11.1 %copy-start.80 = (s32[32,4]{0,1:T(4,128)S(1)}, s32[32,4]{0,1:T(4,128)}, u32[]{:S(2)}) copy-start(s32[32,4]{0,1:T(4,128)} %param.52) | copy-start | bytes 1540
  8.6 11.1 %copy-start.81 = (s32[32,4]{0,1:T(4,128)S(1)}, s32[32,4]{0,1:T(4,128)}, u32[]{:S(2)}) copy-start(s32[32,4]{0,1:T(4,128)} %param.54) | copy-start | bytes 1540
  8.7 12.2 %copy-start.83 = (s32[4]{0:T(128)S(1)}, s32[4]{0:T(128)}, u32[]{:S(2)}) copy-start(s32[4]{0:T(128)} %constant.451.clone.1) | copy-start | bytes 52
  8.7 12.9 %copy-start.18 = (bf16[7,7,256]{2,1,0:T(8,128)(2,1)S(1)}, bf16[7,7,256]{2,1,0:T(8,128)(2,1)}, u32[]{:S(2)}) copy-start(bf16[7,7,256]{2,1,0:T(8,128)(2,1)} %param.47) | copy-start | bytes 75268
  11.2 18.7 %all-to-all-start = ((bf16[16,8,2048]{2,1,0:T(8,128)(2,1)}), bf16[16,8,2048]{2,1,0:T(8,128)(2,1)S(1)}, u32[]{:S(2)}, u32[]{:S(2)}) async-start(bf16[16,8,2048]{2,1,0:T(8,128)(2,1)} %fusion.123), calls=%async_computation | async-start | bytes 1048576 | tf_op jit(solution)/shard_map/all_to_all | solution.py:175
  20.0 16.8 %copy-start.74 = (s32[128]{0:T(128)}, s32[128]{0:T(128)S(1)}, u32[]{:S(2)}) copy-start(s32[128]{0:T(128)S(1)} %eq.44) | copy-start | bytes 1540
  20.2 16.6 %copy-start.72 = (s32[128]{0:T(128)}, s32[128]{0:T(128)S(1)}, u32[]{:S(2)}) copy-start(s32[128]{0:T(128)S(1)} %eq.48) | copy-start | bytes 1540
  31.4 13.9 %all-to-all-start.1 = ((bf16[16,8,2048]{2,1,0:T(8,128)(2,1)}), bf16[16,8,2048]{2,1,0:T(8,128)(2,1)}, u32[]{:S(2)}, u32[]{:S(2)}) async-start(bf16[16,8,2048]{2,1,0:T(8,128)(2,1)} %pad_maximum_fusion.3), calls=%async_computation.1 | async-start | bytes 1048576 | tf_op jit(solution)/shard_map/all_to_all | solution.py:175
  36.9 14.5 %copy-start.78 = (pred[2,4]{1,0:T(4,128)(4,1)}, pred[2,4]{1,0:T(4,128)(4,1)S(1)}, u32[]{:S(2)}) copy-start(pred[2,4]{1,0:T(4,128)(4,1)S(1)} %copy.695) | copy-start | bytes 28
  63.3 2.6 copy-start.20
  63.3 2.6 copy-start.19
  63.3 3.2 copy-start.17
  84.0 9.3 %copy-start.16 = (bf16[2,1,3,32,256]{4,3,2,1,0:T(8,128)(2,1)S(1)}, bf16[2,1,3,32,256]{4,3,2,1,0:T(8,128)(2,1)}, u32[]{:S(2)}) copy-start(bf16[2,1,3,32,256]{4,3,2,1,0:T(8,128)(2,1)} %get-tuple-element.309) | copy-start | bytes 294916
  101.1 2.1 copy-start.25
  101.1 2.1 copy-start.26
  101.1 2.1 copy-start.27
  101.1 2.1 copy-start.28
  101.1 2.1 copy-start.29
  101.1 2.1 copy-start.30
  101.1 2.1 copy-start.31
  101.2 2.1 copy-start.32
  101.2 2.1 copy-start.33
  101.2 2.1 copy-start.34
  101.2 2.1 copy-start.35
  101.2 2.1 copy-start.36
  101.2 2.1 copy-start.37
  101.2 2.1 copy-start.38
  103.1 16.6 %copy-start.2 = (f32[2,38,38,256]{3,1,2,0:T(8,128)}, f32[2,38,38,256]{3,1,2,0:T(8,128)S(1)}, u32[]{:S(2)}) copy-start(f32[2,38,38,256]{3,1,2,0:T(8,128)S(1)} %convert_bitcast_fusion) | copy-start | bytes 8871940
  119.7 2.2 copy-start.76
  119.7 2.2 copy-start.82
  121.0 8.0 %copy-start.7 = (f32[2,32,32,256]{3,2,1,0:T(8,128)}, f32[2,32,32,256]{3,2,1,0:T(8,128)S(1)}, u32[]{:S(2)}) copy-start(f32[2,32,32,256]{3,2,1,0:T(8,128)S(1)} %copy.710) | copy-start | bytes 6291460
  124.2 4.8 %copy-start.8 = (f32[2048,1024]{0,1:T(8,128)}, f32[2048,1024]{0,1:T(8,128)S(1)}, u32[]{:S(2)}) copy-start(f32[2048,1024]{0,1:T(8,128)S(1)} %fusion.162) | copy-start | bytes 25165828
  129.0 2.8 copy-start.86
  131.8 4.8 %copy-start.3 = (f32[2,38,38,256]{3,1,2,0:T(8,128)S(1)}, f32[2,38,38,256]{3,1,2,0:T(8,128)}, u32[]{:S(2)}) copy-start(f32[2,38,38,256]{3,1,2,0:T(8,128)} %copy-done.2) | copy-start | bytes 8871940
  149.0 8.1 %copy-start.60 = (f32[1,1,256]{2,1,0:T(1,128)S(1)}, f32[1,1,256]{2,1,0:T(1,128)}, u32[]{:S(2)}) copy-start(f32[1,1,256]{2,1,0:T(1,128)} %get-tuple-element.332) | copy-start | bytes 3076
  149.0 8.1 %copy-start.61 = (f32[1,1,256]{2,1,0:T(1,128)S(1)}, f32[1,1,256]{2,1,0:T(1,128)}, u32[]{:S(2)}) copy-start(f32[1,1,256]{2,1,0:T(1,128)} %get-tuple-element.333) | copy-start | bytes 3076
  149.0 8.1 %copy-start.62 = (f32[1,1,256]{2,1,0:T(1,128)S(1)}, f32[1,1,256]{2,1,0:T(1,128)}, u32[]{:S(2)}) copy-start(f32[1,1,256]{2,1,0:T(1,128)} %get-tuple-element.334) | copy-start | bytes 3076
  149.0 8.1 %copy-start.63 = (f32[1,1,256]{2,1,0:T(1,128)S(1)}, f32[1,1,256]{2,1,0:T(1,128)}, u32[]{:S(2)}) copy-start(f32[1,1,256]{2,1,0:T(1,128)} %get-tuple-element.335) | copy-start | bytes 3076
  149.0 8.1 %copy-start.64 = (f32[1,1,256]{2,1,0:T(1,128)S(1)}, f32[1,1,256]{2,1,0:T(1,128)}, u32[]{:S(2)}) copy-start(f32[1,1,256]{2,1,0:T(1,128)} %get-tuple-element.336) | copy-start | bytes 3076
  149.0 8.1 %copy-start.65 = (f32[1,1,256]{2,1,0:T(1,128)S(1)}, f32[1,1,256]{2,1,0:T(1,128)}, u32[]{:S(2)}) copy-start(f32[1,1,256]{2,1,0:T(1,128)} %get-tuple-element.337) | copy-start | bytes 3076
  149.0 8.1 %copy-start.66 = (f32[1,1,256]{2,1,0:T(1,128)S(1)}, f32[1,1,256]{2,1,0:T(1,128)}, u32[]{:S(2)}) copy-start(f32[1,1,256]{2,1,0:T(1,128)} %get-tuple-element.338) | copy-start | bytes 3076
  149.0 8.1 %copy-start.67 = (f32[1,1,256]{2,1,0:T(1,128)S(1)}, f32[1,1,256]{2,1,0:T(1,128)}, u32[]{:S(2)}) copy-start(f32[1,1,256]{2,1,0:T(1,128)} %get-tuple-element.339) | copy-start | bytes 3076
  149.1 8.1 %copy-start.68 = (f32[1,1,256]{2,1,0:T(1,128)S(1)}, f32[1,1,256]{2,1,0:T(1,128)}, u32[]{:S(2)}) copy-start(f32[1,1,256]{2,1,0:T(1,128)} %get-tuple-element.340) | copy-start | bytes 3076
  149.1 8.1 %copy-start.69 = (f32[1,1,256]{2,1,0:T(1,128)S(1)}, f32[1,1,256]{2,1,0:T(1,128)}, u32[]{:S(2)}) copy-start(f32[1,1,256]{2,1,0:T(1,128)} %get-tuple-element.341) | copy-start | bytes 3076
  157.0 63.2 %copy-start.6 = (f32[2,32,32,256]{3,1,2,0:T(8,128)S(1)}, f32[2,32,32,256]{3,1,2,0:T(8,128)}, u32[]{:S(2)}) copy-start(f32[2,32,32,256]{3,1,2,0:T(8,128)} %get-tuple-element.302) | copy-start | bytes 6291460
  220.2 23.6 %copy-start.5 = (f32[2,38,38,256]{3,1,2,0:T(8,128)}, f32[2,38,38,256]{3,1,2,0:T(8,128)S(1)}, u32[]{:S(2)}) copy-start(f32[2,38,38,256]{3,1,2,0:T(8,128)S(1)} %fusion.107) | copy-start | bytes 8871940
  244.9 6.5 %copy-start.79 = (pred[2,4]{1,0:T(4,128)(4,1)S(1)}, pred[2,4]{1,0:T(4,128)(4,1)}, u32[]{:S(2)}) copy-start(pred[2,4]{1,0:T(4,128)(4,1)} %copy-done.78) | copy-start | bytes 28
  244.9 7.0 %copy-start.77 = (pred[2,4]{1,0:T(4,128)(4,1)S(1)}, pred[2,4]{1,0:T(4,128)(4,1)}, u32[]{:S(2)}) copy-start(pred[2,4]{1,0:T(4,128)(4,1)} %copy.685) | copy-start | bytes 28
  251.6 6.4 %copy-start.14 = (bf16[1,2,32,32,256]{4,3,2,1,0:T(8,128)(2,1)S(1)}, bf16[1,2,32,32,256]{4,3,2,1,0:T(8,128)(2,1)}, u32[]{:S(2)}) copy-start(bf16[1,2,32,32,256]{4,3,2,1,0:T(8,128)(2,1)} %param.46) | copy-start | bytes 3145732
  254.2 14.0 %all-to-all-start.2 = ((bf16[16,8,2048]{2,1,0:T(8,128)(2,1)}), bf16[16,8,2048]{2,1,0:T(8,128)(2,1)S(1)}, u32[]{:S(2)}, u32[]{:S(2)}) async-start(bf16[16,8,2048]{2,1,0:T(8,128)(2,1)} %fusion.124), calls=%async_computation.2 | async-start | bytes 1048576 | tf_op jit(solution)/shard_map/all_to_all | solution.py:175
  258.0 5.9 %copy-start.10 = (bf16[2048,256]{1,0:T(8,128)(2,1)S(1)}, bf16[2048,256]{1,0:T(8,128)(2,1)}, u32[]{:S(2)}) copy-start(bf16[2048,256]{1,0:T(8,128)(2,1)} %copy-done.9) | copy-start | bytes 3145732
  269.0 15.7 %all-to-all-start.4 = ((bf16[16,64,256]{2,1,0:T(8,128)(2,1)}), bf16[16,64,256]{2,1,0:T(8,128)(2,1)S(1)}, u32[]{:S(2)}, u32[]{:S(2)}) async-start(bf16[16,64,256]{2,1,0:T(8,128)(2,1)} %broadcast_in_dim.47), calls=%async_computation.4 | async-start | bytes 1048576 | tf_op jit(solution)/shard_map/all_to_all | solution.py:266
  275.7 7.2 %copy-start.73 = (s32[128]{0:T(128)S(1)}, s32[128]{0:T(128)}, u32[]{:S(2)}) copy-start(s32[128]{0:T(128)} %copy-done.72) | copy-start | bytes 1540
  275.7 8.2 %copy-start.75 = (s32[128]{0:T(128)S(1)}, s32[128]{0:T(128)}, u32[]{:S(2)}) copy-start(s32[128]{0:T(128)} %copy-done.74) | copy-start | bytes 1540
  285.5 15.9 %all-to-all-start.5 = ((bf16[8,64,256]{2,1,0:T(8,128)(2,1)}), bf16[8,64,256]{2,1,0:T(8,128)(2,1)S(1)}, u32[]{:S(2)}, u32[]{:S(2)}) async-start(bf16[8,64,256]{2,1,0:T(8,128)(2,1)} %broadcast_in_dim.48), calls=%async_computation.5 | async-start | bytes 524288 | tf_op jit(solution)/shard_map/all_to_all | solution.py:266
  301.4 14.4 %all-to-all-start.3 = ((bf16[16,8,2048]{2,1,0:T(8,128)(2,1)}), bf16[16,8,2048]{2,1,0:T(8,128)(2,1)S(1)}, u32[]{:S(2)}, u32[]{:S(2)}) async-start(bf16[16,8,2048]{2,1,0:T(8,128)(2,1)} %pad_maximum_fusion.4), calls=%async_computation.3 | async-start | bytes 1048576 | tf_op jit(solution)/shard_map/all_to_all | solution.py:175
  315.8 26.8 %all-to-all-start.6 = ((bf16[128,16,256]{2,1,0:T(8,128)(2,1)}), bf16[128,16,256]{2,1,0:T(8,128)(2,1)}, u32[]{:S(2)}, u32[]{:S(2)}) async-start(bf16[128,16,256]{2,1,0:T(8,128)(2,1)} %pad_maximum_fusion), calls=%async_computation.6 | async-start | bytes 2097152 | tf_op jit(solution)/shard_map/all_to_all | solution.py:251
  345.1 29.7 %all-to-all-start.7 = ((bf16[128,16,256]{2,1,0:T(8,128)(2,1)}), bf16[128,16,256]{2,1,0:T(8,128)(2,1)S(1)}, u32[]{:S(2)}, u32[]{:S(2)}) async-start(bf16[128,16,256]{2,1,0:T(8,128)(2,1)} %broadcast_in_dim.49), calls=%async_computation.7 | async-start | bytes 2097152 | tf_op jit(solution)/shard_map/all_to_all | solution.py:254
  349.8 7.0 %copy-start.15 = (f32[2,1,3,32,256]{4,3,2,1,0:T(8,128)S(1)}, f32[2,1,3,32,256]{4,3,2,1,0:T(8,128)}, u32[]{:S(2)}) copy-start(f32[2,1,3,32,256]{4,3,2,1,0:T(8,128)} %get-tuple-element.307) | copy-start | bytes 589828
  374.8 2.7 copy-start.1
  (31 other events, 59.8 us)

commit v2 on v0

v2 whole, which is shorter than its diff:
```python
import functools
import math

import jax
import jax.numpy as jnp
import numpy as np
from jax import lax
from jax.experimental import pallas as pl
from jax.experimental.pallas import tpu as pltpu
from jax.sharding import PartitionSpec as P

BF = jnp.bfloat16
F32 = jnp.float32
N = 32
J = 16
C = 256
HALF = 128
HID = 1024
T = 2
PARTS = 16
KB = 8
CANVAS = 64
RIMS = 2 * 3 * CANVAS + 2 * N * 16
VMEM_LIMIT = 60 * 1024 * 1024


def band_pixel(e, r, p):
    return ((r, p), (p, N - 1 - r), (N - 1 - r, N - 1 - p), (N - 1 - p, r))[e]


def turned_pixel(e, i, j):
    last = N + 5
    return ((i, j), (j, last - i), (last - i, last - j), (last - j, i))[e]


def chunk_row(e, r, p):
    return (p // 2) * 4 * KB + e * KB + (p % 2) * 3 + r


def corner_row(e, r, c):
    return (r * 3 + c) * 4 * KB + e * KB + 6


def band_selector():
    sel = np.zeros((PARTS * 4 * KB, N * N), np.float32)
    for e in range(4):
        for r in range(3):
            for p in range(N):
                y, x = band_pixel(e, r, p)
                sel[chunk_row(e, r, p), y * N + x] = 1
            for c in range(3):
                y, x = band_pixel(e, r, c)
                sel[corner_row(e, r, c), y * N + x] = 1
    return sel


def rim_sources():
    table = {}
    for e in range(4):
        for i in range(3):
            for j in range(N):
                pixel = turned_pixel(e, i, j + 3)
                table[pixel] = (e, chunk_row(e, 2 - i, j), chunk_row(e, 2 - i, N - 1 - j))
            for j in range(3):
                pixel = turned_pixel(e, i, j)
                table[pixel] = (
                    4 + e,
                    corner_row(e, 2 - i, 2 - j),
                    corner_row(e, 2 - j, 2 - i),
                )
    return table


def tables_of(pixels):
    table = rim_sources()
    piece = np.zeros((len(pixels), 8), np.int32)
    plain = np.full((len(pixels),), -1, np.int32)
    flipped = np.full((len(pixels),), -1, np.int32)
    for row, pixel in enumerate(pixels):
        if pixel in table:
            which, plain[row], flipped[row] = table[pixel]
            piece[row, which] = 1
    return piece, plain, flipped


def forward_rim_pixels():
    rows = [(p, q - 13) for p in (0, 1, 2, 35, 36, 37) for q in range(CANVAS)]
    rows += [(p, q - 13) for p in range(3, 35) for q in range(16)]
    rows += [(p, q - 13) for p in range(3, 35) for q in range(48, 64)]
    return rows


RIM_PAIRS = (-2, -1, 16, 17)


def backward_rim_pixels():
    rows = [(p, 3 + 2 * j + u) for p in (0, 1, 2, 35, 36, 37) for u in range(2) for j in range(J)]
    rows += [
        (2 * k + v, 3 + 2 * j + u)
        for k in range(19)
        for u in range(2)
        for v in range(2)
        for j in RIM_PAIRS
    ]
    rows += [(-9, -9)] * (512 - len(rows))
    return rows


def one_hot_rows(tables, flags, width):
    piece, plain, flipped = tables
    is_flipped = jnp.sum(piece[None] * flags[:, None, :], axis=2) > 0
    index = jnp.where(is_flipped, flipped[None], plain[None])
    return (index[:, :, None] == jnp.arange(width, dtype=jnp.int32)).astype(BF)


def pair_selector():
    sel = np.zeros((128, CANVAS), np.float32)
    for d in range(4):
        for s in range(2):
            for j in range(J):
                sel[d * 32 + s * 16 + j, 13 + 2 * (j + d) + s] = 1
    return sel


def grad_pair_selector():
    sel = np.zeros((128, 32), np.float32)
    for d in range(4):
        for s in range(2):
            for j in range(J):
                col = 2 * (j + d) + s - 3
                if 0 <= col < N:
                    sel[d * 32 + s * 16 + j, (col % 2) * 16 + col // 2] = 1
    return sel


def grad_rim_selector():
    sel = np.zeros((128, 128), np.float32)
    for d in range(4):
        for s in range(2):
            for v in range(2):
                for t in range(T):
                    for at, j in enumerate(RIM_PAIRS):
                        col = 2 * (j + d) + s - 3
                        if 0 <= col < N:
                            row = (d * 2 + s) * 16 + v * 8 + t * 4 + at
                            sel[row, v * 64 + t * 32 + (col % 2) * 16 + col // 2] = 1
    return sel


def split_columns():
    sel = np.zeros((256, 256), np.float32)
    for r in range(8):
        for col in range(N):
            sel[r * 32 + (col % 2) * 16 + col // 2, r * 32 + col] = 1
    return sel


def dot(a, b):
    return jnp.dot(a, b, preferred_element_type=F32)


def pack_kernel(fields_ref, sel_ref, out_ref):
    for t in range(T):
        x = fields_ref[t].reshape(N * N, C)
        rows = dot(sel_ref[...], x).astype(BF)
        out_ref[:, t * 32 : (t + 1) * 32, :] = rows.reshape(PARTS, 32, C)


def build_weights(kern_ref, w_ref, mirrored):
    eye = lax.broadcasted_iota(jnp.int32, (HALF, HALF), 0) == lax.broadcasted_iota(
        jnp.int32, (HALF, HALF), 1
    )
    zero = jnp.zeros((HALF, HALF), BF)

    def step(a, carry):
        row = 6 - a if mirrored else a
        taps = kern_ref[row]
        for h in range(2):
            blocks = [
                jnp.where(eye, taps[b : b + 1, h * HALF : (h + 1) * HALF], 0.0).astype(BF)
                for b in range(7)
            ]
            if mirrored:
                blocks = blocks[::-1]
            for d in range(4):
                for s in range(2):
                    for u in range(2):
                        b = 2 * d + s - u
                        block = blocks[b] if 0 <= b <= 6 else zero
                        top = d * 256 + s * HALF
                        w_ref[h, a, top : top + HALF, u * HALF : (u + 1) * HALF] = block
        return carry

    lax.fori_loop(0, 7, step, 0)


def spread(picked, q_ref, index, base):
    rows = picked.shape[0] // 8
    for d in range(4):
        for s in range(2):
            at = (d * 2 + s) * rows
            for h in range(2):
                lane = d * 256 + s * HALF
                q_ref[h, index, base : base + rows, lane : lane + HALF] = picked[
                    at : at + rows, h * HALF : (h + 1) * HALF
                ]


def forward_kernel(
    fields_ref,
    og_ref,
    recv_ref,
    rim_ref,
    kern_ref,
    gain_ref,
    shift_ref,
    win_ref,
    wout_ref,
    win_t_ref,
    wout_t_ref,
    psel_ref,
    split_ref,
    merge_ref,
    result_ref,
    wide_ref,
    gz_ref,
    gains_ref,
    q_out_ref,
    pad_ref,
    q_ref,
    w_ref,
    x_ref,
    o_ref,
    z_ref,
    gwin_ref,
    gwout_ref,
    sem,
):
    build_weights(kern_ref, w_ref, False)
    for t in range(T):
        recv = recv_ref[:, t * 32 : (t + 1) * 32, :].reshape(512, C)
        rims = dot(rim_ref[t], recv).astype(BF)
        rows = 3 * CANVAS
        pad_ref[t, 0:3] = rims[:rows].reshape(3, CANVAS, C)
        pad_ref[t, 35:38] = rims[rows : 2 * rows].reshape(3, CANVAS, C)
        pad_ref[t, 3:35, 0:16] = rims[2 * rows : 2 * rows + 512].reshape(N, 16, C)
        pad_ref[t, 3:35, 48:64] = rims[2 * rows + 512 :].reshape(N, 16, C)
        pad_ref[t, 3:35, 16:48] = fields_ref[t]

    def pairs(row, carry):
        for t in range(T):
            picked = dot(psel_ref[...], pad_ref[t, row]).astype(BF)
            spread(picked, q_ref, row, t * 16)
        return carry

    lax.fori_loop(0, N + 6, pairs, 0)
    copy = pltpu.make_async_copy(q_ref, q_out_ref, sem)
    copy.start()

    def order(m, carry):
        for t in range(T):
            rows = pl.ds(m * 8, 8)
            for src, dst in ((fields_ref, x_ref), (og_ref, o_ref)):
                block = src[t, rows].reshape(256, C)
                dst[rows, t * 32 : (t + 1) * 32] = (
                    dot(split_ref[...], block).astype(BF).reshape(8, 32, C)
                )
        return carry

    lax.fori_loop(0, 4, order, 0)

    def conv(m, carry):
        for h in range(2):
            acc = None
            for a in range(7):
                lhs = q_ref[h, pl.ds(m * 8 + a, 8)].reshape(256, 1024)
                part = dot(lhs, w_ref[h, a])
                acc = part if acc is None else acc + part
            acc = acc.reshape(8, T, 16, 256)
            for t in range(T):
                for u in range(2):
                    base = t * 32 + u * 16
                    z_ref[
                        pl.ds(m * 8, 8), base : base + 16, h * HALF : (h + 1) * HALF
                    ] = acc[:, t, :, u * HALF : (u + 1) * HALF]
        return carry

    lax.fori_loop(0, 4, conv, 0)

    gwin_ref[...] = jnp.zeros_like(gwin_ref)
    gwout_ref[...] = jnp.zeros_like(gwout_ref)
    gains_ref[...] = jnp.zeros_like(gains_ref)
    gain = gain_ref[...]
    shift = shift_ref[...]

    def mlp(m, carry):
        rows = pl.ds(m * 4, 4)
        z = z_ref[rows].reshape(256, C)
        average = jnp.mean(z, axis=1, keepdims=True)
        centered = z - average
        variance = jnp.mean(centered * centered, axis=1, keepdims=True)
        inv_std = lax.rsqrt(variance + 1e-06)
        normed = centered * inv_std
        zn = (normed * gain + shift).astype(BF)
        og = o_ref[rows].reshape(256, C)
        hidden = dot(zn, win_ref[...])
        cdf = 0.5 * (1.0 + lax.erf(hidden * (1.0 / math.sqrt(2.0))))
        pdf = jnp.exp(-0.5 * hidden * hidden) * (1.0 / math.sqrt(2.0 * math.pi))
        act = (hidden * cdf).astype(BF)
        slope = cdf + hidden * pdf
        out = x_ref[rows].reshape(256, C).astype(F32) + dot(act, wout_ref[...])
        x_ref[rows] = out.astype(BF).reshape(4, 64, C)
        grad_hidden = (dot(og, wout_t_ref[...]) * slope).astype(BF)
        gwout_ref[...] += dot(og.T, act)
        gwin_ref[...] += dot(zn.T, grad_hidden)
        grad_normed = dot(grad_hidden, win_t_ref[...])
        gains_ref[0:8] += jnp.sum((grad_normed * normed).reshape(32, 8, C), axis=0)
        gains_ref[8:16] += jnp.sum(grad_normed.reshape(32, 8, C), axis=0)
        scaled = grad_normed * gain
        grad_z = inv_std * (
            scaled
            - jnp.mean(scaled, axis=1, keepdims=True)
            - normed * jnp.mean(scaled * normed, axis=1, keepdims=True)
        )
        gz_ref[rows] = grad_z.astype(BF).reshape(4, 64, C)
        return carry

    lax.fori_loop(0, 8, mlp, 0)

    def unorder(m, carry):
        for t in range(T):
            rows = pl.ds(m * 8, 8)
            block = x_ref[rows, t * 32 : (t + 1) * 32].reshape(256, C)
            result_ref[t, rows] = dot(merge_ref[...], block).astype(BF).reshape(8, 32, C)
        return carry

    lax.fori_loop(0, 4, unorder, 0)
    wide_ref[:, 0:8] = gwout_ref[...].T.reshape(128, 8, C).astype(BF)
    wide_ref[:, 8:16] = gwin_ref[...].T.reshape(128, 8, C).astype(BF)
    copy.wait()


def backward_kernel(
    gz_ref,
    q_in_ref,
    kern_ref,
    rim_t_ref,
    gsel_ref,
    rsel_ref,
    sent_ref,
    inner_ref,
    taps_ref,
    q_ref,
    w_ref,
    g_ref,
    r_ref,
    gt_ref,
    edge_ref,
    sem,
):
    copy = pltpu.make_async_copy(q_in_ref, q_ref, sem)
    copy.start()
    build_weights(kern_ref, w_ref, True)
    zeros = jnp.zeros((6, 32, 1024), BF)
    for h in range(2):
        g_ref[h, 0:6] = zeros
        g_ref[h, 38:44] = zeros
        r_ref[0, h, 0:3] = jnp.zeros((3, 16, 1024), BF)
        r_ref[0, h, 19:22] = jnp.zeros((3, 16, 1024), BF)
        r_ref[1, h, 0:2] = jnp.zeros((2, 16, 1024), BF)
        r_ref[1, h, 19:22] = jnp.zeros((3, 16, 1024), BF)

    def pairs(i, carry):
        for v in range(2):
            for t in range(T):
                block = gz_ref[2 * i + v, t * 32 : (t + 1) * 32]
                spread(dot(gsel_ref[...], block).astype(BF), g_ref, 6 + 2 * i + v, t * 16)
        spread(
            dot(rsel_ref[...], gz_ref[pl.ds(2 * i, 2)].reshape(128, C)).astype(BF),
            r_ref.at[0],
            3 + i,
            0,
        )
        return carry

    lax.fori_loop(0, 16, pairs, 0)

    def odd_pairs(i, carry):
        spread(
            dot(rsel_ref[...], gz_ref[pl.ds(2 * i + 1, 2)].reshape(128, C)).astype(BF),
            r_ref.at[1],
            3 + i,
            0,
        )
        return carry

    lax.fori_loop(0, 15, odd_pairs, 0)
    blank = jnp.zeros((64, C), BF)
    first = jnp.concatenate([blank, gz_ref[0]], axis=0)
    spread(dot(rsel_ref[...], first).astype(BF), r_ref.at[1], 2, 0)
    last = jnp.concatenate([gz_ref[31], blank], axis=0)
    spread(dot(rsel_ref[...], last).astype(BF), r_ref.at[1], 18, 0)

    for h in range(2):
        acc = None
        for a in range(7):
            k, v = a // 2, a % 2
            part = dot(r_ref[v, h, k : k + 19].reshape(304, 1024), w_ref[h, a])
            acc = part if acc is None else acc + part
        acc = acc.astype(BF).reshape(19, 16, 256)
        edge_ref[h, 192:496] = acc.reshape(304, 256)

    for h in range(2):
        for base, at in ((0, 0), (35, 96)):
            acc = None
            for a in range(7):
                lhs = g_ref[h, base + a : base + a + 3].reshape(96, 1024)
                part = dot(lhs, w_ref[h, a])
                acc = part if acc is None else acc + part
            edge_ref[h, at : at + 96] = acc.astype(BF)
        edge_ref[h, 496:512] = jnp.zeros((16, 256), BF)

    edges = jnp.concatenate(
        [
            jnp.concatenate([edge_ref[0, :, 0:HALF], edge_ref[1, :, 0:HALF]], axis=1),
            jnp.concatenate([edge_ref[0, :, HALF:], edge_ref[1, :, HALF:]], axis=1),
        ],
        axis=0,
    )
    for t in range(T):
        rows = dot(rim_t_ref[t], edges).astype(BF)
        sent_ref[:, t * 32 : (t + 1) * 32, :] = rows.reshape(PARTS, 32, C)

    def inside(m, carry):
        for h in range(2):
            acc = None
            for a in range(7):
                lhs = g_ref[h, pl.ds(m * 8 + 3 + a, 8)].reshape(256, 1024)
                part = dot(lhs, w_ref[h, a])
                acc = part if acc is None else acc + part
            acc = acc.reshape(8, T, 16, 256)
            for t in range(T):
                for u in range(2):
                    inner_ref[h, t, pl.ds(m * 8, 8), pl.ds(u, 16, stride=2), :] = acc[
                        :, t, :, u * HALF : (u + 1) * HALF
                    ]
        return carry

    lax.fori_loop(0, 4, inside, 0)

    for h in range(2):
        for u in range(2):
            for t in range(T):
                block = gz_ref[:, t * 32 + u * 16 : t * 32 + u * 16 + 16, h * HALF : (h + 1) * HALF]
                g_ref[h, 0:32, t * 16 : t * 16 + 16, u * HALF : (u + 1) * HALF] = block
        gt_ref[h] = g_ref[h, 0:32, :, 0:256].reshape(1024, 256).T
    copy.wait()
    eye = lax.broadcasted_iota(jnp.int32, (HALF, HALF), 0) == lax.broadcasted_iota(
        jnp.int32, (HALF, HALF), 1
    )

    def taps(a, carry):
        for h in range(2):
            prod = dot(gt_ref[h], q_ref[h, pl.ds(a, 32)].reshape(1024, 1024))
            sums = [None] * 7
            for d in range(4):
                for s in range(2):
                    for u in range(2):
                        b = 2 * d + s - u
                        if 0 <= b <= 6:
                            lane = d * 256 + s * HALF
                            block = jnp.where(
                                eye, prod[u * HALF : (u + 1) * HALF, lane : lane + HALF], 0.0
                            )
                            sums[b] = block if sums[b] is None else sums[b] + block
            rows = [jnp.sum(block, axis=0, keepdims=True) for block in sums]
            rows.append(jnp.zeros((1, HALF), F32))
            taps_ref[a, :, h * HALF : (h + 1) * HALF] = jnp.concatenate(rows, axis=0)
        return carry

    lax.fori_loop(0, 7, taps, 0)


def final_kernel(inner_ref, og_ref, recv_ref, sel_t_ref, out_ref):
    for t in range(T):
        recv = recv_ref[:, t * 32 : (t + 1) * 32, :].reshape(512, C)
        back = dot(sel_t_ref[...], recv).reshape(N, N, C)
        inner = jnp.concatenate([inner_ref[0, t], inner_ref[1, t]], axis=2)
        out_ref[t] = (inner + og_ref[t].astype(F32) + back).astype(BF)


def call(kernel, outs, scratch=(), out_specs=None, in_specs=None):
    options = {}
    if in_specs is not None:
        options["in_specs"] = in_specs
    if out_specs is not None:
        options["out_specs"] = out_specs
    return pl.pallas_call(
        kernel,
        out_shape=outs,
        scratch_shapes=list(scratch),
        compiler_params=pltpu.CompilerParams(vmem_limit_bytes=VMEM_LIMIT),
        **options,
    )


def swap(array, axes):
    return lax.all_to_all(array, axes, 0, 0, tiled=True)


def backward_rim_tables():
    pixels, owners = [], []
    for u in range(2):
        for p in (0, 1, 2, 35, 36, 37):
            for t in range(T):
                for j in range(J):
                    pixels.append((p, 3 + 2 * j + u))
                    owners.append(t)
        for k in range(19):
            for v in range(2):
                for t in range(T):
                    for j in RIM_PAIRS:
                        pixels.append((2 * k + v, 3 + 2 * j + u))
                        owners.append(t)
        pixels += [(-9, -9)] * 16
        owners += [0] * 16
    piece, plain, flipped = tables_of(pixels)
    owners = np.array(owners)
    plains, flippeds = [], []
    for t in range(T):
        plains.append(np.where(owners == t, plain, -1))
        flippeds.append(np.where(owners == t, flipped, -1))
    return piece, np.stack(plains), np.stack(flippeds)


def body(
    fields,
    out_grad,
    kernel,
    ln_gain,
    ln_shift,
    w_in,
    w_out,
    edge_tile,
    edge_code,
    corner_tile,
    corner_code,
):
    x = fields[0]
    og = out_grad[0]
    faces = lax.axis_size("face")
    reps = lax.axis_size("rep")
    devices = faces * reps
    norm_scale = 1.0 / math.sqrt(devices * T * N * N)
    offset = lax.axis_index("face") * T
    sel = band_selector()
    vm = pl.BlockSpec(memory_space=pltpu.VMEM)
    hbm = pl.BlockSpec(memory_space=pl.ANY)
    shape = jax.ShapeDtypeStruct

    codes = jnp.concatenate([edge_code, corner_code], axis=1) // 4
    flags = lax.dynamic_slice_in_dim(codes, offset, T, 0)
    edge_rows = (edge_tile * 4 + edge_code % 4).reshape(-1, 1) * KB
    corner_rows = (corner_tile * 4 + corner_code % 4).reshape(-1, 1) * KB
    at = np.arange(KB)[None, :]
    source = jnp.where(at < 6, edge_rows + at, corner_rows + at).reshape(-1)
    every = jnp.arange(source.shape[0], dtype=jnp.int32)
    pick = (source[:, None] == every[None, :]).astype(BF)
    pick_t = (every[:, None] == source[None, :]).astype(BF)
    piece, plain, flipped = tables_of(forward_rim_pixels())
    rim = one_hot_rows((piece, plain, flipped), flags, 512)
    piece, plain, flipped = backward_rim_tables()
    is_flipped = jnp.sum(piece[None] * flags[:, None, :], axis=2) > 0
    index = jnp.where(is_flipped, flipped, plain)
    rim_t = (jnp.arange(512, dtype=jnp.int32)[None, :, None] == index[:, None, :]).astype(BF)

    taps = jnp.pad(kernel.astype(F32), ((0, 0), (0, 1), (0, 0)))

    sent = call(pack_kernel, shape((PARTS, T * 32, C), BF))(x, sel.astype(BF))
    got = swap(sent, "face")
    routed = dot(pick, got.reshape(-1, C)).astype(BF).reshape(got.shape)
    got = swap(routed, "face")

    split = split_columns()
    q_shape = (2, N + 6, 32, 1024)
    result, wide, gz, gains, q = call(
        forward_kernel,
        (
            shape((T, N, N, C), BF),
            shape((128, 16, C), BF),
            shape((N, 64, C), BF),
            shape((16, C), F32),
            shape(q_shape, BF),
        ),
        scratch=(
            pltpu.VMEM((T, N + 6, CANVAS, C), BF),
            pltpu.VMEM(q_shape, BF),
            pltpu.VMEM((2, 7, 1024, 256), BF),
            pltpu.VMEM((N, 64, C), BF),
            pltpu.VMEM((N, 64, C), BF),
            pltpu.VMEM((N, 64, C), F32),
            pltpu.VMEM((C, HID), F32),
            pltpu.VMEM((C, HID), F32),
            pltpu.SemaphoreType.DMA,
        ),
        in_specs=[vm] * 14,
        out_specs=(vm, vm, vm, vm, hbm),
    )(
        x,
        og,
        got,
        rim,
        taps,
        ln_gain[None],
        ln_shift[None],
        w_in,
        w_out,
        w_in.T,
        w_out.T,
        pair_selector().astype(BF),
        split.astype(BF),
        split.T.astype(BF),
    )

    wide = swap(wide, ("face", "rep"))
    wide = jnp.sum(wide.astype(F32), axis=0, keepdims=True) * norm_scale
    wide = jnp.broadcast_to(wide.astype(BF), (devices,) + wide.shape[1:])
    wide = swap(wide, ("face", "rep")).astype(F32)
    grad_wout = wide[:, 0:8].reshape(HID, C)
    grad_win = wide[:, 8:16].reshape(HID, C).T

    sent, inner, tap_grads = call(
        backward_kernel,
        (
            shape((PARTS, T * 32, C), BF),
            shape((2, T, N, N, HALF), F32),
            shape((7, 8, C), F32),
        ),
        scratch=(
            pltpu.VMEM(q_shape, BF),
            pltpu.VMEM((2, 7, 1024, 256), BF),
            pltpu.VMEM((2, 44, 32, 1024), BF),
            pltpu.VMEM((2, 2, 22, 16, 1024), BF),
            pltpu.VMEM((2, 256, 1024), BF),
            pltpu.VMEM((2, 512, 256), BF),
            pltpu.SemaphoreType.DMA,
        ),
        in_specs=[vm, hbm, vm, vm, vm, vm],
        out_specs=(vm, vm, vm),
    )(
        gz,
        q,
        taps,
        rim_t,
        grad_pair_selector().astype(BF),
        grad_rim_selector().astype(BF),
    )

    got = swap(sent, "face")
    routed = dot(pick_t, got.reshape(-1, C)).astype(BF).reshape(got.shape)
    got = swap(routed, "face")
    grad_input = call(final_kernel, shape((T, N, N, C), BF))(
        inner, og, got, sel.T.astype(BF)
    )

    small = jnp.concatenate(
        [
            tap_grads.reshape(56, C),
            jnp.sum(gains[0:8], axis=0, keepdims=True),
            jnp.sum(gains[8:16], axis=0, keepdims=True),
            jnp.zeros((6, C), F32),
        ],
        axis=0,
    )
    for axis, size in (("face", faces), ("rep", reps)):
        small = jnp.broadcast_to(small.astype(BF)[None], (size,) + small.shape)
        small = jnp.sum(swap(small, axis).astype(F32), axis=0)
    small = small * norm_scale
    return (
        result[None],
        grad_input[None],
        small[:56].reshape(7, 8, C)[:, :7],
        small[56],
        small[57],
        grad_win,
        grad_wout,
    )


def solution(mesh):
    return jax.shard_map(
        body,
        mesh=mesh,
        in_specs=(P("rep", "face"), P("rep", "face")) + (P(),) * 9,
        out_specs=(P("rep", "face"), P("rep", "face")) + (P(),) * 5,
        check_vma=False,
    )
```

time: 523 us -> 218 us (0.42)
  waiting for transfers between devices: 194 us -> 57.2 us
  local copies, waits for them, and re-layouts: 94.8 us -> 8.38 us
  other arithmetic: 93.2 us -> 10.9 us
  Pallas kernels: 0 us -> 74.9 us
  blocking collectives: 90.5 us -> 28.8 us
  starting transfers between devices: 0.12 us -> 32.5 us
  matrix products: 28.8 us -> 3.21 us
  between operations: 16.3 us -> 0.87 us
    unnamed x4 -> x0, waiting for transfers between devices: 126 us -> none
    pallas_call x0 -> x4, Pallas kernels: none -> 74.9 us  [the longest x1 35.1 us: body(): call(forward_kernel, (shape((T, N, N, C), BF), shape((128, 16, C), BF), s...]
    psum x1 -> x0, blocking collectives: 66 us -> none  [body(): lax.psum((grads[0], grads[1], grads[2], grads[3], grads[4]), ('face', 're...]
    all_to_all x0 -> x6, waiting for transfers between devices: none -> 57.2 us  [swap(): return lax.all_to_all(array, axes, 0, 0, tiled=True)]
    psum x1 -> x0, waiting for transfers between devices: 40.8 us -> none  [body(): lax.psum((grads[0], grads[1], grads[2], grads[3], grads[4]), ('face', 're...]
    rev x14 -> x0, local copies, waits for them, and re-layouts: 34.7 us -> none  [the longest x3 11.9 us: assemble(): turned = jnp.rot90(padded, e, axes=(1, 2))]
    reduce_sum x5 -> x6, other arithmetic: 35.1 us -> 2.09 us  [the longest x1 0.9 us: one_hot_rows(): is_flipped = jnp.sum(piece[None] * flags[:, None, :], axis=2) > 0]
    all_to_all x0 -> x6, starting transfers between devices: none -> 32.5 us  [swap(): return lax.all_to_all(array, axes, 0, 0, tiled=True)]
  transfers between devices with their start and end apart: 3 -> 6, of which waited for: 3 -> 5; matrix products, arithmetic and copies ran while one was open for 11% -> 7% of each run, Pallas kernels for 0% -> 2%
where the time goes in v2:
time: 218 us; the launch traced here: 217 us
  Pallas kernels  74.9 us (34%)
  waiting for transfers between devices  57.2 us (26%)
  starting transfers between devices  32.5 us (15%)
  blocking collectives  28.8 us (13%)
  other arithmetic  10.9 us (5%)
  local copies, waits for them, and re-layouts  8.38 us (4%)
  matrix products  3.21 us (1%)
    all_to_all x6, waiting for transfers between devices, swap(): return lax.all_to_all(array, axes, 0, 0, tiled=True)  57.2 us
    pallas_call x1, Pallas kernels, body(): call(forward_kernel, (shape((T, N, N, C), BF), shape((128, 16, C), BF), s...  35.1 us
    pallas_call x1, Pallas kernels, body(): call(backward_kernel, (shape((PARTS, T * 32, C), BF), shape((2, T, N, N,...  32.6 us
    all_to_all x6, starting transfers between devices, swap(): return lax.all_to_all(array, axes, 0, 0, tiled=True)  32.5 us
    all_to_all x2, blocking collectives, swap(): return lax.all_to_all(array, axes, 0, 0, tiled=True)  28.8 us
  transfers between devices with their start and end apart: 6, of which 5 were waited for; matrix products, arithmetic and copies ran while one was open for 7% of the time, Pallas kernels for 2%

profile of v2, /device:TPU:1, one launch (start us, length us, event | category | flops | bytes accessed | tf_op | source)
XLA Modules:
  0.0 216.8 jit_solution(16750812045749596940)
XLA Ops:
  0.6 0.0 copy-start.8
  0.6 0.0 copy-start.6
  0.7 0.0 copy-start.7
  0.7 0.0 copy-start.4
  0.7 0.0 copy-start.1
  0.7 0.0 copy-start.2
  0.7 3.1 %shard_map.297 = bf16[16,64,256]{2,1,0:T(8,128)(2,1)} custom-call(bf16[2,32,32,256]{3,2,1,0:T(8,128)(2,1)} %bitcast.27, bf16[512,1024]{1,0:T(8,128)(2,1)} %constant.96.clone.sel_ref), custom_call_target="tpu_custom_call" | custom-call | tf_op jit(solution)/shard_map/pallas_call | solution.py:579
  3.8 8.4 %all-to-all-start = ((bf16[16,64,256]{2,1,0:T(8,128)(2,1)}), bf16[16,64,256]{2,1,0:T(8,128)(2,1)S(1)}, u32[]{:S(2)}, u32[]{:S(2)}) async-start(bf16[16,64,256]{2,1,0:T(8,128)(2,1)} %shard_map.297), calls=%async_computation | async-start | bytes 1048576 | tf_op jit(solution)/shard_map/all_to_all | solution.py:508
  12.3 0.7 add_select_fusion
  13.0 0.1 constant_dynamic-slice_fusion
  13.1 0.1 copy.49
  13.2 0.7 fusion.13
  13.9 0.1 copy.47
  14.0 0.1 mul.80
  14.1 0.7 fusion.16
  14.8 0.1 copy.48
  14.9 0.1 mul.83
  15.0 0.9 multiply_reduce_fusion
  15.9 0.9 multiply_reduce_fusion.1
  16.7 0.7 compare_select_fusion.1
  17.5 2.2 fusion.2.rim_t_ref
  19.6 0.0 copy-done.8
  19.6 0.1 fusion.8
  19.7 0.0 copy-done.4
  19.7 0.6 pad_convert_fusion.kern_ref
  20.4 0.1 select_n.49
  20.5 0.0 copy-done.1
  20.5 1.0 copy.50
  21.5 0.0 copy-done.2
  21.5 1.0 copy.51
  22.5 0.1 pad.11.clone
  22.6 0.0 copy-done.6
  22.6 0.0 copy-done.7
  22.6 0.0 all-to-all-done
  22.6 1.6 fusion.7
  24.2 6.7 %all-to-all-start.1 = ((bf16[16,64,256]{2,1,0:T(8,128)(2,1)}), bf16[16,64,256]{2,1,0:T(8,128)(2,1)S(1)}, u32[]{:S(2)}, u32[]{:S(2)}) async-start(bf16[16,64,256]{2,1,0:T(8,128)(2,1)} %bitcast.3), calls=%async_computation.1 | async-start | bytes 1048576 | tf_op jit(solution)/shard_map/all_to_all | solution.py:508
  30.9 1.9 fusion.rim_ref
  32.8 7.0 %all-to-all-done.1.recv_ref = bf16[16,64,256]{2,1,0:T(8,128)(2,1)S(1)} async-done(((bf16[16,64,256]{2,1,0:T(8,128)(2,1)}), bf16[16,64,256]{2,1,0:T(8,128)(2,1)S(1)}, u32[]{:S(2)}, u32[]{:S(2)}) %all-to-all-start.1) | async-done | bytes 524320 | tf_op jit(solution)/shard_map/all_to_all | solution.py:508
  39.8 0.8 copy-done.3
  40.6 35.1 %shard_map.298 = (bf16[2,32,32,256]{3,2,1,0:T(8,128)(2,1)}, bf16[128,16,256]{2,1,0:T(8,128)(2,1)}, bf16[32,64,256]{2,1,0:T(8,128)(2,1)}, f32[16,256]{1,0:T(8,128)}, bf16[2,38,32,1024]{3,2,1,0:T(8,128)(2,1)}) custom-call(bf16[2,32,32,256]{3,2,1,0:T(8,128)(2,1)} %bitcast.28, bf16[2,32,32,256]{3,2,1,0:T(8,128)(2,1)} %bitcast.29, ...), custom_call_target="tpu_custom_call" | custom-call | tf_op jit(solution)/shard_map/pallas_call | solution.py:586
  75.7 32.6 %shard_map.299 = (bf16[16,64,256]{2,1,0:T(8,128)(2,1)}, f32[2,2,32,32,128]{4,3,2,1,0:T(8,128)}, f32[7,8,256]{2,1,0:T(8,128)}) custom-call(bf16[32,64,256]{2,1,0:T(8,128)(2,1)} %get-tuple-element.16.gz_ref, bf16[2,38,32,1024]{3,2,1,0:T(8,128)(2,1)} %get-tuple-element.17.q_in_ref, f32[7,8,256]{2,1,0:T(8,128)} %pad_convert_fusion.kern_ref, ...), custom_call_target="tpu_custom_call" | custom-call | tf_op jit(solution)/shard_map/pallas_call | solution.py:632
  108.4 0.8 convert_bitcast_fusion
  109.2 0.0 copy-done.5
  109.2 0.1 maximum_maximum_fusion
  109.4 13.2 %all_to_all.40 = bf16[16,64,256]{2,1,0:T(8,128)(2,1)S(1)} all-to-all(bf16[16,64,256]{2,1,0:T(8,128)(2,1)S(1)} %broadcast_in_dim.84), channel_id=1, replica_groups=mesh['face'=16,'rep'=8] {'face'}, dimensions={0} | all-to-all | bytes 1048576 | tf_op jit(solution)/shard_map/all_to_all | solution.py:508
  122.5 3.6 %all-to-all-start.2 = ((bf16[16,64,256]{2,1,0:T(8,128)(2,1)}), bf16[16,64,256]{2,1,0:T(8,128)(2,1)S(1)}, u32[]{:S(2)}, u32[]{:S(2)}) async-start(bf16[16,64,256]{2,1,0:T(8,128)(2,1)} %get-tuple-element.19), calls=%async_computation.2 | async-start | bytes 1048576 | tf_op jit(solution)/shard_map/all_to_all | solution.py:508
  126.1 0.1 reduce_sum.70
  126.2 8.8 %all-to-all-done.2 = bf16[16,64,256]{2,1,0:T(8,128)(2,1)S(1)} async-done(((bf16[16,64,256]{2,1,0:T(8,128)(2,1)}), bf16[16,64,256]{2,1,0:T(8,128)(2,1)S(1)}, u32[]{:S(2)}, u32[]{:S(2)}) %all-to-all-start.2) | async-done | bytes 524320 | tf_op jit(solution)/shard_map/all_to_all | solution.py:508
  135.1 15.6 %all_to_all.41 = bf16[8,64,256]{2,1,0:T(8,128)(2,1)S(1)} all-to-all(bf16[8,64,256]{2,1,0:T(8,128)(2,1)S(1)} %broadcast_in_dim.85), channel_id=1, replica_groups=mesh['face'=16,'rep'=8] {'rep'}, dimensions={0} | all-to-all | bytes 524288 | tf_op jit(solution)/shard_map/all_to_all | solution.py:508
  150.7 4.6 %all-to-all-start.6 = ((bf16[128,16,256]{2,1,0:T(8,128)(2,1)}), bf16[128,16,256]{2,1,0:T(8,128)(2,1)S(1)}, u32[]{:S(2)}, u32[]{:S(2)}) async-start(bf16[128,16,256]{2,1,0:T(8,128)(2,1)} %get-tuple-element.22), calls=%async_computation.6 | async-start | bytes 2097152 | tf_op jit(solution)/shard_map/all_to_all | solution.py:508
  155.3 1.6 fusion.6
  156.9 17.5 %all-to-all-done.6 = bf16[128,16,256]{2,1,0:T(8,128)(2,1)S(1)} async-done(((bf16[128,16,256]{2,1,0:T(8,128)(2,1)}), bf16[128,16,256]{2,1,0:T(8,128)(2,1)S(1)}, u32[]{:S(2)}, u32[]{:S(2)}) %all-to-all-start.6) | async-done | bytes 1048608 | tf_op jit(solution)/shard_map/all_to_all | solution.py:508
  174.4 3.6 %all-to-all-start.3 = ((bf16[16,64,256]{2,1,0:T(8,128)(2,1)}), bf16[16,64,256]{2,1,0:T(8,128)(2,1)S(1)}, u32[]{:S(2)}, u32[]{:S(2)}) async-start(bf16[16,64,256]{2,1,0:T(8,128)(2,1)} %bitcast.10), calls=%async_computation.3 | async-start | bytes 1048576 | tf_op jit(solution)/shard_map/all_to_all | solution.py:508
  178.0 0.2 convert_reduce_fusion
  178.2 9.9 %all-to-all-done.3.recv_ref = bf16[16,64,256]{2,1,0:T(8,128)(2,1)S(1)} async-done(((bf16[16,64,256]{2,1,0:T(8,128)(2,1)}), bf16[16,64,256]{2,1,0:T(8,128)(2,1)S(1)}, u32[]{:S(2)}, u32[]{:S(2)}) %all-to-all-start.3) | async-done | bytes 524320 | tf_op jit(solution)/shard_map/all_to_all | solution.py:508
  188.1 1.1 broadcast_in_dim.86
  189.2 5.7 %all-to-all-start.7 = ((bf16[128,16,256]{2,1,0:T(8,128)(2,1)}), bf16[128,16,256]{2,1,0:T(8,128)(2,1)S(1)}, u32[]{:S(2)}, u32[]{:S(2)}) async-start(bf16[128,16,256]{2,1,0:T(8,128)(2,1)} %broadcast_in_dim.86), calls=%async_computation.7 | async-start | bytes 2097152 | tf_op jit(solution)/shard_map/all_to_all | solution.py:508
  195.0 0.6 fusion.17
  195.6 0.6 slice_bitcast_fusion.2
  196.2 4.0 %shard_map.300 = bf16[2,32,32,256]{3,2,1,0:T(8,128)(2,1)} custom-call(f32[2,2,32,32,128]{4,3,2,1,0:T(8,128)} %get-tuple-element.18.inner_ref, bf16[2,32,32,256]{3,2,1,0:T(8,128)(2,1)} %bitcast.30, bf16[16,64,256]{2,1,0:T(8,128)(2,1)} %copy-done, bf16[1024,512]{1,0:T(8,128)(2,1)} %constant.102.clone.sel_t_ref), custom_call_target="tpu_custom_call" | custom-call | tf_op jit(solution)/shard_map/pallas_call | solution.py:662
  200.2 13.9 %all-to-all-done.7 = bf16[128,16,256]{2,1,0:T(8,128)(2,1)S(1)} async-done(((bf16[128,16,256]{2,1,0:T(8,128)(2,1)}), bf16[128,16,256]{2,1,0:T(8,128)(2,1)S(1)}, u32[]{:S(2)}, u32[]{:S(2)}) %all-to-all-start.7) | async-done | bytes 1048608 | tf_op jit(solution)/shard_map/all_to_all | solution.py:508
  214.1 0.3 convert_element_type.48
  214.4 1.1 slice_bitcast_fusion
  215.5 1.3 copy.53
  (14 shorter events, 0.2 us)
Async XLA Ops:
  0.6 19.0 %copy-start.8 = (pred[8]{0:T(512)(128)(4,1)S(1)}, pred[8]{0:T(512)(128)(4,1)}, u32[]{:S(2)}) copy-start(pred[8]{0:T(512)(128)(4,1)} %constant.107) | copy-start | bytes 28
  0.6 21.9 %copy-start.6 = (s32[1408]{0:T(1024)S(1)}, s32[1408]{0:T(1024)}, u32[]{:S(2)}) copy-start(s32[1408]{0:T(1024)} %constant.110) | copy-start | bytes 16900
  0.7 21.9 %copy-start.7 = (s32[1408]{0:T(1024)S(1)}, s32[1408]{0:T(1024)}, u32[]{:S(2)}) copy-start(s32[1408]{0:T(1024)} %constant.111) | copy-start | bytes 16900
  0.7 19.1 %copy-start.4 = (bf16[7,7,256]{2,1,0:T(8,128)(2,1)S(1)}, bf16[7,7,256]{2,1,0:T(8,128)(2,1)}, u32[]{:S(2)}) copy-start(bf16[7,7,256]{2,1,0:T(8,128)(2,1)} %param.28) | copy-start | bytes 75268
  0.7 19.8 %copy-start.1 = (bf16[256,1024]{1,0:T(8,128)(2,1)S(1)}, bf16[256,1024]{1,0:T(8,128)(2,1)}, u32[]{:S(2)}) copy-start(bf16[256,1024]{1,0:T(8,128)(2,1)} %win_ref.1) | copy-start | bytes 1572868
  0.7 20.8 %copy-start.2 = (bf16[1024,256]{1,0:T(8,128)(2,1)S(1)}, bf16[1024,256]{1,0:T(8,128)(2,1)}, u32[]{:S(2)}) copy-start(bf16[1024,256]{1,0:T(8,128)(2,1)} %wout_ref.1) | copy-start | bytes 1572868
  3.8 18.7 %all-to-all-start = ((bf16[16,64,256]{2,1,0:T(8,128)(2,1)}), bf16[16,64,256]{2,1,0:T(8,128)(2,1)S(1)}, u32[]{:S(2)}, u32[]{:S(2)}) async-start(bf16[16,64,256]{2,1,0:T(8,128)(2,1)} %shard_map.297), calls=%async_computation | async-start | bytes 1048576 | tf_op jit(solution)/shard_map/all_to_all | solution.py:508
  24.2 15.6 %all-to-all-start.1 = ((bf16[16,64,256]{2,1,0:T(8,128)(2,1)}), bf16[16,64,256]{2,1,0:T(8,128)(2,1)S(1)}, u32[]{:S(2)}, u32[]{:S(2)}) async-start(bf16[16,64,256]{2,1,0:T(8,128)(2,1)} %bitcast.3), calls=%async_computation.1 | async-start | bytes 1048576 | tf_op jit(solution)/shard_map/all_to_all | solution.py:508
  39.8 0.8 copy-start.3
  75.7 33.5 %copy-start.5 = (f32[16,256]{1,0:T(8,128)S(1)}, f32[16,256]{1,0:T(8,128)}, u32[]{:S(2)}) copy-start(f32[16,256]{1,0:T(8,128)} %get-tuple-element.21) | copy-start | bytes 49156
  122.5 12.5 %all-to-all-start.2 = ((bf16[16,64,256]{2,1,0:T(8,128)(2,1)}), bf16[16,64,256]{2,1,0:T(8,128)(2,1)S(1)}, u32[]{:S(2)}, u32[]{:S(2)}) async-start(bf16[16,64,256]{2,1,0:T(8,128)(2,1)} %get-tuple-element.19), calls=%async_computation.2 | async-start | bytes 1048576 | tf_op jit(solution)/shard_map/all_to_all | solution.py:508
  150.7 23.7 %all-to-all-start.6 = ((bf16[128,16,256]{2,1,0:T(8,128)(2,1)}), bf16[128,16,256]{2,1,0:T(8,128)(2,1)S(1)}, u32[]{:S(2)}, u32[]{:S(2)}) async-start(bf16[128,16,256]{2,1,0:T(8,128)(2,1)} %get-tuple-element.22), calls=%async_computation.6 | async-start | bytes 2097152 | tf_op jit(solution)/shard_map/all_to_all | solution.py:508
  174.4 13.7 %all-to-all-start.3 = ((bf16[16,64,256]{2,1,0:T(8,128)(2,1)}), bf16[16,64,256]{2,1,0:T(8,128)(2,1)S(1)}, u32[]{:S(2)}, u32[]{:S(2)}) async-start(bf16[16,64,256]{2,1,0:T(8,128)(2,1)} %bitcast.10), calls=%async_computation.3 | async-start | bytes 1048576 | tf_op jit(solution)/shard_map/all_to_all | solution.py:508
  188.1 8.1 %copy-start = (bf16[16,64,256]{2,1,0:T(8,128)(2,1)}, bf16[16,64,256]{2,1,0:T(8,128)(2,1)S(1)}, u32[]{:S(2)}) copy-start(bf16[16,64,256]{2,1,0:T(8,128)(2,1)S(1)} %all-to-all-done.3.recv_ref) | copy-start | bytes 1572868
  189.2 24.9 %all-to-all-start.7 = ((bf16[128,16,256]{2,1,0:T(8,128)(2,1)}), bf16[128,16,256]{2,1,0:T(8,128)(2,1)S(1)}, u32[]{:S(2)}, u32[]{:S(2)}) async-start(bf16[128,16,256]{2,1,0:T(8,128)(2,1)} %broadcast_in_dim.86), calls=%async_computation.7 | async-start | bytes 2097152 | tf_op jit(solution)/shard_map/all_to_all | solution.py:508

commit v3 on v2

v3 whole, which is shorter than its diff:
```python
import functools
import math

import jax
import jax.numpy as jnp
import numpy as np
from jax import lax
from jax.experimental import pallas as pl
from jax.experimental.pallas import tpu as pltpu
from jax.sharding import PartitionSpec as P

BF = jnp.bfloat16
F32 = jnp.float32
N = 32
J = 16
C = 256
HALF = 128
HID = 1024
T = 2
PARTS = 16
KB = 48
SENT = PARTS * KB
LOCAL = 2 * 3 * N
SIDE = 8
MIB = 1024 * 1024


def band_pixel(e, r, p):
    return ((r, p), (p, N - 1 - r), (N - 1 - r, N - 1 - p), (N - 1 - p, r))[e]


def turned_pixel(e, i, j):
    last = N + 5
    return ((i, j), (j, last - i), (last - i, last - j), (last - j, i))[e]


def block_of(e):
    return (0, 1, 0, 2)[e]


def edge_of(t, block):
    return ((0, 1, 3), (2, 1, 3))[t][block]


def chunk_row(t, e, r, p):
    return (p // 2) * KB + block_of(e) * 16 + t * 6 + (p % 2) * 3 + r


def corner_row(t, e, r, c):
    return (r * 3 + c) * KB + t * 16 + 12 + e


def source_pixels():
    pixels = np.full((SENT,), -1, np.int32)
    for t in range(T):
        for e in range(4):
            for r in range(3):
                if e != 2 - 2 * t:
                    for p in range(N):
                        y, x = band_pixel(e, r, p)
                        pixels[chunk_row(t, e, r, p)] = t * N * N + y * N + x
                for c in range(3):
                    y, x = band_pixel(e, r, c)
                    pixels[corner_row(t, e, r, c)] = t * N * N + y * N + x
    return pixels


def rim_sources(t):
    table = {}
    for e in range(4):
        for i in range(3):
            for j in range(N):
                pixel = turned_pixel(e, i, j + 3)
                if e == 2 - 2 * t:
                    y, x = band_pixel((e + 2) % 4, 2 - i, j)
                    y = y if t == 0 else y - (N - 3)
                    row = SENT + t * 3 * N + y * N + x
                    table[pixel] = (e, row, row)
                else:
                    flipped = chunk_row(t, e, 2 - i, N - 1 - j)
                    table[pixel] = (e, chunk_row(t, e, 2 - i, j), flipped)
            for j in range(3):
                pixel = turned_pixel(e, i, j)
                table[pixel] = (
                    4 + e,
                    corner_row(t, e, 2 - i, 2 - j),
                    corner_row(t, e, 2 - j, 2 - i),
                )
    return table


def tables_of(pixels):
    tables = [rim_sources(t) for t in range(T)]
    piece = np.zeros((len(pixels), T * 8), np.int32)
    plain = np.full((len(pixels),), -1, np.int32)
    flipped = np.full((len(pixels),), -1, np.int32)
    for row, (t, p, q) in enumerate(pixels):
        if (p, q) in tables[t]:
            which, plain[row], flipped[row] = tables[t][p, q]
            piece[row, t * 8 + which] = 1
    return piece, plain, flipped


def rows_of(tables, flags):
    piece, plain, flipped = tables
    is_flipped = jnp.sum(piece * flags.reshape(1, -1), axis=1) > 0
    return jnp.where(is_flipped, flipped, plain)


def forward_rim_pixels():
    rows = [(t, p, q + 3) for p in (0, 1, 2, 35, 36, 37) for t in range(T) for q in range(N)]
    for p in range(N + 6):
        for t in range(T):
            rows += [(t, p, q) for q in (0, 1, 2, 35, 36, 37)] + [(t, -9, -9)] * 2
    return rows


RIM_PAIRS = (-2, -1, 16, 17)


def backward_rim_pixels():
    rows = []
    for u in range(2):
        for p in (0, 1, 2, 35, 36, 37):
            rows += [(t, p, 3 + 2 * j + u) for t in range(T) for j in range(J)]
        for k in range(19):
            for v in range(2):
                rows += [(t, 2 * k + v, 3 + 2 * j + u) for t in range(T) for j in RIM_PAIRS]
        rows += [(0, -9, -9)] * 16
    return rows


def pair_selector():
    sel = np.zeros((4, 128, 4 * (N + SIDE)), np.float32)
    for d in range(4):
        for s in range(2):
            for j in range(J):
                q = 2 * (j + d) + s
                for at in range(4):
                    if q < 3:
                        column = 4 * N + at * SIDE + q
                    elif q < N + 3:
                        column = at * N + q - 3
                    else:
                        column = 4 * N + at * SIDE + q - N
                    sel[at, d * 32 + s * 16 + j, column] = 1
    return sel.reshape(512, 4 * (N + SIDE))


def grad_selector():
    sel = np.zeros((768, 3, T, 32), np.float32)
    for d in range(4):
        for s in range(2):
            for j in range(J):
                col = 2 * (j + d) + s - 3
                if 0 <= col < N:
                    for v in range(2):
                        for t in range(T):
                            row = (v * T + t) * 128 + d * 32 + s * 16 + j
                            sel[row, 1 + v, t, (col % 2) * 16 + col // 2] = 1
    rim = grad_rim_selector().reshape(128, 2, T, 32)
    sel[512:640, 1:3] = rim
    sel[640:768, 0:2] = rim
    return sel.reshape(768, 192)


def grad_rim_selector():
    sel = np.zeros((128, 128), np.float32)
    for d in range(4):
        for s in range(2):
            for v in range(2):
                for t in range(T):
                    for at, j in enumerate(RIM_PAIRS):
                        col = 2 * (j + d) + s - 3
                        if 0 <= col < N:
                            row = (d * 2 + s) * 16 + v * 8 + t * 4 + at
                            sel[row, v * 64 + t * 32 + (col % 2) * 16 + col // 2] = 1
    return sel


def split_columns():
    sel = np.zeros((256, 256), np.float32)
    for r in range(8):
        for col in range(N):
            sel[r * 32 + (col % 2) * 16 + col // 2, r * 32 + col] = 1
    return sel


def dot(a, b):
    return jnp.dot(a, b, preferred_element_type=F32)


def fetch(pairs, sems):
    copies = [
        pltpu.make_async_copy(src, dst, sems.at[i]) for i, (src, dst) in enumerate(pairs)
    ]
    for copy in copies:
        copy.start()
    return copies


def pack_kernel(fields_in, pixel_in, out_ref, fields_ref, pixel_ref, sems):
    for copy in fetch([(pixel_in, pixel_ref), (fields_in, fields_ref)], sems):
        copy.wait()
    x = fields_ref[...].reshape(T * N * N, C)
    for m in range(4):
        rows = SENT // 4
        pixel = pixel_ref[m * rows : (m + 1) * rows]
        columns = lax.broadcasted_iota(jnp.int32, (rows, T * N * N), 1)
        pick = jnp.where(columns == pixel, 1.0, 0.0).astype(BF)
        out_ref[m * 4 : (m + 1) * 4] = dot(pick, x).astype(BF).reshape(4, KB, C)


def build_weights(kern_ref, w_ref, mirrored, halves=(0, 1)):
    eye = lax.broadcasted_iota(jnp.int32, (HALF, HALF), 0) == lax.broadcasted_iota(
        jnp.int32, (HALF, HALF), 1
    )
    zero = jnp.zeros((HALF, HALF), BF)

    def step(a, carry):
        row = 6 - a if mirrored else a
        taps = kern_ref[row]
        for at, h in enumerate(halves):
            blocks = [
                jnp.where(eye, taps[b : b + 1, h * HALF : (h + 1) * HALF], 0.0).astype(BF)
                for b in range(7)
            ]
            if mirrored:
                blocks = blocks[::-1]
            for d in range(4):
                for s in range(2):
                    for u in range(2):
                        b = 2 * d + s - u
                        block = blocks[b] if 0 <= b <= 6 else zero
                        top = d * 256 + s * HALF
                        w_ref[at, a, top : top + HALF, u * HALF : (u + 1) * HALF] = block
        return carry

    lax.fori_loop(0, 7, step, 0)


def spread(picked, q_ref, index, base):
    rows = picked.shape[0] // 8
    for d in range(4):
        for s in range(2):
            at = (d * 2 + s) * rows
            for h in range(2):
                lane = d * 256 + s * HALF
                q_ref[h, index, base : base + rows, lane : lane + HALF] = picked[
                    at : at + rows, h * HALF : (h + 1) * HALF
                ]


def forward_kernel(
    fields_in,
    og_in,
    recv_in,
    rim_in,
    kern_ref,
    gain_ref,
    shift_ref,
    win_in,
    wout_in,
    win_t_in,
    wout_t_in,
    psel_in,
    split_in,
    merge_in,
    result_out,
    wide_ref,
    gz_out,
    fields_ref,
    recv_ref,
    rim_ref,
    og_ref,
    win_ref,
    wout_ref,
    win_t_ref,
    wout_t_ref,
    psel_ref,
    split_ref,
    merge_ref,
    result_ref,
    gz_ref,
    mid_ref,
    side_ref,
    q_ref,
    w_ref,
    x_ref,
    o_ref,
    z_ref,
    gwin_ref,
    gwout_ref,
    gains_ref,
    g_ref,
    gt_ref,
    small_ref,
    sems,
):
    copies = fetch(
        [
            (rim_in, rim_ref),
            (recv_in, recv_ref),
            (fields_in, fields_ref),
            (psel_in, psel_ref),
            (og_in, og_ref),
            (split_in, split_ref),
            (win_in, win_ref),
            (wout_in, wout_ref),
            (win_t_in, win_t_ref),
            (wout_t_in, wout_t_ref),
            (merge_in, merge_ref),
        ],
        sems,
    )
    build_weights(kern_ref, w_ref, False)
    for copy in copies[:4]:
        copy.wait()
    source = jnp.concatenate(
        [
            recv_ref[...].reshape(SENT, C),
            fields_ref[1, 0:3].reshape(3 * N, C),
            fields_ref[0, N - 3 :].reshape(3 * N, C),
        ],
        axis=0,
    )
    outer = 6 * T * N
    rims = dot(rim_ref[0:outer], source).astype(BF).reshape(6, T, N, C)
    mid_ref[0:3] = rims[0:3]
    mid_ref[N + 3 :] = rims[3:6]
    side_ref[...] = dot(rim_ref[outer:], source).astype(BF).reshape(N + 6, T * SIDE, C)
    for t in range(T):
        mid_ref[3 : N + 3, t] = fields_ref[t]

    def pairs(i, carry):
        block = jnp.concatenate(
            [
                mid_ref[pl.ds(2 * i, 2)].reshape(4 * N, C),
                side_ref[pl.ds(2 * i, 2)].reshape(4 * SIDE, C),
            ],
            axis=0,
        )
        picked = dot(psel_ref[...], block).astype(BF)
        for v in range(2):
            for t in range(T):
                at = (v * T + t) * 128
                spread(picked[at : at + 128], q_ref, 2 * i + v, t * 16)
        return carry

    lax.fori_loop(0, (N + 6) // 2, pairs, 0)

    copies[4].wait()
    copies[5].wait()

    def order(m, carry):
        for t in range(T):
            rows = pl.ds(m * 8, 8)
            for src, dst in ((fields_ref, x_ref), (og_ref, o_ref)):
                block = src[t, rows].reshape(256, C)
                dst[rows, t * 32 : (t + 1) * 32] = (
                    dot(split_ref[...], block).astype(BF).reshape(8, 32, C)
                )
        return carry

    lax.fori_loop(0, 4, order, 0)

    def conv(m, carry):
        for h in range(2):
            acc = None
            for a in range(7):
                lhs = q_ref[h, pl.ds(m * 8 + a, 8)].reshape(256, 1024)
                part = dot(lhs, w_ref[h, a])
                acc = part if acc is None else acc + part
            acc = acc.reshape(8, T, 16, 256)
            for t in range(T):
                for u in range(2):
                    base = t * 32 + u * 16
                    z_ref[
                        pl.ds(m * 8, 8), base : base + 16, h * HALF : (h + 1) * HALF
                    ] = acc[:, t, :, u * HALF : (u + 1) * HALF]
        return carry

    lax.fori_loop(0, 4, conv, 0)

    for copy in copies[6:]:
        copy.wait()
    gwin_ref[...] = jnp.zeros_like(gwin_ref)
    gwout_ref[...] = jnp.zeros_like(gwout_ref)
    gains_ref[...] = jnp.zeros_like(gains_ref)
    gz_ref[0] = jnp.zeros((64, C), BF)
    gz_ref[N + 1] = jnp.zeros((64, C), BF)
    gain = gain_ref[...]
    shift = shift_ref[...]

    def mlp(m, carry):
        rows = pl.ds(m * 4, 4)
        z = z_ref[rows].reshape(256, C)
        average = jnp.mean(z, axis=1, keepdims=True)
        centered = z - average
        variance = jnp.mean(centered * centered, axis=1, keepdims=True)
        inv_std = lax.rsqrt(variance + 1e-06)
        normed = centered * inv_std
        zn = (normed * gain + shift).astype(BF)
        og = o_ref[rows].reshape(256, C)
        hidden = dot(zn, win_ref[...])
        cdf = 0.5 * (1.0 + lax.erf(hidden * (1.0 / math.sqrt(2.0))))
        pdf = jnp.exp(-0.5 * hidden * hidden) * (1.0 / math.sqrt(2.0 * math.pi))
        act = (hidden * cdf).astype(BF)
        slope = cdf + hidden * pdf
        out = x_ref[rows].reshape(256, C).astype(F32) + dot(act, wout_ref[...])
        x_ref[rows] = out.astype(BF).reshape(4, 64, C)
        grad_hidden = (dot(og, wout_t_ref[...]) * slope).astype(BF)
        gwout_ref[...] += dot(og.T, act)
        gwin_ref[...] += dot(zn.T, grad_hidden)
        grad_normed = dot(grad_hidden, win_t_ref[...])
        gains_ref[0:8] += jnp.sum((grad_normed * normed).reshape(32, 8, C), axis=0)
        gains_ref[8:16] += jnp.sum(grad_normed.reshape(32, 8, C), axis=0)
        scaled = grad_normed * gain
        grad_z = inv_std * (
            scaled
            - jnp.mean(scaled, axis=1, keepdims=True)
            - normed * jnp.mean(scaled * normed, axis=1, keepdims=True)
        )
        grad_z = grad_z.astype(BF).reshape(4, 64, C)
        gz_ref[pl.ds(m * 4 + 1, 4)] = grad_z
        for h in range(2):
            for t in range(T):
                for u in range(2):
                    g_ref[h, rows, t * 16 : (t + 1) * 16, u * HALF : (u + 1) * HALF] = grad_z[
                        :, t * 32 + u * 16 : t * 32 + u * 16 + 16, h * HALF : (h + 1) * HALF
                    ]
        return carry

    lax.fori_loop(0, 8, mlp, 0)

    def unorder(m, carry):
        for t in range(T):
            rows = pl.ds(m * 8, 8)
            block = x_ref[rows, t * 32 : (t + 1) * 32].reshape(256, C)
            result_ref[t, rows] = dot(merge_ref[...], block).astype(BF).reshape(8, 32, C)
        return carry

    lax.fori_loop(0, 4, unorder, 0)
    copies = fetch([(result_ref, result_out), (gz_ref, gz_out)], sems)

    for h in range(2):
        gt_ref[h] = g_ref[h].reshape(1024, 256).T
    eye = lax.broadcasted_iota(jnp.int32, (HALF, HALF), 0) == lax.broadcasted_iota(
        jnp.int32, (HALF, HALF), 1
    )

    def taps(a, carry):
        for h in range(2):
            prod = dot(gt_ref[h], q_ref[h, pl.ds(a, 32)].reshape(1024, 1024))
            sums = [None] * 7
            for d in range(4):
                for s in range(2):
                    for u in range(2):
                        b = 2 * d + s - u
                        if 0 <= b <= 6:
                            lane = d * 256 + s * HALF
                            block = jnp.where(
                                eye, prod[u * HALF : (u + 1) * HALF, lane : lane + HALF], 0.0
                            )
                            sums[b] = block if sums[b] is None else sums[b] + block
            rows = [jnp.sum(block, axis=0, keepdims=True) for block in sums]
            rows.append(jnp.zeros((1, HALF), F32))
            small_ref[a, :, h * HALF : (h + 1) * HALF] = jnp.concatenate(rows, axis=0)
        return carry

    lax.fori_loop(0, 7, taps, 0)
    small_ref[7] = jnp.concatenate(
        [
            jnp.sum(gains_ref[0:8], axis=0, keepdims=True),
            jnp.sum(gains_ref[8:16], axis=0, keepdims=True),
            jnp.zeros((6, C), F32),
        ],
        axis=0,
    )
    half = wide_ref.shape[0] // 2
    wide_ref[:half, 0:256] = gwout_ref[...].T.astype(BF).reshape(half, 256, C)
    wide_ref[half:, 0:256] = gwin_ref[...].T.astype(BF).reshape(half, 256, C)
    blank = jnp.zeros((8, 8, C), F32)
    wide_ref[:, 256:272] = jnp.concatenate([small_ref[...], blank], axis=1).astype(BF)
    for copy in copies:
        copy.wait()


def rims_kernel(
    gz_ref,
    kern_ref,
    row_ref,
    gsel_ref,
    rsel_ref,
    sent_ref,
    near_ref,
    w_ref,
    g_ref,
    r_ref,
    edge_ref,
):
    build_weights(kern_ref, w_ref, True)
    for h in range(2):
        g_ref[h, 0:6] = jnp.zeros((6, 32, 1024), BF)
        g_ref[h, 12:18] = jnp.zeros((6, 32, 1024), BF)
        r_ref[0, h, 0:3] = jnp.zeros((3, 16, 1024), BF)
        r_ref[0, h, 19:22] = jnp.zeros((3, 16, 1024), BF)
        r_ref[1, h, 0:2] = jnp.zeros((2, 16, 1024), BF)
        r_ref[1, h, 19:22] = jnp.zeros((3, 16, 1024), BF)

    def rim_pairs(i, carry):
        block = gz_ref[pl.ds(2 * i, 3)].reshape(192, C)
        picked = dot(gsel_ref[512:], block).astype(BF)
        spread(picked[0:128], r_ref.at[0], 3 + i, 0)
        spread(picked[128:256], r_ref.at[1], 2 + i, 0)
        return carry

    lax.fori_loop(0, 16, rim_pairs, 0)
    last = dot(rsel_ref[...], gz_ref[N : N + 2].reshape(128, C)).astype(BF)
    spread(last, r_ref.at[1], 18, 0)
    for first, row in ((0, 6), (1, 7), (29, 9), (30, 10)):
        picked = dot(gsel_ref[0:512], gz_ref[first : first + 3].reshape(192, C)).astype(BF)
        for v in range(2):
            for t in range(T):
                at = (v * T + t) * 128
                spread(picked[at : at + 128], g_ref, row + v, t * 16)

    for h in range(2):
        acc = None
        for a in range(7):
            k, v = a // 2, a % 2
            lhs = jnp.concatenate(
                [
                    g_ref[h, a : a + 3].reshape(96, 1024),
                    g_ref[h, 9 + a : 12 + a].reshape(96, 1024),
                    r_ref[v, h, k : k + 19].reshape(304, 1024),
                ],
                axis=0,
            )
            part = dot(lhs, w_ref[h, a])
            acc = part if acc is None else acc + part
        edge_ref[h, 0:496] = acc.astype(BF)
        edge_ref[h, 496:512] = jnp.zeros((16, 256), BF)

    edges = jnp.concatenate(
        [
            jnp.concatenate([edge_ref[0, :, 0:HALF], edge_ref[1, :, 0:HALF]], axis=1),
            jnp.concatenate([edge_ref[0, :, HALF:], edge_ref[1, :, HALF:]], axis=1),
        ],
        axis=0,
    )
    rows = SENT + LOCAL
    pick = lax.broadcasted_iota(jnp.int32, (rows, 1024), 0) == row_ref[...]
    back = dot(jnp.where(pick, 1.0, 0.0).astype(BF), edges)
    sent_ref[...] = back[:SENT].astype(BF).reshape(PARTS, KB, C)
    near_ref[...] = back[SENT:].reshape(2, 3, N, C)


def inside_kernel(h, gz_in, kern_ref, gsel_ref, inner_ref, w_ref, g_ref, gz_ref, sems):
    copies = fetch([(gz_in, gz_ref)], sems)
    build_weights(kern_ref, w_ref, True, (h,))
    g_ref[0:3] = jnp.zeros((3, 32, 1024), BF)
    g_ref[35:38] = jnp.zeros((3, 32, 1024), BF)
    copies[0].wait()

    def pairs(i, carry):
        block = gz_ref[pl.ds(2 * i, 3), :, h * HALF : (h + 1) * HALF].reshape(192, HALF)
        picked = dot(gsel_ref[0:512], block).astype(BF)
        for v in range(2):
            for t in range(T):
                for ds in range(8):
                    at = (v * T + t) * 128 + ds * 16
                    rows = slice(t * 16, (t + 1) * 16)
                    lanes = slice(ds * HALF, (ds + 1) * HALF)
                    g_ref[3 + 2 * i + v, rows, lanes] = picked[at : at + 16]
        return carry

    lax.fori_loop(0, 16, pairs, 0)

    def inside(m, carry):
        acc = None
        for a in range(7):
            lhs = g_ref[pl.ds(m * 8 + a, 8)].reshape(256, 1024)
            part = dot(lhs, w_ref[0, a])
            acc = part if acc is None else acc + part
        acc = acc.reshape(8, T, 16, 256)
        for t in range(T):
            for u in range(2):
                inner_ref[t, pl.ds(m * 8, 8), pl.ds(u, 16, stride=2), :] = acc[
                    :, t, :, u * HALF : (u + 1) * HALF
                ]
        return carry

    lax.fori_loop(0, 4, inside, 0)


def join_kernel(sent_ref, wide_ref, out_ref):
    total = wide_ref[0].astype(F32)
    for rep in range(1, wide_ref.shape[0]):
        total = total + wide_ref[rep].astype(F32)
    total = total.astype(BF)
    out_ref[:, 0:KB] = sent_ref[...]
    out_ref[:, KB : KB + 16] = total[0:256].reshape(PARTS, 16, C)
    for part in range(PARTS):
        out_ref[part, KB + 16 :] = total[256:272]


def return_kernel(got_ref, source_ref, out_ref, small_ref):
    pick = lax.broadcasted_iota(jnp.int32, (SENT, SENT), 0) == source_ref[...]
    pick = jnp.where(pick, 1.0, 0.0).astype(BF)
    routed = dot(pick, got_ref[:, 0:KB].reshape(SENT, C)).astype(BF)
    out_ref[:, 0:KB] = routed.reshape(PARTS, KB, C)
    total = got_ref[0, KB:].astype(F32)
    for part in range(1, PARTS):
        total = total + got_ref[part, KB:].astype(F32)
    total = total.astype(BF)
    small_ref[...] = total[16:]
    for part in range(PARTS):
        out_ref[part, KB:] = total[:16]


def spread_kernel(got_ref, small_ref, out_ref):
    wide = got_ref[:, KB : KB + 16].reshape(256, C)
    small = small_ref[...]
    for rep in range(out_ref.shape[0]):
        out_ref[rep, 0:256] = wide
        out_ref[rep, 256:272] = small


def final_kernel(inner0_ref, inner1_ref, near_ref, og_ref, recv_ref, pixel_ref, out_ref):
    recv = recv_ref[:, 0:KB].reshape(SENT, C)
    for t in range(T):
        for m in range(2):
            rows = N * N // 2
            first = (t * 2 + m) * rows
            pick = lax.broadcasted_iota(jnp.int32, (rows, SENT), 0) + first == pixel_ref[...]
            back = dot(jnp.where(pick, 1.0, 0.0).astype(BF), recv).reshape(N // 2, N, C)
            half = slice(m * N // 2, (m + 1) * N // 2)
            inner = jnp.concatenate([inner0_ref[t, half], inner1_ref[t, half]], axis=2)
            total = inner + og_ref[t, half].astype(F32) + back
            if (t, m) == (1, 0):
                total = jnp.concatenate([total[:3] + near_ref[0], total[3:]], axis=0)
            if (t, m) == (0, 1):
                total = jnp.concatenate([total[:-3], total[-3:] + near_ref[1]], axis=0)
            out_ref[t, half] = total.astype(BF)


def unpack_kernel(norm_scale, got_ref, wout_ref, win_ref, taps_ref, gain_ref, shift_ref):
    half = got_ref.shape[0] // 2
    small = got_ref[:, 256:272].astype(F32) * norm_scale
    taps_ref[...] = small[0:7, 0:7]
    gain_ref[...] = small[7, 0:1]
    shift_ref[...] = small[7, 1:2]
    for rep in range(half):
        rows = slice(rep * 256, (rep + 1) * 256)
        wout_ref[rows] = got_ref[rep, 0:256].astype(F32) * norm_scale
        win_ref[:, rows] = (got_ref[half + rep, 0:256].astype(F32) * norm_scale).T


def call(kernel, outs, scratch=(), out_specs=None, in_specs=None, flops=0, vmem=16):
    options = {}
    if flops:
        options["cost_estimate"] = pl.CostEstimate(
            flops=flops, bytes_accessed=10_000_000, transcendentals=0
        )
    if in_specs is not None:
        options["in_specs"] = in_specs
    if out_specs is not None:
        options["out_specs"] = out_specs
    return pl.pallas_call(
        kernel,
        out_shape=outs,
        scratch_shapes=list(scratch),
        compiler_params=pltpu.CompilerParams(vmem_limit_bytes=vmem * MIB),
        **options,
    )


def swap(array, axes):
    return lax.all_to_all(array, axes, 0, 0, tiled=True)


def body(
    fields,
    out_grad,
    kernel,
    ln_gain,
    ln_shift,
    w_in,
    w_out,
    edge_tile,
    edge_code,
    corner_tile,
    corner_code,
):
    x = fields[0]
    og = out_grad[0]
    faces = lax.axis_size("face")
    reps = lax.axis_size("rep")
    devices = faces * reps
    norm_scale = 1.0 / math.sqrt(devices * T * N * N)
    offset = lax.axis_index("face") * T
    vm = pl.BlockSpec(memory_space=pltpu.VMEM)
    hbm = pl.BlockSpec(memory_space=pltpu.HBM)
    shape = jax.ShapeDtypeStruct

    codes = jnp.concatenate([edge_code, corner_code], axis=1) // 4
    flags = lax.dynamic_slice_in_dim(codes, offset, T, 0)
    odd = jnp.arange(edge_tile.shape[0]) % T
    blocks = []
    for block in range(3):
        edge = [edge_of(t, block) for t in range(T)]
        tile = jnp.where(odd == 0, edge_tile[:, edge[0]], edge_tile[:, edge[1]])
        code = jnp.where(odd == 0, edge_code[:, edge[0]], edge_code[:, edge[1]]) % 4
        place = jnp.where(code == 1, 16, jnp.where(code == 3, 32, 0))
        first = tile // T * KB + place + tile % T * 6
        blocks.append((first[:, None] + np.arange(6)).reshape(-1, 12))
    corners = corner_tile // T * KB + corner_tile % T * 16 + 12 + corner_code % 4
    corners = corners.reshape(-1, T, 4)
    none = jnp.full_like(corners[:, 0], -1)
    source = jnp.concatenate(
        [blocks[0], corners[:, 0], blocks[1], corners[:, 1], blocks[2], none], axis=1
    ).reshape(-1)
    pick = (source[:, None] == jnp.arange(SENT, dtype=jnp.int32)).astype(BF)
    rim_rows = rows_of(tables_of(forward_rim_pixels()), flags)
    rim = (rim_rows[:, None] == jnp.arange(SENT + LOCAL, dtype=jnp.int32)).astype(BF)
    edge_rows = rows_of(tables_of(backward_rim_pixels()), flags)
    pixels = source_pixels()

    taps = jnp.pad(kernel.astype(F32), ((0, 0), (0, 1), (0, 0)))

    sent = call(
        pack_kernel,
        shape((PARTS, KB, C), BF),
        scratch=(
            pltpu.VMEM((T, N, N, C), BF),
            pltpu.VMEM((SENT, 1), jnp.int32),
            pltpu.SemaphoreType.DMA((2,)),
        ),
        in_specs=[hbm, hbm],
        out_specs=vm,
        vmem=60,
    )(x, pixels[:, None])
    got = swap(sent, "face")
    routed = dot(pick, got.reshape(-1, C)).astype(BF).reshape(got.shape)
    got = swap(routed, "face")

    split = split_columns()
    result, wide, gz = call(
        forward_kernel,
        (
            shape((T, N, N, C), BF),
            shape((reps, 272, C), BF),
            shape((N + 2, 64, C), BF),
        ),
        scratch=(
            pltpu.VMEM((T, N, N, C), BF),
            pltpu.VMEM((PARTS, KB, C), BF),
            pltpu.VMEM(rim.shape, BF),
            pltpu.VMEM((T, N, N, C), BF),
            pltpu.VMEM((C, HID), BF),
            pltpu.VMEM((HID, C), BF),
            pltpu.VMEM((HID, C), BF),
            pltpu.VMEM((C, HID), BF),
            pltpu.VMEM((512, 4 * (N + SIDE)), BF),
            pltpu.VMEM((256, 256), BF),
            pltpu.VMEM((256, 256), BF),
            pltpu.VMEM((T, N, N, C), BF),
            pltpu.VMEM((N + 2, 64, C), BF),
            pltpu.VMEM((N + 6, T, N, C), BF),
            pltpu.VMEM((N + 6, T * SIDE, C), BF),
            pltpu.VMEM((2, N + 6, 32, 1024), BF),
            pltpu.VMEM((2, 7, 1024, 256), BF),
            pltpu.VMEM((N, 64, C), BF),
            pltpu.VMEM((N, 64, C), BF),
            pltpu.VMEM((N, 64, C), F32),
            pltpu.VMEM((C, HID), F32),
            pltpu.VMEM((C, HID), F32),
            pltpu.VMEM((16, C), F32),
            pltpu.VMEM((2, N, 32, 256), BF),
            pltpu.VMEM((2, 256, 1024), BF),
            pltpu.VMEM((8, 8, C), F32),
            pltpu.SemaphoreType.DMA((11,)),
        ),
        in_specs=[hbm] * 4 + [vm] * 3 + [hbm] * 7,
        out_specs=(hbm, vm, hbm),
        flops=40_000_000_000,
        vmem=60,
    )(
        x,
        og,
        got,
        rim,
        taps,
        ln_gain[None],
        ln_shift[None],
        w_in,
        w_out,
        w_in.T,
        w_out.T,
        pair_selector().astype(BF),
        split.astype(BF),
        split.T.astype(BF),
    )

    wide = swap(wide, "rep")
    gsel = grad_selector().astype(BF)
    sent, near = call(
        rims_kernel,
        (shape((PARTS, KB, C), BF), shape((2, 3, N, C), F32)),
        scratch=(
            pltpu.VMEM((2, 7, 1024, 256), BF),
            pltpu.VMEM((2, 18, 32, 1024), BF),
            pltpu.VMEM((2, 2, 22, 16, 1024), BF),
            pltpu.VMEM((2, 512, 256), BF),
        ),
        flops=12_000_000_000,
        vmem=32,
    )(gz, taps, edge_rows[None], gsel, grad_rim_selector().astype(BF))
    inner = [
        call(
            functools.partial(inside_kernel, h),
            shape((T, N, N, HALF), F32),
            scratch=(
                pltpu.VMEM((1, 7, 1024, 256), BF),
                pltpu.VMEM((N + 6, 32, 1024), BF),
                pltpu.VMEM((N + 2, 64, C), BF),
                pltpu.SemaphoreType.DMA((1,)),
            ),
            in_specs=[hbm, vm, vm],
            out_specs=vm,
            flops=9_000_000_000,
            vmem=20,
        )(gz, taps, gsel)
        for h in range(2)
    ]
    sent = call(join_kernel, shape((PARTS, KB + 32, C), BF))(sent, wide)
    got = swap(sent, "face")
    routed, small = call(
        return_kernel, (shape((PARTS, KB + 16, C), BF), shape((16, C), BF))
    )(got, source[None])
    got = swap(routed, "face")
    wide = call(spread_kernel, shape((reps, 272, C), BF))(got, small)
    wide = swap(wide, "rep")
    grad_input = call(final_kernel, shape((T, N, N, C), BF), flops=5_000_000_000)(
        *inner, near, og, got, pixels[None]
    )
    grad_wout, grad_win, grad_taps, grad_gain, grad_shift = call(
        functools.partial(unpack_kernel, norm_scale),
        (
            shape((HID, C), F32),
            shape((C, HID), F32),
            shape(kernel.shape, F32),
            shape((1, C), F32),
            shape((1, C), F32),
        ),
    )(wide)
    return (
        result[None],
        grad_input[None],
        grad_taps,
        grad_gain[0],
        grad_shift[0],
        grad_win,
        grad_wout,
    )


def solution(mesh):
    return jax.shard_map(
        body,
        mesh=mesh,
        in_specs=(P("rep", "face"), P("rep", "face")) + (P(),) * 9,
        out_specs=(P("rep", "face"), P("rep", "face")) + (P(),) * 5,
        check_vma=False,
    )
```

time: 218 us -> 155 us (0.71)
  blocking collectives: 28.8 us -> 0 us
  waiting for transfers between devices: 57.2 us -> 32.3 us
  other arithmetic: 10.9 us -> 2.66 us
    all_to_all x2 -> x0, blocking collectives: 28.8 us -> none  [swap(): return lax.all_to_all(array, axes, 0, 0, tiled=True)]
    all_to_all x6, waiting for transfers between devices: 57.2 us -> 32.3 us  [swap(): return lax.all_to_all(array, axes, 0, 0, tiled=True)]
    convert_element_type x4 -> x1, other arithmetic: 4.34 us -> 1.7 us  [body(): (rim_rows[:, None] == jnp.arange(SENT + LOCAL, dtype=jnp.int32)).astype(BF)]
    pallas_call x4 -> x10, Pallas kernels: 74.9 us -> 76.5 us  [the longest x1 40 us: body(): call(forward_kernel, (shape((T, N, N, C), BF), shape((reps, 272, C), BF),...]
    unnamed x21 -> x46, local copies, waits for them, and re-layouts: 4.15 us -> 5.34 us
  transfers between devices with their start and end apart: 6 -> 6, of which waited for: 5 -> 5; matrix products, arithmetic and copies ran while one was open for 7% -> 4% of each run, Pallas kernels for 2% -> 18%
where the time goes in v3:
time: 155 us; the launch traced here: 154 us
  Pallas kernels  76.5 us (49%)
  starting transfers between devices  33.7 us (22%)
  waiting for transfers between devices  32.3 us (21%)
  local copies, waits for them, and re-layouts  6.8 us (4%)
  other arithmetic  2.66 us (2%)
    pallas_call x1, Pallas kernels, body(): call(forward_kernel, (shape((T, N, N, C), BF), shape((reps, 272, C), BF),...  40 us
    all_to_all x6, starting transfers between devices, swap(): return lax.all_to_all(array, axes, 0, 0, tiled=True)  33.7 us
    all_to_all x6, waiting for transfers between devices, swap(): return lax.all_to_all(array, axes, 0, 0, tiled=True)  32.3 us
    pallas_call x2, Pallas kernels, body(): call(functools.partial(inside_kernel, h), shape((T, N, N, HALF), F32), sc...  17.3 us
    pallas_call x1, Pallas kernels, body(): call(rims_kernel, (shape((PARTS, KB, C), BF), shape((2, 3, N, C), F32)),...  8.94 us
    unnamed x46, local copies, waits for them, and re-layouts  5.34 us
    pallas_call x1, Pallas kernels, body(): call(pack_kernel, shape((PARTS, KB, C), BF), scratch=(pltpu.VMEM((T, N, N...  3.22 us
  transfers between devices with their start and end apart: 6, of which 5 were waited for; matrix products, arithmetic and copies ran while one was open for 4% of the time, Pallas kernels for 18%

profile of v3, /device:TPU:1, one launch (start us, length us, event | category | flops | bytes accessed | tf_op | source)
XLA Modules:
  0.0 154.2 jit_solution(10608890283207691719)
XLA Ops:
  0.6 0.0 copy-start.12
  0.6 0.0 copy-start.18
  0.7 0.0 copy-start.19
  0.7 0.0 copy-start.8
  0.7 0.0 copy-start.9
  0.7 3.2 %shard_map.306 = bf16[16,48,256]{2,1,0:T(8,128)(2,1)} custom-call(bf16[2,32,32,256]{3,2,1,0:T(8,128)(2,1)} %bitcast.26, s32[768,1]{1,0:T(8,128)} %constant.171.clone.pixel_in), custom_call_target="tpu_custom_call" | custom-call | tf_op jit(solution)/shard_map/pallas_call | solution.py:732
  4.0 0.0 copy-start.11
  4.0 0.0 copy-start.16
  4.0 0.0 copy-start.17
  4.0 8.6 %all-to-all-start = ((bf16[16,48,256]{2,1,0:T(8,128)(2,1)}), bf16[16,48,256]{2,1,0:T(8,128)(2,1)S(1)}, u32[]{:S(2)}, u32[]{:S(2)}) async-start(bf16[16,48,256]{2,1,0:T(8,128)(2,1)} %shard_map.306), calls=%async_computation | async-start | bytes 786432 | tf_op jit(solution)/shard_map/all_to_all | solution.py:680
  12.6 0.1 add.179
  12.7 0.0 copy-done.21
  12.7 0.0 copy-done.14
  12.8 0.0 copy-done.20
  12.8 0.1 constant_dynamic-slice_fusion
  12.9 0.1 copy.88
  12.9 0.1 mul.68
  13.0 0.1 add.203
  13.1 0.1 copy.82
  13.2 0.1 add.175
  13.3 0.1 copy.77
  13.4 0.1 add.192
  13.5 0.1 copy.80
  13.6 0.1 copy.78
  13.7 0.1 multiply_reduce_fusion
  13.8 0.1 broadcast_add_fusion
  13.9 0.1 copy.87
  14.0 0.1 copy.85
  14.0 0.1 copy.83
  14.1 0.1 concatenate.6
  14.2 0.1 eq.87
  14.3 1.0 copy.89
  15.3 1.0 copy.90
  16.3 0.1 multiply_reduce_fusion.1
  16.4 4.4 %all-to-all-done = bf16[16,48,256]{2,1,0:T(8,128)(2,1)S(1)} async-done(((bf16[16,48,256]{2,1,0:T(8,128)(2,1)}), bf16[16,48,256]{2,1,0:T(8,128)(2,1)S(1)}, u32[]{:S(2)}, u32[]{:S(2)}) %all-to-all-start) | async-done | bytes 393248 | tf_op jit(solution)/shard_map/all_to_all | solution.py:680
  20.8 1.3 fusion.2
  22.2 4.1 %all-to-all-start.1 = ((bf16[16,48,256]{2,1,0:T(8,128)(2,1)}), bf16[16,48,256]{2,1,0:T(8,128)(2,1)S(1)}, u32[]{:S(2)}, u32[]{:S(2)}) async-start(bf16[16,48,256]{2,1,0:T(8,128)(2,1)} %bitcast.6), calls=%async_computation.1 | async-start | bytes 786432 | tf_op jit(solution)/shard_map/all_to_all | solution.py:680
  26.3 0.6 pad_convert_fusion.kern_ref
  26.9 1.7 %fusion.rim_in = bf16[992,960]{1,0:T(8,128)(2,1)} fusion(s32[992]{0:T(1024)S(1)} %compare_select_fusion.1), kind=kLoop, calls=%fused_computation.1 | loop fusion | flops 1904640 | bytes 1908608 | tf_op jit(solution)/shard_map/convert_element_type | solution.py:726
  28.6 5.6 %all-to-all-done.1.recv_in = bf16[16,48,256]{2,1,0:T(8,128)(2,1)S(1)} async-done(((bf16[16,48,256]{2,1,0:T(8,128)(2,1)}), bf16[16,48,256]{2,1,0:T(8,128)(2,1)S(1)}, u32[]{:S(2)}, u32[]{:S(2)}) %all-to-all-start.1) | async-done | bytes 393248 | tf_op jit(solution)/shard_map/all_to_all | solution.py:680
  34.2 0.7 copy-done.10
  35.0 40.0 %shard_map.307 = (bf16[2,32,32,256]{3,2,1,0:T(8,128)(2,1)}, bf16[8,272,256]{2,1,0:T(8,128)(2,1)}, bf16[34,64,256]{2,1,0:T(8,128)(2,1)}) custom-call(bf16[2,32,32,256]{3,2,1,0:T(8,128)(2,1)} %bitcast.27, bf16[2,32,32,256]{3,2,1,0:T(8,128)(2,1)} %bitcast.24, bf16[16,48,256]{2,1,0:T(8,128)(2,1)} %copy-done.10, bf16[992,960]{1,0:T(8,128)(2,1)} %fusion.rim_in, ...), custom_call_target="tpu_custom_call" | custom-call | flops 40000000000 | bytes 10000000 | tf_op jit(solution)/shard_map/pallas_call | solution.py:749
  75.0 0.0 copy-start
  75.0 0.0 copy-start.2
  75.0 0.0 copy-start.3
  75.0 7.9 %all-to-all-start.2 = ((bf16[8,272,256]{2,1,0:T(8,128)(2,1)}), bf16[8,272,256]{2,1,0:T(8,128)(2,1)S(1)}, u32[]{:S(2)}, u32[]{:S(2)}) async-start(bf16[8,272,256]{2,1,0:T(8,128)(2,1)} %get-tuple-element.23), calls=%async_computation.2 | async-start | bytes 2228224 | tf_op jit(solution)/shard_map/all_to_all | solution.py:680
  82.9 8.9 %shard_map.310 = (bf16[16,48,256]{2,1,0:T(8,128)(2,1)S(1)}, f32[2,3,32,256]{3,2,1,0:T(8,128)S(1)}) custom-call(bf16[34,64,256]{2,1,0:T(8,128)(2,1)S(1)} %copy-done.5, f32[7,8,256]{2,1,0:T(8,128)S(1)} %copy-done, s32[1,1024]{1,0:T(1,128)S(1)} %bitcast.23, bf16[768,192]{1,0:T(8,128)(2,1)S(1)} %copy-done.2, bf16[128,128]{1,0:T(8,128)(2,1)S(1)} %copy-done.3), custom_call_target="tpu_custom_call" | custom-call | flops 12000000000 | bytes 10000000 | tf_op jit(solution)/shard_map/pallas_call | solution.py:808
  91.9 6.8 %all-to-all-done.2.wide_ref = bf16[8,272,256]{2,1,0:T(8,128)(2,1)S(1)} async-done(((bf16[8,272,256]{2,1,0:T(8,128)(2,1)}), bf16[8,272,256]{2,1,0:T(8,128)(2,1)S(1)}, u32[]{:S(2)}, u32[]{:S(2)}) %all-to-all-start.2) | async-done | bytes 1114144 | tf_op jit(solution)/shard_map/all_to_all | solution.py:680
  98.7 1.0 shard_map.311
  99.7 3.6 %all-to-all-start.3 = ((bf16[16,80,256]{2,1,0:T(8,128)(2,1)}), bf16[16,80,256]{2,1,0:T(8,128)(2,1)S(1)}, u32[]{:S(2)}, u32[]{:S(2)}) async-start(bf16[16,80,256]{2,1,0:T(8,128)(2,1)} %shard_map.311), calls=%async_computation.3 | async-start | bytes 1310720 | tf_op jit(solution)/shard_map/all_to_all | solution.py:680
  103.3 0.1 broadcast_in_dim_reshape.4.source_ref
  103.4 11.5 %all-to-all-done.3.got_ref = bf16[16,80,256]{2,1,0:T(8,128)(2,1)S(1)} async-done(((bf16[16,80,256]{2,1,0:T(8,128)(2,1)}), bf16[16,80,256]{2,1,0:T(8,128)(2,1)S(1)}, u32[]{:S(2)}, u32[]{:S(2)}) %all-to-all-start.3) | async-done | bytes 655392 | tf_op jit(solution)/shard_map/all_to_all | solution.py:680
  114.9 1.3 shard_map.312
  116.2 3.6 %all-to-all-start.4 = ((bf16[16,64,256]{2,1,0:T(8,128)(2,1)}), bf16[16,64,256]{2,1,0:T(8,128)(2,1)S(1)}, u32[]{:S(2)}, u32[]{:S(2)}) async-start(bf16[16,64,256]{2,1,0:T(8,128)(2,1)} %get-tuple-element.24), calls=%async_computation.4 | async-start | bytes 1048576 | tf_op jit(solution)/shard_map/all_to_all | solution.py:680
  119.8 1.2 copy-done.6
  121.0 8.6 %shard_map.309.inner1_ref = f32[2,32,32,128]{3,2,1,0:T(8,128)S(1)} custom-call(bf16[34,64,256]{2,1,0:T(8,128)(2,1)S(1)} %copy-done.6, f32[7,8,256]{2,1,0:T(8,128)S(1)} %copy-done, bf16[768,192]{1,0:T(8,128)(2,1)S(1)} %copy-done.2), custom_call_target="tpu_custom_call" | custom-call | flops 8999999488 | bytes 10000000 | tf_op jit(solution)/shard_map/pallas_call | solution.py:821
  129.7 0.0 all-to-all-done.4.recv_ref.got_ref
  129.7 1.1 shard_map.314
  130.8 6.0 %all-to-all-start.5 = ((bf16[8,272,256]{2,1,0:T(8,128)(2,1)}), bf16[8,272,256]{2,1,0:T(8,128)(2,1)S(1)}, u32[]{:S(2)}, u32[]{:S(2)}) async-start(bf16[8,272,256]{2,1,0:T(8,128)(2,1)} %shard_map.314), calls=%async_computation.5 | async-start | bytes 2228224 | tf_op jit(solution)/shard_map/all_to_all | solution.py:680
  136.7 1.2 copy-done.7
  138.0 8.6 %shard_map.308.inner0_ref = f32[2,32,32,128]{3,2,1,0:T(8,128)S(1)} custom-call(bf16[34,64,256]{2,1,0:T(8,128)(2,1)S(1)} %copy-done.7, f32[7,8,256]{2,1,0:T(8,128)S(1)} %copy-done, bf16[768,192]{1,0:T(8,128)(2,1)S(1)} %copy-done.2), custom_call_target="tpu_custom_call" | custom-call | flops 8999999488 | bytes 10000000 | tf_op jit(solution)/shard_map/pallas_call | solution.py:821
  146.6 2.0 %shard_map.313 = bf16[2,32,32,256]{3,2,1,0:T(8,128)(2,1)} custom-call(f32[2,32,32,128]{3,2,1,0:T(8,128)S(1)} %shard_map.308.inner0_ref, f32[2,32,32,128]{3,2,1,0:T(8,128)S(1)} %shard_map.309.inner1_ref, f32[2,3,32,256]{3,2,1,0:T(8,128)S(1)} %get-tuple-element.21.near_ref, bf16[2,32,32,256]{3,2,1,0:T(8,128)(2,1)S(1)} %bitcast.25, ...), custom_call_target="tpu_custom_call" | custom-call | flops 5000000000 | bytes 10000000 | tf_op jit(solution)/shard_map/pallas_call | solution.py:845
  148.7 3.9 %all-to-all-done.5.got_ref = bf16[8,272,256]{2,1,0:T(8,128)(2,1)S(1)} async-done(((bf16[8,272,256]{2,1,0:T(8,128)(2,1)}), bf16[8,272,256]{2,1,0:T(8,128)(2,1)S(1)}, u32[]{:S(2)}, u32[]{:S(2)}) %all-to-all-start.5) | async-done | bytes 1114144 | tf_op jit(solution)/shard_map/all_to_all | solution.py:680
  152.5 1.7 %shard_map.315 = (f32[1024,256]{1,0:T(8,128)}, f32[256,1024]{1,0:T(8,128)}, f32[7,7,256]{2,1,0:T(8,128)}, f32[1,256]{1,0:T(1,128)}, f32[1,256]{1,0:T(1,128)}) custom-call(bf16[8,272,256]{2,1,0:T(8,128)(2,1)S(1)} %all-to-all-done.5.got_ref), custom_call_target="tpu_custom_call" | custom-call | tf_op jit(solution)/shard_map/pallas_call | solution.py:848
  (41 shorter events, 0.2 us)
Async XLA Ops:
  0.6 13.1 %copy-start.12 = (s32[1024,16]{0,1:T(8,128)S(1)}, s32[1024,16]{0,1:T(8,128)}, u32[]{:S(2)}) copy-start(s32[1024,16]{0,1:T(8,128)} %constant.168.clone) | copy-start | bytes 196612
  0.6 13.2 %copy-start.18 = (s32[1024]{0:T(1024)S(1)}, s32[1024]{0:T(1024)}, u32[]{:S(2)}) copy-start(s32[1024]{0:T(1024)} %constant.170.clone) | copy-start | bytes 12292
  0.7 13.2 %copy-start.19 = (s32[1024]{0:T(1024)S(1)}, s32[1024]{0:T(1024)}, u32[]{:S(2)}) copy-start(s32[1024]{0:T(1024)} %constant.169.clone) | copy-start | bytes 12292
  0.7 12.0 %copy-start.15 = (s32[32,4]{0,1:T(4,128)S(1)}, s32[32,4]{0,1:T(4,128)}, u32[]{:S(2)}) copy-start(s32[32,4]{0,1:T(4,128)} %param.35) | copy-start | bytes 1540
  0.7 12.0 %copy-start.21 = (s32[32,4]{0,1:T(4,128)S(1)}, s32[32,4]{0,1:T(4,128)}, u32[]{:S(2)}) copy-start(s32[32,4]{0,1:T(4,128)} %param.34) | copy-start | bytes 1540
  0.7 12.0 %copy-start.14 = (s32[32,4]{0,1:T(4,128)S(1)}, s32[32,4]{0,1:T(4,128)}, u32[]{:S(2)}) copy-start(s32[32,4]{0,1:T(4,128)} %param.37) | copy-start | bytes 1540
  0.7 12.1 %copy-start.20 = (s32[32,4]{0,1:T(4,128)S(1)}, s32[32,4]{0,1:T(4,128)}, u32[]{:S(2)}) copy-start(s32[32,4]{0,1:T(4,128)} %param.36) | copy-start | bytes 1540
  0.7 13.6 %copy-start.8 = (bf16[256,1024]{1,0:T(8,128)(2,1)S(1)}, bf16[256,1024]{1,0:T(8,128)(2,1)}, u32[]{:S(2)}) copy-start(bf16[256,1024]{1,0:T(8,128)(2,1)} %win_in.1) | copy-start | bytes 1572868
  0.7 14.6 %copy-start.9 = (bf16[1024,256]{1,0:T(8,128)(2,1)S(1)}, bf16[1024,256]{1,0:T(8,128)(2,1)}, u32[]{:S(2)}) copy-start(bf16[1024,256]{1,0:T(8,128)(2,1)} %wout_in.1) | copy-start | bytes 1572868
  4.0 12.3 %copy-start.11 = (s32[992,16]{0,1:T(8,128)S(1)}, s32[992,16]{0,1:T(8,128)}, u32[]{:S(2)}) copy-start(s32[992,16]{0,1:T(8,128)} %constant.165.clone) | copy-start | bytes 190468
  4.0 12.4 %copy-start.16 = (s32[992]{0:T(1024)S(1)}, s32[992]{0:T(1024)}, u32[]{:S(2)}) copy-start(s32[992]{0:T(1024)} %constant.167.clone) | copy-start | bytes 11908
  4.0 12.4 %copy-start.17 = (s32[992]{0:T(1024)S(1)}, s32[992]{0:T(1024)}, u32[]{:S(2)}) copy-start(s32[992]{0:T(1024)} %constant.166.clone) | copy-start | bytes 11908
  4.0 16.8 %all-to-all-start = ((bf16[16,48,256]{2,1,0:T(8,128)(2,1)}), bf16[16,48,256]{2,1,0:T(8,128)(2,1)S(1)}, u32[]{:S(2)}, u32[]{:S(2)}) async-start(bf16[16,48,256]{2,1,0:T(8,128)(2,1)} %shard_map.306), calls=%async_computation | async-start | bytes 786432 | tf_op jit(solution)/shard_map/all_to_all | solution.py:680
  15.3 11.0 %copy-start.13 = (bf16[7,7,256]{2,1,0:T(8,128)(2,1)S(1)}, bf16[7,7,256]{2,1,0:T(8,128)(2,1)}, u32[]{:S(2)}) copy-start(bf16[7,7,256]{2,1,0:T(8,128)(2,1)} %param.29) | copy-start | bytes 75268
  22.2 12.1 %all-to-all-start.1 = ((bf16[16,48,256]{2,1,0:T(8,128)(2,1)}), bf16[16,48,256]{2,1,0:T(8,128)(2,1)S(1)}, u32[]{:S(2)}, u32[]{:S(2)}) async-start(bf16[16,48,256]{2,1,0:T(8,128)(2,1)} %bitcast.6), calls=%async_computation.1 | async-start | bytes 786432 | tf_op jit(solution)/shard_map/all_to_all | solution.py:680
  34.2 0.7 copy-start.10
  75.0 8.0 %copy-start = (f32[7,8,256]{2,1,0:T(8,128)S(1)}, f32[7,8,256]{2,1,0:T(8,128)}, u32[]{:S(2)}) copy-start(f32[7,8,256]{2,1,0:T(8,128)} %pad_convert_fusion.kern_ref) | copy-start | bytes 172036
  75.0 7.9 %copy-start.2 = (bf16[768,192]{1,0:T(8,128)(2,1)S(1)}, bf16[768,192]{1,0:T(8,128)(2,1)}, u32[]{:S(2)}) copy-start(bf16[768,192]{1,0:T(8,128)(2,1)} %constant.175.clone.gsel_ref) | copy-start | bytes 884740
  75.0 7.9 %copy-start.3 = (bf16[128,128]{1,0:T(8,128)(2,1)S(1)}, bf16[128,128]{1,0:T(8,128)(2,1)}, u32[]{:S(2)}) copy-start(bf16[128,128]{1,0:T(8,128)(2,1)} %constant.176.clone.rsel_ref) | copy-start | bytes 98308
  75.0 7.9 %copy-start.5 = (bf16[34,64,256]{2,1,0:T(8,128)(2,1)S(1)}, bf16[34,64,256]{2,1,0:T(8,128)(2,1)}, u32[]{:S(2)}) copy-start(bf16[34,64,256]{2,1,0:T(8,128)(2,1)} %get-tuple-element.20.gz_in.gz_ref) | copy-start | bytes 3342340
  75.0 23.7 %all-to-all-start.2 = ((bf16[8,272,256]{2,1,0:T(8,128)(2,1)}), bf16[8,272,256]{2,1,0:T(8,128)(2,1)S(1)}, u32[]{:S(2)}, u32[]{:S(2)}) async-start(bf16[8,272,256]{2,1,0:T(8,128)(2,1)} %get-tuple-element.23), calls=%async_computation.2 | async-start | bytes 2228224 | tf_op jit(solution)/shard_map/all_to_all | solution.py:680
  99.7 15.2 %all-to-all-start.3 = ((bf16[16,80,256]{2,1,0:T(8,128)(2,1)}), bf16[16,80,256]{2,1,0:T(8,128)(2,1)S(1)}, u32[]{:S(2)}, u32[]{:S(2)}) async-start(bf16[16,80,256]{2,1,0:T(8,128)(2,1)} %shard_map.311), calls=%async_computation.3 | async-start | bytes 1310720 | tf_op jit(solution)/shard_map/all_to_all | solution.py:680
  116.2 13.5 %all-to-all-start.4 = ((bf16[16,64,256]{2,1,0:T(8,128)(2,1)}), bf16[16,64,256]{2,1,0:T(8,128)(2,1)S(1)}, u32[]{:S(2)}, u32[]{:S(2)}) async-start(bf16[16,64,256]{2,1,0:T(8,128)(2,1)} %get-tuple-element.24), calls=%async_computation.4 | async-start | bytes 1048576 | tf_op jit(solution)/shard_map/all_to_all | solution.py:680
  119.8 1.2 copy-start.6
  130.8 21.8 %all-to-all-start.5 = ((bf16[8,272,256]{2,1,0:T(8,128)(2,1)}), bf16[8,272,256]{2,1,0:T(8,128)(2,1)S(1)}, u32[]{:S(2)}, u32[]{:S(2)}) async-start(bf16[8,272,256]{2,1,0:T(8,128)(2,1)} %shard_map.314), calls=%async_computation.5 | async-start | bytes 2228224 | tf_op jit(solution)/shard_map/all_to_all | solution.py:680
  136.7 1.2 copy-start.7
  138.0 8.6 %copy-start.1 = (bf16[1,2,32,32,256]{4,3,2,1,0:T(8,128)(2,1)S(1)}, bf16[1,2,32,32,256]{4,3,2,1,0:T(8,128)(2,1)}, u32[]{:S(2)}) copy-start(bf16[1,2,32,32,256]{4,3,2,1,0:T(8,128)(2,1)} %param.28) | copy-start | bytes 3145732
  138.0 8.6 %copy-start.4 = (s32[1,768]{1,0:T(1,128)S(1)}, s32[1,768]{1,0:T(1,128)}, u32[]{:S(2)}) copy-start(s32[1,768]{1,0:T(1,128)} %constant.177.clone.pixel_ref) | copy-start | bytes 9220

commit v4 on v3

--- a/solution.py
+++ b/solution.py
@@ -255,7 +255,7 @@
     fields_in,
     og_in,
     recv_in,
-    rim_in,
+    row_ref,
     kern_ref,
     gain_ref,
     shift_ref,
@@ -271,7 +271,6 @@
     gz_out,
     fields_ref,
     recv_ref,
-    rim_ref,
     og_ref,
     win_ref,
     wout_ref,
@@ -299,10 +298,17 @@
 ):
     copies = fetch(
         [
-            (rim_in, rim_ref),
             (recv_in, recv_ref),
             (fields_in, fields_ref),
             (psel_in, psel_ref),
+        ],
+        sems,
+    )
+    build_weights(kern_ref, w_ref, False)
+    for copy in copies:
+        copy.wait()
+    copies = fetch(
+        [
             (og_in, og_ref),
             (split_in, split_ref),
             (win_in, win_ref),
@@ -313,9 +319,6 @@
         ],
         sems,
     )
-    build_weights(kern_ref, w_ref, False)
-    for copy in copies[:4]:
-        copy.wait()
     source = jnp.concatenate(
         [
             recv_ref[...].reshape(SENT, C),
@@ -325,10 +328,14 @@
         axis=0,
     )
     outer = 6 * T * N
-    rims = dot(rim_ref[0:outer], source).astype(BF).reshape(6, T, N, C)
+    row = jnp.broadcast_to(row_ref[...], (8, row_ref.shape[1])).T[:, 0:1]
+    columns = lax.broadcasted_iota(jnp.int32, (row.shape[0], SENT + LOCAL), 1)
+    pick = jnp.where(columns == row, 1.0, 0.0).astype(BF)
+    rims = dot(pick, source)
+    rims, sides = rims[:outer].astype(BF).reshape(6, T, N, C), rims[outer:]
     mid_ref[0:3] = rims[0:3]
     mid_ref[N + 3 :] = rims[3:6]
-    side_ref[...] = dot(rim_ref[outer:], source).astype(BF).reshape(N + 6, T * SIDE, C)
+    side_ref[...] = sides.astype(BF).reshape(N + 6, T * SIDE, C)
     for t in range(T):
         mid_ref[3 : N + 3, t] = fields_ref[t]
 
@@ -347,10 +354,11 @@
                 spread(picked[at : at + 128], q_ref, 2 * i + v, t * 16)
         return carry
 
-    lax.fori_loop(0, (N + 6) // 2, pairs, 0)
-
-    copies[4].wait()
-    copies[5].wait()
+    for i in range((N + 6) // 2):
+        pairs(i, 0)
+
+    copies[0].wait()
+    copies[1].wait()
 
     def order(m, carry):
         for t in range(T):
@@ -362,7 +370,8 @@
                 )
         return carry
 
-    lax.fori_loop(0, 4, order, 0)
+    for m in range(4):
+        order(m, 0)
 
     def conv(m, carry):
         for h in range(2):
@@ -382,7 +391,7 @@
 
     lax.fori_loop(0, 4, conv, 0)
 
-    for copy in copies[6:]:
+    for copy in copies[2:]:
         copy.wait()
     gwin_ref[...] = jnp.zeros_like(gwin_ref)
     gwout_ref[...] = jnp.zeros_like(gwout_ref)
@@ -393,36 +402,36 @@
     shift = shift_ref[...]
 
     def mlp(m, carry):
-        rows = pl.ds(m * 4, 4)
-        z = z_ref[rows].reshape(256, C)
+        rows = pl.ds(m * 8, 8)
+        z = z_ref[rows].reshape(512, C)
         average = jnp.mean(z, axis=1, keepdims=True)
         centered = z - average
         variance = jnp.mean(centered * centered, axis=1, keepdims=True)
         inv_std = lax.rsqrt(variance + 1e-06)
         normed = centered * inv_std
         zn = (normed * gain + shift).astype(BF)
-        og = o_ref[rows].reshape(256, C)
+        og = o_ref[rows].reshape(512, C)
         hidden = dot(zn, win_ref[...])
         cdf = 0.5 * (1.0 + lax.erf(hidden * (1.0 / math.sqrt(2.0))))
         pdf = jnp.exp(-0.5 * hidden * hidden) * (1.0 / math.sqrt(2.0 * math.pi))
         act = (hidden * cdf).astype(BF)
         slope = cdf + hidden * pdf
-        out = x_ref[rows].reshape(256, C).astype(F32) + dot(act, wout_ref[...])
-        x_ref[rows] = out.astype(BF).reshape(4, 64, C)
+        out = x_ref[rows].reshape(512, C).astype(F32) + dot(act, wout_ref[...])
+        x_ref[rows] = out.astype(BF).reshape(8, 64, C)
         grad_hidden = (dot(og, wout_t_ref[...]) * slope).astype(BF)
         gwout_ref[...] += dot(og.T, act)
         gwin_ref[...] += dot(zn.T, grad_hidden)
         grad_normed = dot(grad_hidden, win_t_ref[...])
-        gains_ref[0:8] += jnp.sum((grad_normed * normed).reshape(32, 8, C), axis=0)
-        gains_ref[8:16] += jnp.sum(grad_normed.reshape(32, 8, C), axis=0)
+        gains_ref[0:8] += jnp.sum((grad_normed * normed).reshape(64, 8, C), axis=0)
+        gains_ref[8:16] += jnp.sum(grad_normed.reshape(64, 8, C), axis=0)
         scaled = grad_normed * gain
         grad_z = inv_std * (
             scaled
             - jnp.mean(scaled, axis=1, keepdims=True)
             - normed * jnp.mean(scaled * normed, axis=1, keepdims=True)
         )
-        grad_z = grad_z.astype(BF).reshape(4, 64, C)
-        gz_ref[pl.ds(m * 4 + 1, 4)] = grad_z
+        grad_z = grad_z.astype(BF).reshape(8, 64, C)
+        gz_ref[pl.ds(m * 8 + 1, 8)] = grad_z
         for h in range(2):
             for t in range(T):
                 for u in range(2):
@@ -431,7 +440,8 @@
                     ]
         return carry
 
-    lax.fori_loop(0, 8, mlp, 0)
+    for m in range(4):
+        mlp(m, 0)
 
     def unorder(m, carry):
         for t in range(T):
@@ -440,7 +450,8 @@
             result_ref[t, rows] = dot(merge_ref[...], block).astype(BF).reshape(8, 32, C)
         return carry
 
-    lax.fori_loop(0, 4, unorder, 0)
+    for m in range(4):
+        unorder(m, 0)
     copies = fetch([(result_ref, result_out), (gz_ref, gz_out)], sems)
 
     for h in range(2):
@@ -468,7 +479,8 @@
             small_ref[a, :, h * HALF : (h + 1) * HALF] = jnp.concatenate(rows, axis=0)
         return carry
 
-    lax.fori_loop(0, 7, taps, 0)
+    for a in range(7):
+        taps(a, 0)
     small_ref[7] = jnp.concatenate(
         [
             jnp.sum(gains_ref[0:8], axis=0, keepdims=True),
@@ -515,7 +527,8 @@
         spread(picked[128:256], r_ref.at[1], 2 + i, 0)
         return carry
 
-    lax.fori_loop(0, 16, rim_pairs, 0)
+    for i in range(16):
+        rim_pairs(i, 0)
     last = dot(rsel_ref[...], gz_ref[N : N + 2].reshape(128, C)).astype(BF)
     spread(last, r_ref.at[1], 18, 0)
     for first, row in ((0, 6), (1, 7), (29, 9), (30, 10)):
@@ -575,7 +588,8 @@
                     g_ref[3 + 2 * i + v, rows, lanes] = picked[at : at + 16]
         return carry
 
-    lax.fori_loop(0, 16, pairs, 0)
+    for i in range(16):
+        pairs(i, 0)
 
     def inside(m, carry):
         acc = None
@@ -723,7 +737,6 @@
     ).reshape(-1)
     pick = (source[:, None] == jnp.arange(SENT, dtype=jnp.int32)).astype(BF)
     rim_rows = rows_of(tables_of(forward_rim_pixels()), flags)
-    rim = (rim_rows[:, None] == jnp.arange(SENT + LOCAL, dtype=jnp.int32)).astype(BF)
     edge_rows = rows_of(tables_of(backward_rim_pixels()), flags)
     pixels = source_pixels()
 
@@ -756,7 +769,6 @@
         scratch=(
             pltpu.VMEM((T, N, N, C), BF),
             pltpu.VMEM((PARTS, KB, C), BF),
-            pltpu.VMEM(rim.shape, BF),
             pltpu.VMEM((T, N, N, C), BF),
             pltpu.VMEM((C, HID), BF),
             pltpu.VMEM((HID, C), BF),
@@ -780,9 +792,9 @@
             pltpu.VMEM((2, N, 32, 256), BF),
             pltpu.VMEM((2, 256, 1024), BF),
             pltpu.VMEM((8, 8, C), F32),
-            pltpu.SemaphoreType.DMA((11,)),
+            pltpu.SemaphoreType.DMA((7,)),
         ),
-        in_specs=[hbm] * 4 + [vm] * 3 + [hbm] * 7,
+        in_specs=[hbm] * 3 + [vm] * 4 + [hbm] * 7,
         out_specs=(hbm, vm, hbm),
         flops=40_000_000_000,
         vmem=60,
@@ -790,7 +802,7 @@
         x,
         og,
         got,
-        rim,
+        rim_rows[None],
         taps,
         ln_gain[None],
         ln_shift[None],

time: 155 us -> 148 us (0.955)
  Pallas kernels: 76.5 us -> 62 us
  waiting for transfers between devices: 32.3 us -> 39.6 us
    pallas_call x1, Pallas kernels: 40 us -> 32.6 us  [body(): call(forward_kernel, (shape((T, N, N, C), BF), shape((reps, 272, C), BF),...]
    all_to_all x6, waiting for transfers between devices: 32.3 us -> 39.6 us  [swap(): return lax.all_to_all(array, axes, 0, 0, tiled=True)]
    pallas_call x2, Pallas kernels: 17.3 us -> 12.8 us  [body(): call(functools.partial(inside_kernel, h), shape((T, N, N, HALF), F32), sc...]
    pallas_call x1, Pallas kernels: 8.94 us -> 6.43 us  [body(): call(rims_kernel, (shape((PARTS, KB, C), BF), shape((2, 3, N, C), F32)),...]
    convert_element_type x1 -> x0, other arithmetic: 1.7 us -> none  [body(): (rim_rows[:, None] == jnp.arange(SENT + LOCAL, dtype=jnp.int32)).astype(BF)]
  transfers between devices with their start and end apart: 6 -> 6, of which waited for: 5 -> 6; matrix products, arithmetic and copies ran while one was open for 4% -> 3% of each run, Pallas kernels for 18% -> 14%
where the time goes in v4:
time: 148 us; the launch traced here: 147 us
  Pallas kernels  62 us (42%)
  waiting for transfers between devices  39.6 us (27%)
  starting transfers between devices  34.5 us (23%)
  local copies, waits for them, and re-layouts  6.79 us (5%)
  other arithmetic  1.54 us (1%)
    all_to_all x6, waiting for transfers between devices, swap(): return lax.all_to_all(array, axes, 0, 0, tiled=True)  39.6 us
    all_to_all x6, starting transfers between devices, swap(): return lax.all_to_all(array, axes, 0, 0, tiled=True)  34.5 us
    pallas_call x1, Pallas kernels, body(): call(forward_kernel, (shape((T, N, N, C), BF), shape((reps, 272, C), BF),...  32.6 us
    pallas_call x2, Pallas kernels, body(): call(functools.partial(inside_kernel, h), shape((T, N, N, HALF), F32), sc...  12.8 us
    pallas_call x1, Pallas kernels, body(): call(rims_kernel, (shape((PARTS, KB, C), BF), shape((2, 3, N, C), F32)),...  6.43 us
    unnamed x46, local copies, waits for them, and re-layouts  5.33 us
    pallas_call x1, Pallas kernels, body(): call(pack_kernel, shape((PARTS, KB, C), BF), scratch=(pltpu.VMEM((T, N, N...  3.18 us
  transfers between devices with their start and end apart: 6, of which 6 were waited for; matrix products, arithmetic and copies ran while one was open for 3% of the time, Pallas kernels for 14%

profile of v4, /device:TPU:1, one launch (start us, length us, event | category | flops | bytes accessed | tf_op | source)
XLA Modules:
  0.0 146.7 jit_solution(14394436526943105027)
XLA Ops:
  0.6 0.0 copy-start.15
  0.6 0.0 copy-start.21
  0.7 0.0 copy-start.14
  0.7 0.0 copy-start.20
  0.7 0.0 copy-start.12
  0.7 0.0 copy-start.18
  0.7 0.0 copy-start.19
  0.7 3.2 %shard_map.306 = bf16[16,48,256]{2,1,0:T(8,128)(2,1)} custom-call(bf16[2,32,32,256]{3,2,1,0:T(8,128)(2,1)} %bitcast.27, s32[768,1]{1,0:T(8,128)} %constant.171.clone.pixel_in), custom_call_target="tpu_custom_call" | custom-call | tf_op jit(solution)/shard_map/pallas_call | solution.py:745
  3.9 8.4 %all-to-all-start = ((bf16[16,48,256]{2,1,0:T(8,128)(2,1)}), bf16[16,48,256]{2,1,0:T(8,128)(2,1)S(1)}, u32[]{:S(2)}, u32[]{:S(2)}) async-start(bf16[16,48,256]{2,1,0:T(8,128)(2,1)} %shard_map.306), calls=%async_computation | async-start | bytes 786432 | tf_op jit(solution)/shard_map/all_to_all | solution.py:694
  12.4 0.1 add.179
  12.4 0.0 copy-done.21
  12.5 0.1 add.203
  12.6 0.1 copy.82
  12.7 0.1 add.175
  12.8 0.1 copy.77
  12.9 0.1 add.192
  13.0 0.1 copy.80
  13.1 0.1 copy.78
  13.2 0.1 broadcast_add_fusion
  13.3 0.1 constant_dynamic-slice_fusion
  13.4 0.1 copy.88
  13.4 0.1 mul.68
  13.5 0.1 copy.87
  13.6 0.1 copy.85
  13.7 0.1 copy.83
  13.8 0.1 concatenate.6
  13.9 0.1 eq.74
  13.9 0.1 multiply_reduce_fusion
  14.1 6.5 %all-to-all-done = bf16[16,48,256]{2,1,0:T(8,128)(2,1)S(1)} async-done(((bf16[16,48,256]{2,1,0:T(8,128)(2,1)}), bf16[16,48,256]{2,1,0:T(8,128)(2,1)S(1)}, u32[]{:S(2)}, u32[]{:S(2)}) %all-to-all-start) | async-done | bytes 393248 | tf_op jit(solution)/shard_map/all_to_all | solution.py:694
  20.6 1.3 fusion.1
  21.9 4.2 %all-to-all-start.1 = ((bf16[16,48,256]{2,1,0:T(8,128)(2,1)}), bf16[16,48,256]{2,1,0:T(8,128)(2,1)S(1)}, u32[]{:S(2)}, u32[]{:S(2)}) async-start(bf16[16,48,256]{2,1,0:T(8,128)(2,1)} %bitcast.6), calls=%async_computation.1 | async-start | bytes 786432 | tf_op jit(solution)/shard_map/all_to_all | solution.py:694
  26.2 0.0 copy-start.11
  26.2 0.0 copy-start.16
  26.2 0.0 copy-start.17
  26.2 0.6 pad_convert_fusion.kern_ref
  26.8 1.0 copy.89
  27.8 1.0 copy.90
  28.8 0.1 multiply_reduce_fusion.1
  29.0 0.6 compare_select_fusion.1
  29.5 4.6 %all-to-all-done.1.recv_in = bf16[16,48,256]{2,1,0:T(8,128)(2,1)S(1)} async-done(((bf16[16,48,256]{2,1,0:T(8,128)(2,1)}), bf16[16,48,256]{2,1,0:T(8,128)(2,1)S(1)}, u32[]{:S(2)}, u32[]{:S(2)}) %all-to-all-start.1) | async-done | bytes 393248 | tf_op jit(solution)/shard_map/all_to_all | solution.py:694
  34.1 0.7 copy-done.10
  34.9 32.6 %shard_map.307 = (bf16[2,32,32,256]{3,2,1,0:T(8,128)(2,1)}, bf16[8,272,256]{2,1,0:T(8,128)(2,1)}, bf16[34,64,256]{2,1,0:T(8,128)(2,1)}) custom-call(bf16[2,32,32,256]{3,2,1,0:T(8,128)(2,1)} %bitcast.28, bf16[2,32,32,256]{3,2,1,0:T(8,128)(2,1)} %bitcast.25, bf16[16,48,256]{2,1,0:T(8,128)(2,1)} %copy-done.10, s32[1,992]{1,0:T(1,128)} %bitcast.35, ...), custom_call_target="tpu_custom_call" | custom-call | flops 40000000000 | bytes 10000000 | tf_op jit(solution)/shard_map/pallas_call | solution.py:762
  67.5 0.0 copy-start
  67.5 0.0 copy-start.2
  67.5 0.0 copy-start.3
  67.5 7.9 %all-to-all-start.2 = ((bf16[8,272,256]{2,1,0:T(8,128)(2,1)}), bf16[8,272,256]{2,1,0:T(8,128)(2,1)S(1)}, u32[]{:S(2)}, u32[]{:S(2)}) async-start(bf16[8,272,256]{2,1,0:T(8,128)(2,1)} %get-tuple-element.23), calls=%async_computation.2 | async-start | bytes 2228224 | tf_op jit(solution)/shard_map/all_to_all | solution.py:694
  75.5 6.4 %shard_map.310 = (bf16[16,48,256]{2,1,0:T(8,128)(2,1)S(1)}, f32[2,3,32,256]{3,2,1,0:T(8,128)S(1)}) custom-call(bf16[34,64,256]{2,1,0:T(8,128)(2,1)S(1)} %copy-done.5, f32[7,8,256]{2,1,0:T(8,128)S(1)} %copy-done, s32[1,1024]{1,0:T(1,128)S(1)} %bitcast.24, bf16[768,192]{1,0:T(8,128)(2,1)S(1)} %copy-done.2, bf16[128,128]{1,0:T(8,128)(2,1)S(1)} %copy-done.3), custom_call_target="tpu_custom_call" | custom-call | flops 12000000000 | bytes 10000000 | tf_op jit(solution)/shard_map/pallas_call | solution.py:820
  81.9 9.3 %all-to-all-done.2.wide_ref = bf16[8,272,256]{2,1,0:T(8,128)(2,1)S(1)} async-done(((bf16[8,272,256]{2,1,0:T(8,128)(2,1)}), bf16[8,272,256]{2,1,0:T(8,128)(2,1)S(1)}, u32[]{:S(2)}, u32[]{:S(2)}) %all-to-all-start.2) | async-done | bytes 1114144 | tf_op jit(solution)/shard_map/all_to_all | solution.py:694
  91.2 1.0 shard_map.311
  92.3 3.6 %all-to-all-start.3 = ((bf16[16,80,256]{2,1,0:T(8,128)(2,1)}), bf16[16,80,256]{2,1,0:T(8,128)(2,1)S(1)}, u32[]{:S(2)}, u32[]{:S(2)}) async-start(bf16[16,80,256]{2,1,0:T(8,128)(2,1)} %shard_map.311), calls=%async_computation.3 | async-start | bytes 1310720 | tf_op jit(solution)/shard_map/all_to_all | solution.py:694
  95.9 0.1 broadcast_in_dim_reshape.4.source_ref
  95.9 11.5 %all-to-all-done.3.got_ref = bf16[16,80,256]{2,1,0:T(8,128)(2,1)S(1)} async-done(((bf16[16,80,256]{2,1,0:T(8,128)(2,1)}), bf16[16,80,256]{2,1,0:T(8,128)(2,1)S(1)}, u32[]{:S(2)}, u32[]{:S(2)}) %all-to-all-start.3) | async-done | bytes 655392 | tf_op jit(solution)/shard_map/all_to_all | solution.py:694
  107.5 1.3 shard_map.312
  108.7 3.6 %all-to-all-start.4 = ((bf16[16,64,256]{2,1,0:T(8,128)(2,1)}), bf16[16,64,256]{2,1,0:T(8,128)(2,1)S(1)}, u32[]{:S(2)}, u32[]{:S(2)}) async-start(bf16[16,64,256]{2,1,0:T(8,128)(2,1)} %get-tuple-element.24), calls=%async_computation.4 | async-start | bytes 1048576 | tf_op jit(solution)/shard_map/all_to_all | solution.py:694
  112.3 1.2 copy-done.6
  113.6 6.4 %shard_map.309.inner1_ref = f32[2,32,32,128]{3,2,1,0:T(8,128)S(1)} custom-call(bf16[34,64,256]{2,1,0:T(8,128)(2,1)S(1)} %copy-done.6, f32[7,8,256]{2,1,0:T(8,128)S(1)} %copy-done, bf16[768,192]{1,0:T(8,128)(2,1)S(1)} %copy-done.2), custom_call_target="tpu_custom_call" | custom-call | flops 8999999488 | bytes 10000000 | tf_op jit(solution)/shard_map/pallas_call | solution.py:833
  119.9 1.5 %all-to-all-done.4.recv_ref.got_ref = bf16[16,64,256]{2,1,0:T(8,128)(2,1)S(1)} async-done(((bf16[16,64,256]{2,1,0:T(8,128)(2,1)}), bf16[16,64,256]{2,1,0:T(8,128)(2,1)S(1)}, u32[]{:S(2)}, u32[]{:S(2)}) %all-to-all-start.4) | async-done | bytes 524320 | tf_op jit(solution)/shard_map/all_to_all | solution.py:694
  121.5 1.1 shard_map.314
  122.5 6.7 %all-to-all-start.5 = ((bf16[8,272,256]{2,1,0:T(8,128)(2,1)}), bf16[8,272,256]{2,1,0:T(8,128)(2,1)S(1)}, u32[]{:S(2)}, u32[]{:S(2)}) async-start(bf16[8,272,256]{2,1,0:T(8,128)(2,1)} %shard_map.314), calls=%async_computation.5 | async-start | bytes 2228224 | tf_op jit(solution)/shard_map/all_to_all | solution.py:694
  129.2 1.2 copy-done.7
  130.5 6.4 %shard_map.308.inner0_ref = f32[2,32,32,128]{3,2,1,0:T(8,128)S(1)} custom-call(bf16[34,64,256]{2,1,0:T(8,128)(2,1)S(1)} %copy-done.7, f32[7,8,256]{2,1,0:T(8,128)S(1)} %copy-done, bf16[768,192]{1,0:T(8,128)(2,1)S(1)} %copy-done.2), custom_call_target="tpu_custom_call" | custom-call | flops 8999999488 | bytes 10000000 | tf_op jit(solution)/shard_map/pallas_call | solution.py:833
  136.9 2.0 %shard_map.313 = bf16[2,32,32,256]{3,2,1,0:T(8,128)(2,1)} custom-call(f32[2,32,32,128]{3,2,1,0:T(8,128)S(1)} %shard_map.308.inner0_ref, f32[2,32,32,128]{3,2,1,0:T(8,128)S(1)} %shard_map.309.inner1_ref, f32[2,3,32,256]{3,2,1,0:T(8,128)S(1)} %get-tuple-element.21.near_ref, bf16[2,32,32,256]{3,2,1,0:T(8,128)(2,1)S(1)} %bitcast.26, ...), custom_call_target="tpu_custom_call" | custom-call | flops 5000000000 | bytes 10000000 | tf_op jit(solution)/shard_map/pallas_call | solution.py:857
  138.9 6.1 %all-to-all-done.5.got_ref = bf16[8,272,256]{2,1,0:T(8,128)(2,1)S(1)} async-done(((bf16[8,272,256]{2,1,0:T(8,128)(2,1)}), bf16[8,272,256]{2,1,0:T(8,128)(2,1)S(1)}, u32[]{:S(2)}, u32[]{:S(2)}) %all-to-all-start.5) | async-done | bytes 1114144 | tf_op jit(solution)/shard_map/all_to_all | solution.py:694
  145.1 1.7 %shard_map.315 = (f32[1024,256]{1,0:T(8,128)}, f32[256,1024]{1,0:T(8,128)}, f32[7,7,256]{2,1,0:T(8,128)}, f32[1,256]{1,0:T(1,128)}, f32[1,256]{1,0:T(1,128)}) custom-call(bf16[8,272,256]{2,1,0:T(8,128)(2,1)S(1)} %all-to-all-done.5.got_ref), custom_call_target="tpu_custom_call" | custom-call | tf_op jit(solution)/shard_map/pallas_call | solution.py:860
  (40 shorter events, 0.2 us)
Async XLA Ops:
  0.6 11.8 %copy-start.15 = (s32[32,4]{0,1:T(4,128)S(1)}, s32[32,4]{0,1:T(4,128)}, u32[]{:S(2)}) copy-start(s32[32,4]{0,1:T(4,128)} %param.35) | copy-start | bytes 1540
  0.6 11.8 %copy-start.21 = (s32[32,4]{0,1:T(4,128)S(1)}, s32[32,4]{0,1:T(4,128)}, u32[]{:S(2)}) copy-start(s32[32,4]{0,1:T(4,128)} %param.34) | copy-start | bytes 1540
  0.7 11.8 %copy-start.14 = (s32[32,4]{0,1:T(4,128)S(1)}, s32[32,4]{0,1:T(4,128)}, u32[]{:S(2)}) copy-start(s32[32,4]{0,1:T(4,128)} %param.37) | copy-start | bytes 1540
  0.7 11.9 %copy-start.20 = (s32[32,4]{0,1:T(4,128)S(1)}, s32[32,4]{0,1:T(4,128)}, u32[]{:S(2)}) copy-start(s32[32,4]{0,1:T(4,128)} %param.36) | copy-start | bytes 1540
  0.7 13.3 %copy-start.12 = (s32[1024,16]{0,1:T(8,128)S(1)}, s32[1024,16]{0,1:T(8,128)}, u32[]{:S(2)}) copy-start(s32[1024,16]{0,1:T(8,128)} %constant.168.clone) | copy-start | bytes 196612
  0.7 13.3 %copy-start.18 = (s32[1024]{0:T(1024)S(1)}, s32[1024]{0:T(1024)}, u32[]{:S(2)}) copy-start(s32[1024]{0:T(1024)} %constant.170.clone) | copy-start | bytes 12292
  0.7 13.3 %copy-start.19 = (s32[1024]{0:T(1024)S(1)}, s32[1024]{0:T(1024)}, u32[]{:S(2)}) copy-start(s32[1024]{0:T(1024)} %constant.169.clone) | copy-start | bytes 12292
  3.9 16.7 %all-to-all-start = ((bf16[16,48,256]{2,1,0:T(8,128)(2,1)}), bf16[16,48,256]{2,1,0:T(8,128)(2,1)S(1)}, u32[]{:S(2)}, u32[]{:S(2)}) async-start(bf16[16,48,256]{2,1,0:T(8,128)(2,1)} %shard_map.306), calls=%async_computation | async-start | bytes 786432 | tf_op jit(solution)/shard_map/all_to_all | solution.py:694
  20.6 5.6 %copy-start.13 = (bf16[7,7,256]{2,1,0:T(8,128)(2,1)S(1)}, bf16[7,7,256]{2,1,0:T(8,128)(2,1)}, u32[]{:S(2)}) copy-start(bf16[7,7,256]{2,1,0:T(8,128)(2,1)} %param.29) | copy-start | bytes 75268
  20.6 6.2 %copy-start.8 = (bf16[256,1024]{1,0:T(8,128)(2,1)S(1)}, bf16[256,1024]{1,0:T(8,128)(2,1)}, u32[]{:S(2)}) copy-start(bf16[256,1024]{1,0:T(8,128)(2,1)} %win_in.1) | copy-start | bytes 1572868
  21.9 5.9 %copy-start.9 = (bf16[1024,256]{1,0:T(8,128)(2,1)S(1)}, bf16[1024,256]{1,0:T(8,128)(2,1)}, u32[]{:S(2)}) copy-start(bf16[1024,256]{1,0:T(8,128)(2,1)} %wout_in.1) | copy-start | bytes 1572868
  21.9 12.2 %all-to-all-start.1 = ((bf16[16,48,256]{2,1,0:T(8,128)(2,1)}), bf16[16,48,256]{2,1,0:T(8,128)(2,1)S(1)}, u32[]{:S(2)}, u32[]{:S(2)}) async-start(bf16[16,48,256]{2,1,0:T(8,128)(2,1)} %bitcast.6), calls=%async_computation.1 | async-start | bytes 786432 | tf_op jit(solution)/shard_map/all_to_all | solution.py:694
  26.2 2.7 %copy-start.11 = (s32[992,16]{0,1:T(8,128)S(1)}, s32[992,16]{0,1:T(8,128)}, u32[]{:S(2)}) copy-start(s32[992,16]{0,1:T(8,128)} %constant.165.clone) | copy-start | bytes 190468
  26.2 2.8 %copy-start.16 = (s32[992]{0:T(1024)S(1)}, s32[992]{0:T(1024)}, u32[]{:S(2)}) copy-start(s32[992]{0:T(1024)} %constant.167.clone) | copy-start | bytes 11908
  26.2 2.8 %copy-start.17 = (s32[992]{0:T(1024)S(1)}, s32[992]{0:T(1024)}, u32[]{:S(2)}) copy-start(s32[992]{0:T(1024)} %constant.166.clone) | copy-start | bytes 11908
  34.1 0.7 copy-start.10
  67.5 8.0 %copy-start = (f32[7,8,256]{2,1,0:T(8,128)S(1)}, f32[7,8,256]{2,1,0:T(8,128)}, u32[]{:S(2)}) copy-start(f32[7,8,256]{2,1,0:T(8,128)} %pad_convert_fusion.kern_ref) | copy-start | bytes 172036
  67.5 8.0 %copy-start.2 = (bf16[768,192]{1,0:T(8,128)(2,1)S(1)}, bf16[768,192]{1,0:T(8,128)(2,1)}, u32[]{:S(2)}) copy-start(bf16[768,192]{1,0:T(8,128)(2,1)} %constant.175.clone.gsel_ref) | copy-start | bytes 884740
  67.5 7.9 %copy-start.3 = (bf16[128,128]{1,0:T(8,128)(2,1)S(1)}, bf16[128,128]{1,0:T(8,128)(2,1)}, u32[]{:S(2)}) copy-start(bf16[128,128]{1,0:T(8,128)(2,1)} %constant.176.clone.rsel_ref) | copy-start | bytes 98308
  67.5 7.9 %copy-start.5 = (bf16[34,64,256]{2,1,0:T(8,128)(2,1)S(1)}, bf16[34,64,256]{2,1,0:T(8,128)(2,1)}, u32[]{:S(2)}) copy-start(bf16[34,64,256]{2,1,0:T(8,128)(2,1)} %get-tuple-element.20.gz_in.gz_ref) | copy-start | bytes 3342340
  67.5 23.7 %all-to-all-start.2 = ((bf16[8,272,256]{2,1,0:T(8,128)(2,1)}), bf16[8,272,256]{2,1,0:T(8,128)(2,1)S(1)}, u32[]{:S(2)}, u32[]{:S(2)}) async-start(bf16[8,272,256]{2,1,0:T(8,128)(2,1)} %get-tuple-element.23), calls=%async_computation.2 | async-start | bytes 2228224 | tf_op jit(solution)/shard_map/all_to_all | solution.py:694
  92.3 15.2 %all-to-all-start.3 = ((bf16[16,80,256]{2,1,0:T(8,128)(2,1)}), bf16[16,80,256]{2,1,0:T(8,128)(2,1)S(1)}, u32[]{:S(2)}, u32[]{:S(2)}) async-start(bf16[16,80,256]{2,1,0:T(8,128)(2,1)} %shard_map.311), calls=%async_computation.3 | async-start | bytes 1310720 | tf_op jit(solution)/shard_map/all_to_all | solution.py:694
  108.7 12.7 %all-to-all-start.4 = ((bf16[16,64,256]{2,1,0:T(8,128)(2,1)}), bf16[16,64,256]{2,1,0:T(8,128)(2,1)S(1)}, u32[]{:S(2)}, u32[]{:S(2)}) async-start(bf16[16,64,256]{2,1,0:T(8,128)(2,1)} %get-tuple-element.24), calls=%async_computation.4 | async-start | bytes 1048576 | tf_op jit(solution)/shard_map/all_to_all | solution.py:694
  112.3 1.2 copy-start.6
  122.5 22.5 %all-to-all-start.5 = ((bf16[8,272,256]{2,1,0:T(8,128)(2,1)}), bf16[8,272,256]{2,1,0:T(8,128)(2,1)S(1)}, u32[]{:S(2)}, u32[]{:S(2)}) async-start(bf16[8,272,256]{2,1,0:T(8,128)(2,1)} %shard_map.314), calls=%async_computation.5 | async-start | bytes 2228224 | tf_op jit(solution)/shard_map/all_to_all | solution.py:694
  129.2 1.2 copy-start.7
  130.5 6.4 %copy-start.1 = (bf16[1,2,32,32,256]{4,3,2,1,0:T(8,128)(2,1)S(1)}, bf16[1,2,32,32,256]{4,3,2,1,0:T(8,128)(2,1)}, u32[]{:S(2)}) copy-start(bf16[1,2,32,32,256]{4,3,2,1,0:T(8,128)(2,1)} %param.28) | copy-start | bytes 3145732
  130.5 6.4 %copy-start.4 = (s32[1,768]{1,0:T(1,128)S(1)}, s32[1,768]{1,0:T(1,128)}, u32[]{:S(2)}) copy-start(s32[1,768]{1,0:T(1,128)} %constant.177.clone.pixel_ref) | copy-start | bytes 9220

commit v5 on v4

--- a/solution.py
+++ b/solution.py
@@ -199,6 +199,10 @@
     return copies
 
 
+def column_of(row):
+    return jnp.broadcast_to(row, (8, row.shape[1])).T[:, 0:1]
+
+
 def pack_kernel(fields_in, pixel_in, out_ref, fields_ref, pixel_ref, sems):
     for copy in fetch([(pixel_in, pixel_ref), (fields_in, fields_ref)], sems):
         copy.wait()
@@ -209,6 +213,17 @@
         columns = lax.broadcasted_iota(jnp.int32, (rows, T * N * N), 1)
         pick = jnp.where(columns == pixel, 1.0, 0.0).astype(BF)
         out_ref[m * 4 : (m + 1) * 4] = dot(pick, x).astype(BF).reshape(4, KB, C)
+
+
+def order_kernel(fields_ref, og_ref, split_ref, x_ref, o_ref):
+    for m in range(4):
+        for t in range(T):
+            rows = slice(m * 8, (m + 1) * 8)
+            for src, dst in ((fields_ref, x_ref), (og_ref, o_ref)):
+                block = src[t, rows].reshape(256, C)
+                dst[rows, t * 32 : (t + 1) * 32] = (
+                    dot(split_ref[...], block).astype(BF).reshape(8, 32, C)
+                )
 
 
 def build_weights(kern_ref, w_ref, mirrored, halves=(0, 1)):
@@ -253,7 +268,8 @@
 
 def forward_kernel(
     fields_in,
-    og_in,
+    x_in,
+    o_in,
     recv_in,
     row_ref,
     kern_ref,
@@ -264,23 +280,21 @@
     win_t_in,
     wout_t_in,
     psel_in,
-    split_in,
     merge_in,
     result_out,
-    wide_ref,
+    wide_out,
     gz_out,
     fields_ref,
     recv_ref,
-    og_ref,
     win_ref,
     wout_ref,
     win_t_ref,
     wout_t_ref,
     psel_ref,
-    split_ref,
     merge_ref,
     result_ref,
     gz_ref,
+    wide_ref,
     mid_ref,
     side_ref,
     q_ref,
@@ -309,8 +323,8 @@
         copy.wait()
     copies = fetch(
         [
-            (og_in, og_ref),
-            (split_in, split_ref),
+            (x_in, x_ref),
+            (o_in, o_ref),
             (win_in, win_ref),
             (wout_in, wout_ref),
             (win_t_in, win_t_ref),
@@ -328,7 +342,7 @@
         axis=0,
     )
     outer = 6 * T * N
-    row = jnp.broadcast_to(row_ref[...], (8, row_ref.shape[1])).T[:, 0:1]
+    row = column_of(row_ref[...])
     columns = lax.broadcasted_iota(jnp.int32, (row.shape[0], SENT + LOCAL), 1)
     pick = jnp.where(columns == row, 1.0, 0.0).astype(BF)
     rims = dot(pick, source)
@@ -356,22 +370,6 @@
 
     for i in range((N + 6) // 2):
         pairs(i, 0)
-
-    copies[0].wait()
-    copies[1].wait()
-
-    def order(m, carry):
-        for t in range(T):
-            rows = pl.ds(m * 8, 8)
-            for src, dst in ((fields_ref, x_ref), (og_ref, o_ref)):
-                block = src[t, rows].reshape(256, C)
-                dst[rows, t * 32 : (t + 1) * 32] = (
-                    dot(split_ref[...], block).astype(BF).reshape(8, 32, C)
-                )
-        return carry
-
-    for m in range(4):
-        order(m, 0)
 
     def conv(m, carry):
         for h in range(2):
@@ -391,7 +389,7 @@
 
     lax.fori_loop(0, 4, conv, 0)
 
-    for copy in copies[2:]:
+    for copy in copies:
         copy.wait()
     gwin_ref[...] = jnp.zeros_like(gwin_ref)
     gwout_ref[...] = jnp.zeros_like(gwout_ref)
@@ -452,7 +450,17 @@
 
     for m in range(4):
         unorder(m, 0)
-    copies = fetch([(result_ref, result_out), (gz_ref, gz_out)], sems)
+    half = wide_ref.shape[0] // 2
+    wide_ref[:half, 0:256] = gwout_ref[...].T.astype(BF).reshape(half, 256, C)
+    wide_ref[half:, 0:256] = gwin_ref[...].T.astype(BF).reshape(half, 256, C)
+    copies = fetch(
+        [
+            (wide_ref.at[:, 0:256], wide_out.at[:, 0:256]),
+            (result_ref, result_out),
+            (gz_ref, gz_out),
+        ],
+        sems,
+    )
 
     for h in range(2):
         gt_ref[h] = g_ref[h].reshape(1024, 256).T
@@ -489,11 +497,9 @@
         ],
         axis=0,
     )
-    half = wide_ref.shape[0] // 2
-    wide_ref[:half, 0:256] = gwout_ref[...].T.astype(BF).reshape(half, 256, C)
-    wide_ref[half:, 0:256] = gwin_ref[...].T.astype(BF).reshape(half, 256, C)
     blank = jnp.zeros((8, 8, C), F32)
     wide_ref[:, 256:272] = jnp.concatenate([small_ref[...], blank], axis=1).astype(BF)
+    copies += fetch([(wide_ref.at[:, 256:272], wide_out.at[:, 256:272])], sems.at[3:4])
     for copy in copies:
         copy.wait()
 
@@ -754,11 +760,15 @@
         out_specs=vm,
         vmem=60,
     )(x, pixels[:, None])
+    split = split_columns()
+    ordered = shape((N, 64, C), BF)
+    x_ord, og_ord = call(order_kernel, (ordered, ordered), flops=3_000_000_000)(
+        x, og, split.astype(BF)
+    )
     got = swap(sent, "face")
     routed = dot(pick, got.reshape(-1, C)).astype(BF).reshape(got.shape)
     got = swap(routed, "face")
 
-    split = split_columns()
     result, wide, gz = call(
         forward_kernel,
         (
@@ -769,16 +779,15 @@
         scratch=(
             pltpu.VMEM((T, N, N, C), BF),
             pltpu.VMEM((PARTS, KB, C), BF),
-            pltpu.VMEM((T, N, N, C), BF),
             pltpu.VMEM((C, HID), BF),
             pltpu.VMEM((HID, C), BF),
             pltpu.VMEM((HID, C), BF),
             pltpu.VMEM((C, HID), BF),
             pltpu.VMEM((512, 4 * (N + SIDE)), BF),
             pltpu.VMEM((256, 256), BF),
-            pltpu.VMEM((256, 256), BF),
             pltpu.VMEM((T, N, N, C), BF),
             pltpu.VMEM((N + 2, 64, C), BF),
+            pltpu.VMEM((reps, 272, C), BF),
             pltpu.VMEM((N + 6, T, N, C), BF),
             pltpu.VMEM((N + 6, T * SIDE, C), BF),
             pltpu.VMEM((2, N + 6, 32, 1024), BF),
@@ -794,13 +803,14 @@
             pltpu.VMEM((8, 8, C), F32),
             pltpu.SemaphoreType.DMA((7,)),
         ),
-        in_specs=[hbm] * 3 + [vm] * 4 + [hbm] * 7,
-        out_specs=(hbm, vm, hbm),
+        in_specs=[hbm] * 4 + [vm] * 4 + [hbm] * 6,
+        out_specs=(hbm, hbm, hbm),
         flops=40_000_000_000,
         vmem=60,
     )(
         x,
-        og,
+        x_ord,
+        og_ord,
         got,
         rim_rows[None],
         taps,
@@ -811,7 +821,6 @@
         w_in.T,
         w_out.T,
         pair_selector().astype(BF),
-        split.astype(BF),
         split.T.astype(BF),
     )
 

time: 148 us -> 147 us (level)
  waiting for transfers between devices: 39.6 us -> 34.8 us
  local copies, waits for them, and re-layouts: 6.79 us -> 10.9 us
    all_to_all x6, waiting for transfers between devices: 39.6 us -> 34.8 us  [swap(): return lax.all_to_all(array, axes, 0, 0, tiled=True)]
    unnamed x46 -> x58, local copies, waits for them, and re-layouts: 5.33 us -> 9.48 us
  transfers between devices with their start and end apart: 6 -> 6, of which waited for: 6 -> 6; matrix products, arithmetic and copies ran while one was open for 3% -> 3% of each run, Pallas kernels for 14% -> 15%
where the time goes in v5:
time: 147 us; the launch traced here: 146 us
  Pallas kernels  61.6 us (42%)
  waiting for transfers between devices  34.8 us (24%)
  starting transfers between devices  34.4 us (23%)
  local copies, waits for them, and re-layouts  10.9 us (7%)
  other arithmetic  1.55 us (1%)
    all_to_all x6, waiting for transfers between devices, swap(): return lax.all_to_all(array, axes, 0, 0, tiled=True)  34.8 us
    all_to_all x6, starting transfers between devices, swap(): return lax.all_to_all(array, axes, 0, 0, tiled=True)  34.4 us
    pallas_call x1, Pallas kernels, body(): call(forward_kernel, (shape((T, N, N, C), BF), shape((reps, 272, C), BF),...  31.5 us
    pallas_call x2, Pallas kernels, body(): call(functools.partial(inside_kernel, h), shape((T, N, N, HALF), F32), sc...  12.8 us
    unnamed x58, local copies, waits for them, and re-layouts  9.48 us
    pallas_call x1, Pallas kernels, body(): call(rims_kernel, (shape((PARTS, KB, C), BF), shape((2, 3, N, C), F32)),...  6.42 us
    pallas_call x1, Pallas kernels, body(): call(pack_kernel, shape((PARTS, KB, C), BF), scratch=(pltpu.VMEM((T, N, N...  3.19 us
  transfers between devices with their start and end apart: 6, of which 6 were waited for; matrix products, arithmetic and copies ran while one was open for 3% of the time, Pallas kernels for 15%

profile of v5, /device:TPU:1, one launch (start us, length us, event | category | flops | bytes accessed | tf_op | source)
XLA Modules:
  0.0 145.7 jit_solution(5275463113498810292)
XLA Ops:
  0.7 0.0 copy-start.18
  0.7 0.0 copy-start.24
  0.7 0.0 copy-start.25
  0.7 3.2 %shard_map.307 = bf16[16,48,256]{2,1,0:T(8,128)(2,1)} custom-call(bf16[2,32,32,256]{3,2,1,0:T(8,128)(2,1)} %bitcast.24, s32[768,1]{1,0:T(8,128)} %constant.171.clone.pixel_in), custom_call_target="tpu_custom_call" | custom-call | tf_op jit(solution)/shard_map/pallas_call | solution.py:751
  3.9 8.6 %all-to-all-start = ((bf16[16,48,256]{2,1,0:T(8,128)(2,1)}), bf16[16,48,256]{2,1,0:T(8,128)(2,1)S(1)}, u32[]{:S(2)}, u32[]{:S(2)}) async-start(bf16[16,48,256]{2,1,0:T(8,128)(2,1)} %shard_map.307), calls=%async_computation | async-start | bytes 786432 | tf_op jit(solution)/shard_map/all_to_all | solution.py:700
  12.5 0.1 add.179
  12.7 0.1 constant_dynamic-slice_fusion
  12.8 0.1 copy.88
  12.9 0.1 mul.68
  13.0 0.1 add.203
  13.0 0.1 copy.82
  13.1 0.1 add.175
  13.2 0.1 copy.77
  13.3 0.1 add.192
  13.4 0.1 copy.80
  13.5 0.1 copy.78
  13.6 0.1 multiply_reduce_fusion
  13.7 0.1 broadcast_add_fusion
  13.8 0.0 copy-start.17
  13.8 0.1 copy.87
  13.9 0.1 copy.85
  14.0 0.1 copy.83
  14.1 0.1 concatenate.6
  14.2 0.1 eq.74
  14.2 1.0 copy.89
  15.2 1.0 copy.90
  16.3 0.1 multiply_reduce_fusion.1
  16.4 0.6 compare_select_fusion.1
  17.0 3.8 %all-to-all-done = bf16[16,48,256]{2,1,0:T(8,128)(2,1)S(1)} async-done(((bf16[16,48,256]{2,1,0:T(8,128)(2,1)}), bf16[16,48,256]{2,1,0:T(8,128)(2,1)S(1)}, u32[]{:S(2)}, u32[]{:S(2)}) %all-to-all-start) | async-done | bytes 393248 | tf_op jit(solution)/shard_map/all_to_all | solution.py:700
  20.8 1.3 fusion.1
  22.1 4.1 %all-to-all-start.1 = ((bf16[16,48,256]{2,1,0:T(8,128)(2,1)}), bf16[16,48,256]{2,1,0:T(8,128)(2,1)S(1)}, u32[]{:S(2)}, u32[]{:S(2)}) async-start(bf16[16,48,256]{2,1,0:T(8,128)(2,1)} %bitcast.6), calls=%async_computation.1 | async-start | bytes 786432 | tf_op jit(solution)/shard_map/all_to_all | solution.py:700
  26.2 0.6 pad_convert_fusion.kern_ref
  26.8 0.7 shard_map.306
  27.6 0.0 copy-start.7
  27.6 1.0 copy-done.7
  28.5 1.0 copy-done.8
  29.5 4.7 %all-to-all-done.1.recv_in = bf16[16,48,256]{2,1,0:T(8,128)(2,1)S(1)} async-done(((bf16[16,48,256]{2,1,0:T(8,128)(2,1)}), bf16[16,48,256]{2,1,0:T(8,128)(2,1)S(1)}, u32[]{:S(2)}, u32[]{:S(2)}) %all-to-all-start.1) | async-done | bytes 393248 | tf_op jit(solution)/shard_map/all_to_all | solution.py:700
  34.2 0.7 copy-done.16
  34.9 31.5 %shard_map.308 = (bf16[2,32,32,256]{3,2,1,0:T(8,128)(2,1)}, bf16[8,272,256]{2,1,0:T(8,128)(2,1)}, bf16[34,64,256]{2,1,0:T(8,128)(2,1)}) custom-call(bf16[2,32,32,256]{3,2,1,0:T(8,128)(2,1)} %bitcast.25, bf16[32,64,256]{2,1,0:T(8,128)(2,1)} %copy-done.7, bf16[32,64,256]{2,1,0:T(8,128)(2,1)} %copy-done.8, bf16[16,48,256]{2,1,0:T(8,128)(2,1)} %copy-done.16, ...), custom_call_target="tpu_custom_call" | custom-call | flops 40000000000 | bytes 10000000 | tf_op jit(solution)/shard_map/pallas_call | solution.py:772
  66.4 0.0 copy-start.1
  66.5 0.0 copy-start.3
  66.5 0.0 copy-start.5
  66.5 7.9 %all-to-all-start.2 = ((bf16[8,272,256]{2,1,0:T(8,128)(2,1)}), bf16[8,272,256]{2,1,0:T(8,128)(2,1)S(1)}, u32[]{:S(2)}, u32[]{:S(2)}) async-start(bf16[8,272,256]{2,1,0:T(8,128)(2,1)} %get-tuple-element.27), calls=%async_computation.2 | async-start | bytes 2228224 | tf_op jit(solution)/shard_map/all_to_all | solution.py:700
  74.4 1.2 copy-done.11
  75.7 6.4 %shard_map.311 = (bf16[16,48,256]{2,1,0:T(8,128)(2,1)S(1)}, f32[2,3,32,256]{3,2,1,0:T(8,128)S(1)}) custom-call(bf16[34,64,256]{2,1,0:T(8,128)(2,1)S(1)} %copy-done.11, f32[7,8,256]{2,1,0:T(8,128)S(1)} %copy-done.1, s32[1,1024]{1,0:T(1,128)S(1)} %bitcast.27, bf16[768,192]{1,0:T(8,128)(2,1)S(1)} %copy-done.3, bf16[128,128]{1,0:T(8,128)(2,1)S(1)} %copy-done.5), custom_call_target="tpu_custom_call" | custom-call | flops 12000000000 | bytes 10000000 | tf_op jit(solution)/shard_map/pallas_call | solution.py:829
  82.1 8.1 %all-to-all-done.2.wide_ref = bf16[8,272,256]{2,1,0:T(8,128)(2,1)S(1)} async-done(((bf16[8,272,256]{2,1,0:T(8,128)(2,1)}), bf16[8,272,256]{2,1,0:T(8,128)(2,1)S(1)}, u32[]{:S(2)}, u32[]{:S(2)}) %all-to-all-start.2) | async-done | bytes 1114144 | tf_op jit(solution)/shard_map/all_to_all | solution.py:700
  90.2 1.0 shard_map.312
  91.2 3.6 %all-to-all-start.3 = ((bf16[16,80,256]{2,1,0:T(8,128)(2,1)}), bf16[16,80,256]{2,1,0:T(8,128)(2,1)S(1)}, u32[]{:S(2)}, u32[]{:S(2)}) async-start(bf16[16,80,256]{2,1,0:T(8,128)(2,1)} %shard_map.312), calls=%async_computation.3 | async-start | bytes 1310720 | tf_op jit(solution)/shard_map/all_to_all | solution.py:700
  94.8 0.1 broadcast_in_dim_reshape.4.source_ref
  94.9 11.5 %all-to-all-done.3.got_ref = bf16[16,80,256]{2,1,0:T(8,128)(2,1)S(1)} async-done(((bf16[16,80,256]{2,1,0:T(8,128)(2,1)}), bf16[16,80,256]{2,1,0:T(8,128)(2,1)S(1)}, u32[]{:S(2)}, u32[]{:S(2)}) %all-to-all-start.3) | async-done | bytes 655392 | tf_op jit(solution)/shard_map/all_to_all | solution.py:700
  106.4 1.3 shard_map.313
  107.7 3.6 %all-to-all-start.4 = ((bf16[16,64,256]{2,1,0:T(8,128)(2,1)}), bf16[16,64,256]{2,1,0:T(8,128)(2,1)S(1)}, u32[]{:S(2)}, u32[]{:S(2)}) async-start(bf16[16,64,256]{2,1,0:T(8,128)(2,1)} %get-tuple-element.28), calls=%async_computation.4 | async-start | bytes 1048576 | tf_op jit(solution)/shard_map/all_to_all | solution.py:700
  111.3 1.2 copy-done.12
  112.5 6.4 %shard_map.310.inner1_ref = f32[2,32,32,128]{3,2,1,0:T(8,128)S(1)} custom-call(bf16[34,64,256]{2,1,0:T(8,128)(2,1)S(1)} %copy-done.12, f32[7,8,256]{2,1,0:T(8,128)S(1)} %copy-done.1, bf16[768,192]{1,0:T(8,128)(2,1)S(1)} %copy-done.3), custom_call_target="tpu_custom_call" | custom-call | flops 8999999488 | bytes 10000000 | tf_op jit(solution)/shard_map/pallas_call | solution.py:842
  118.9 0.0 copy-start.9
  118.9 1.0 copy-done.9
  119.9 0.6 all-to-all-done.4.recv_ref.got_ref
  120.4 1.1 shard_map.315
  121.5 6.7 %all-to-all-start.5 = ((bf16[8,272,256]{2,1,0:T(8,128)(2,1)}), bf16[8,272,256]{2,1,0:T(8,128)(2,1)S(1)}, u32[]{:S(2)}, u32[]{:S(2)}) async-start(bf16[8,272,256]{2,1,0:T(8,128)(2,1)} %shard_map.315), calls=%async_computation.5 | async-start | bytes 2228224 | tf_op jit(solution)/shard_map/all_to_all | solution.py:700
  128.2 1.2 copy-done.13
  129.4 6.4 %shard_map.309.inner0_ref = f32[2,32,32,128]{3,2,1,0:T(8,128)S(1)} custom-call(bf16[34,64,256]{2,1,0:T(8,128)(2,1)S(1)} %copy-done.13, f32[7,8,256]{2,1,0:T(8,128)S(1)} %copy-done.1, bf16[768,192]{1,0:T(8,128)(2,1)S(1)} %copy-done.3), custom_call_target="tpu_custom_call" | custom-call | flops 8999999488 | bytes 10000000 | tf_op jit(solution)/shard_map/pallas_call | solution.py:842
  135.8 2.0 %shard_map.314 = bf16[2,32,32,256]{3,2,1,0:T(8,128)(2,1)} custom-call(f32[2,32,32,128]{3,2,1,0:T(8,128)S(1)} %shard_map.309.inner0_ref, f32[2,32,32,128]{3,2,1,0:T(8,128)S(1)} %copy-done.10, f32[2,3,32,256]{3,2,1,0:T(8,128)S(1)} %get-tuple-element.25.near_ref, bf16[2,32,32,256]{3,2,1,0:T(8,128)(2,1)S(1)} %bitcast.29, ...), custom_call_target="tpu_custom_call" | custom-call | flops 5000000000 | bytes 10000000 | tf_op jit(solution)/shard_map/pallas_call | solution.py:866
  137.8 6.2 %all-to-all-done.5.got_ref = bf16[8,272,256]{2,1,0:T(8,128)(2,1)S(1)} async-done(((bf16[8,272,256]{2,1,0:T(8,128)(2,1)}), bf16[8,272,256]{2,1,0:T(8,128)(2,1)S(1)}, u32[]{:S(2)}, u32[]{:S(2)}) %all-to-all-start.5) | async-done | bytes 1114144 | tf_op jit(solution)/shard_map/all_to_all | solution.py:700
  144.0 1.7 %shard_map.316 = (f32[1024,256]{1,0:T(8,128)}, f32[256,1024]{1,0:T(8,128)}, f32[7,7,256]{2,1,0:T(8,128)}, f32[1,256]{1,0:T(1,128)}, f32[1,256]{1,0:T(1,128)}) custom-call(bf16[8,272,256]{2,1,0:T(8,128)(2,1)S(1)} %all-to-all-done.5.got_ref), custom_call_target="tpu_custom_call" | custom-call | tf_op jit(solution)/shard_map/pallas_call | solution.py:869
  (53 shorter events, 0.2 us)
Async XLA Ops:
  0.6 12.0 %copy-start.21 = (s32[32,4]{0,1:T(4,128)S(1)}, s32[32,4]{0,1:T(4,128)}, u32[]{:S(2)}) copy-start(s32[32,4]{0,1:T(4,128)} %param.35) | copy-start | bytes 1540
  0.6 12.0 %copy-start.27 = (s32[32,4]{0,1:T(4,128)S(1)}, s32[32,4]{0,1:T(4,128)}, u32[]{:S(2)}) copy-start(s32[32,4]{0,1:T(4,128)} %param.34) | copy-start | bytes 1540
  0.7 12.0 %copy-start.20 = (s32[32,4]{0,1:T(4,128)S(1)}, s32[32,4]{0,1:T(4,128)}, u32[]{:S(2)}) copy-start(s32[32,4]{0,1:T(4,128)} %param.37) | copy-start | bytes 1540
  0.7 12.0 %copy-start.26 = (s32[32,4]{0,1:T(4,128)S(1)}, s32[32,4]{0,1:T(4,128)}, u32[]{:S(2)}) copy-start(s32[32,4]{0,1:T(4,128)} %param.36) | copy-start | bytes 1540
  0.7 13.0 %copy-start.18 = (s32[1024,16]{0,1:T(8,128)S(1)}, s32[1024,16]{0,1:T(8,128)}, u32[]{:S(2)}) copy-start(s32[1024,16]{0,1:T(8,128)} %constant.168.clone) | copy-start | bytes 196612
  0.7 13.1 %copy-start.24 = (s32[1024]{0:T(1024)S(1)}, s32[1024]{0:T(1024)}, u32[]{:S(2)}) copy-start(s32[1024]{0:T(1024)} %constant.170.clone) | copy-start | bytes 12292
  0.7 13.1 %copy-start.25 = (s32[1024]{0:T(1024)S(1)}, s32[1024]{0:T(1024)}, u32[]{:S(2)}) copy-start(s32[1024]{0:T(1024)} %constant.169.clone) | copy-start | bytes 12292
  0.7 13.5 %copy-start.14 = (bf16[256,1024]{1,0:T(8,128)(2,1)S(1)}, bf16[256,1024]{1,0:T(8,128)(2,1)}, u32[]{:S(2)}) copy-start(bf16[256,1024]{1,0:T(8,128)(2,1)} %win_in.1) | copy-start | bytes 1572868
  3.9 11.3 %copy-start.15 = (bf16[1024,256]{1,0:T(8,128)(2,1)S(1)}, bf16[1024,256]{1,0:T(8,128)(2,1)}, u32[]{:S(2)}) copy-start(bf16[1024,256]{1,0:T(8,128)(2,1)} %wout_in.1) | copy-start | bytes 1572868
  3.9 16.8 %all-to-all-start = ((bf16[16,48,256]{2,1,0:T(8,128)(2,1)}), bf16[16,48,256]{2,1,0:T(8,128)(2,1)S(1)}, u32[]{:S(2)}, u32[]{:S(2)}) async-start(bf16[16,48,256]{2,1,0:T(8,128)(2,1)} %shard_map.307), calls=%async_computation | async-start | bytes 786432 | tf_op jit(solution)/shard_map/all_to_all | solution.py:700
  13.8 2.4 %copy-start.17 = (s32[992,16]{0,1:T(8,128)S(1)}, s32[992,16]{0,1:T(8,128)}, u32[]{:S(2)}) copy-start(s32[992,16]{0,1:T(8,128)} %constant.165.clone) | copy-start | bytes 190468
  14.1 2.3 %copy-start.22 = (s32[992]{0:T(1024)S(1)}, s32[992]{0:T(1024)}, u32[]{:S(2)}) copy-start(s32[992]{0:T(1024)} %constant.167.clone) | copy-start | bytes 11908
  14.1 2.3 %copy-start.23 = (s32[992]{0:T(1024)S(1)}, s32[992]{0:T(1024)}, u32[]{:S(2)}) copy-start(s32[992]{0:T(1024)} %constant.166.clone) | copy-start | bytes 11908
  20.8 5.4 %copy-start.19 = (bf16[7,7,256]{2,1,0:T(8,128)(2,1)S(1)}, bf16[7,7,256]{2,1,0:T(8,128)(2,1)}, u32[]{:S(2)}) copy-start(bf16[7,7,256]{2,1,0:T(8,128)(2,1)} %param.29) | copy-start | bytes 75268
  20.8 6.1 %copy-start = (bf16[1,2,32,32,256]{4,3,2,1,0:T(8,128)(2,1)S(1)}, bf16[1,2,32,32,256]{4,3,2,1,0:T(8,128)(2,1)}, u32[]{:S(2)}) copy-start(bf16[1,2,32,32,256]{4,3,2,1,0:T(8,128)(2,1)} %param.27) | copy-start | bytes 3145732
  20.8 6.1 %copy-start.2 = (bf16[1,2,32,32,256]{4,3,2,1,0:T(8,128)(2,1)S(1)}, bf16[1,2,32,32,256]{4,3,2,1,0:T(8,128)(2,1)}, u32[]{:S(2)}) copy-start(bf16[1,2,32,32,256]{4,3,2,1,0:T(8,128)(2,1)} %param.28) | copy-start | bytes 3145732
  20.8 6.1 %copy-start.4 = (bf16[256,256]{1,0:T(8,128)(2,1)S(1)}, bf16[256,256]{1,0:T(8,128)(2,1)}, u32[]{:S(2)}) copy-start(bf16[256,256]{1,0:T(8,128)(2,1)} %constant.172.clone.split_ref) | copy-start | bytes 393220
  22.1 12.1 %all-to-all-start.1 = ((bf16[16,48,256]{2,1,0:T(8,128)(2,1)}), bf16[16,48,256]{2,1,0:T(8,128)(2,1)S(1)}, u32[]{:S(2)}, u32[]{:S(2)}) async-start(bf16[16,48,256]{2,1,0:T(8,128)(2,1)} %bitcast.6), calls=%async_computation.1 | async-start | bytes 786432 | tf_op jit(solution)/shard_map/all_to_all | solution.py:700
  27.6 1.0 copy-start.7
  28.5 1.0 copy-start.8
  34.2 0.7 copy-start.16
  66.4 8.0 %copy-start.1 = (f32[7,8,256]{2,1,0:T(8,128)S(1)}, f32[7,8,256]{2,1,0:T(8,128)}, u32[]{:S(2)}) copy-start(f32[7,8,256]{2,1,0:T(8,128)} %pad_convert_fusion.kern_ref) | copy-start | bytes 172036
  66.5 7.9 %copy-start.3 = (bf16[768,192]{1,0:T(8,128)(2,1)S(1)}, bf16[768,192]{1,0:T(8,128)(2,1)}, u32[]{:S(2)}) copy-start(bf16[768,192]{1,0:T(8,128)(2,1)} %constant.175.clone.gsel_ref) | copy-start | bytes 884740
  66.5 7.9 %copy-start.5 = (bf16[128,128]{1,0:T(8,128)(2,1)S(1)}, bf16[128,128]{1,0:T(8,128)(2,1)}, u32[]{:S(2)}) copy-start(bf16[128,128]{1,0:T(8,128)(2,1)} %constant.176.clone.rsel_ref) | copy-start | bytes 98308
  66.5 23.7 %all-to-all-start.2 = ((bf16[8,272,256]{2,1,0:T(8,128)(2,1)}), bf16[8,272,256]{2,1,0:T(8,128)(2,1)S(1)}, u32[]{:S(2)}, u32[]{:S(2)}) async-start(bf16[8,272,256]{2,1,0:T(8,128)(2,1)} %get-tuple-element.27), calls=%async_computation.2 | async-start | bytes 2228224 | tf_op jit(solution)/shard_map/all_to_all | solution.py:700
  74.4 1.2 copy-start.11
  91.2 15.2 %all-to-all-start.3 = ((bf16[16,80,256]{2,1,0:T(8,128)(2,1)}), bf16[16,80,256]{2,1,0:T(8,128)(2,1)S(1)}, u32[]{:S(2)}, u32[]{:S(2)}) async-start(bf16[16,80,256]{2,1,0:T(8,128)(2,1)} %shard_map.312), calls=%async_computation.3 | async-start | bytes 1310720 | tf_op jit(solution)/shard_map/all_to_all | solution.py:700
  107.7 12.8 %all-to-all-start.4 = ((bf16[16,64,256]{2,1,0:T(8,128)(2,1)}), bf16[16,64,256]{2,1,0:T(8,128)(2,1)S(1)}, u32[]{:S(2)}, u32[]{:S(2)}) async-start(bf16[16,64,256]{2,1,0:T(8,128)(2,1)} %get-tuple-element.28), calls=%async_computation.4 | async-start | bytes 1048576 | tf_op jit(solution)/shard_map/all_to_all | solution.py:700
  111.3 1.2 copy-start.12
  118.9 1.0 copy-start.9
  121.5 22.5 %all-to-all-start.5 = ((bf16[8,272,256]{2,1,0:T(8,128)(2,1)}), bf16[8,272,256]{2,1,0:T(8,128)(2,1)S(1)}, u32[]{:S(2)}, u32[]{:S(2)}) async-start(bf16[8,272,256]{2,1,0:T(8,128)(2,1)} %shard_map.315), calls=%async_computation.5 | async-start | bytes 2228224 | tf_op jit(solution)/shard_map/all_to_all | solution.py:700
  128.2 1.2 copy-start.13
  129.4 6.4 %copy-start.6 = (s32[1,768]{1,0:T(1,128)S(1)}, s32[1,768]{1,0:T(1,128)}, u32[]{:S(2)}) copy-start(s32[1,768]{1,0:T(1,128)} %constant.177.clone.pixel_ref) | copy-start | bytes 9220
  129.4 6.4 %copy-start.10 = (f32[2,32,32,128]{3,2,1,0:T(8,128)S(1)}, f32[2,32,32,128]{3,2,1,0:T(8,128)}, u32[]{:S(2)}) copy-start(f32[2,32,32,128]{3,2,1,0:T(8,128)} %copy-done.9) | copy-start | bytes 3145732

commit v6 on v5

--- a/solution.py
+++ b/solution.py
@@ -857,6 +857,7 @@
     ]
     sent = call(join_kernel, shape((PARTS, KB + 32, C), BF))(sent, wide)
     got = swap(sent, "face")
+    got, inner[1] = lax.optimization_barrier((got, inner[1]))
     routed, small = call(
         return_kernel, (shape((PARTS, KB + 16, C), BF), shape((16, C), BF))
     )(got, source[None])

time: 147 us -> 146 us (level)
  blocking collectives: 0 us -> 12.6 us
  waiting for transfers between devices: 34.8 us -> 25.7 us
  starting transfers between devices: 34.4 us -> 30.8 us
    all_to_all x0 -> x1, blocking collectives: none -> 12.6 us  [swap(): return lax.all_to_all(array, axes, 0, 0, tiled=True)]
    all_to_all x6 -> x5, waiting for transfers between devices: 34.8 us -> 25.7 us  [swap(): return lax.all_to_all(array, axes, 0, 0, tiled=True)]
    all_to_all x6 -> x5, starting transfers between devices: 34.4 us -> 30.8 us  [swap(): return lax.all_to_all(array, axes, 0, 0, tiled=True)]
  transfers between devices with their start and end apart: 6 -> 5, of which waited for: 6 -> 5; matrix products, arithmetic and copies ran while one was open for 3% -> 3% of each run, Pallas kernels for 15% -> 15%
where the time goes in v6:
time: 146 us; the launch traced here: 145 us
  Pallas kernels  60.8 us (42%)
  starting transfers between devices  30.8 us (21%)
  waiting for transfers between devices  25.7 us (18%)
  blocking collectives  12.6 us (9%)
  local copies, waits for them, and re-layouts  11 us (8%)
  other arithmetic  1.54 us (1%)
    pallas_call x1, Pallas kernels, body(): call(forward_kernel, (shape((T, N, N, C), BF), shape((reps, 272, C), BF),...  31.5 us
    all_to_all x5, starting transfers between devices, swap(): return lax.all_to_all(array, axes, 0, 0, tiled=True)  30.8 us
    all_to_all x5, waiting for transfers between devices, swap(): return lax.all_to_all(array, axes, 0, 0, tiled=True)  25.7 us
    pallas_call x2, Pallas kernels, body(): call(functools.partial(inside_kernel, h), shape((T, N, N, HALF), F32), sc...  12.8 us
    all_to_all x1, blocking collectives, swap(): return lax.all_to_all(array, axes, 0, 0, tiled=True)  12.6 us
    unnamed x58, local copies, waits for them, and re-layouts  9.49 us
    pallas_call x1, Pallas kernels, body(): call(rims_kernel, (shape((PARTS, KB, C), BF), shape((2, 3, N, C), F32)),...  6.42 us
    pallas_call x1, Pallas kernels, body(): call(pack_kernel, shape((PARTS, KB, C), BF), scratch=(pltpu.VMEM((T, N, N...  3.18 us
  transfers between devices with their start and end apart: 5, of which 5 were waited for; matrix products, arithmetic and copies ran while one was open for 3% of the time, Pallas kernels for 15%

profile of v6, /device:TPU:1, one launch (start us, length us, event | category | flops | bytes accessed | tf_op | source)
XLA Modules:
  0.0 144.8 jit_solution(1070216089840764558)
XLA Ops:
  0.7 0.0 copy-start.18
  0.7 0.0 copy-start.24
  0.7 0.0 copy-start.25
  0.7 3.2 %shard_map.307 = bf16[16,48,256]{2,1,0:T(8,128)(2,1)} custom-call(bf16[2,32,32,256]{3,2,1,0:T(8,128)(2,1)} %bitcast.24, s32[768,1]{1,0:T(8,128)} %constant.171.clone.pixel_in), custom_call_target="tpu_custom_call" | custom-call | tf_op jit(solution)/shard_map/pallas_call | solution.py:751
  3.9 0.0 copy-start.14
  3.9 0.0 copy-start.15
  3.9 8.6 %all-to-all-start = ((bf16[16,48,256]{2,1,0:T(8,128)(2,1)}), bf16[16,48,256]{2,1,0:T(8,128)(2,1)S(1)}, u32[]{:S(2)}, u32[]{:S(2)}) async-start(bf16[16,48,256]{2,1,0:T(8,128)(2,1)} %shard_map.307), calls=%async_computation | async-start | bytes 786432 | tf_op jit(solution)/shard_map/all_to_all | solution.py:700
  12.5 0.1 add.179
  12.7 0.1 constant_dynamic-slice_fusion
  12.8 0.1 copy.88
  12.9 0.1 mul.68
  12.9 0.1 add.203
  13.0 0.1 copy.82
  13.1 0.1 add.175
  13.2 0.1 copy.77
  13.3 0.1 add.192
  13.4 0.1 copy.80
  13.5 0.1 copy.78
  13.6 0.1 multiply_reduce_fusion
  13.7 0.1 broadcast_add_fusion
  13.8 0.1 copy.87
  13.9 0.1 copy.85
  14.0 0.1 copy.83
  14.1 0.1 concatenate.6
  14.1 0.1 broadcast_in_dim_reshape.4.source_ref
  14.2 0.1 eq.74
  14.3 1.0 copy.89
  15.3 1.0 copy.90
  16.3 0.1 multiply_reduce_fusion.1
  16.4 0.6 compare_select_fusion.1
  17.0 3.7 %all-to-all-done = bf16[16,48,256]{2,1,0:T(8,128)(2,1)S(1)} async-done(((bf16[16,48,256]{2,1,0:T(8,128)(2,1)}), bf16[16,48,256]{2,1,0:T(8,128)(2,1)S(1)}, u32[]{:S(2)}, u32[]{:S(2)}) %all-to-all-start) | async-done | bytes 393248 | tf_op jit(solution)/shard_map/all_to_all | solution.py:700
  20.8 1.3 fusion.1
  22.1 4.1 %all-to-all-start.1 = ((bf16[16,48,256]{2,1,0:T(8,128)(2,1)}), bf16[16,48,256]{2,1,0:T(8,128)(2,1)S(1)}, u32[]{:S(2)}, u32[]{:S(2)}) async-start(bf16[16,48,256]{2,1,0:T(8,128)(2,1)} %bitcast.6), calls=%async_computation.1 | async-start | bytes 786432 | tf_op jit(solution)/shard_map/all_to_all | solution.py:700
  26.2 0.6 pad_convert_fusion.kern_ref
  26.8 0.7 shard_map.306
  27.6 0.0 copy-start.7
  27.6 1.0 copy-done.7
  28.5 1.0 copy-done.8
  29.5 4.7 %all-to-all-done.1.recv_in = bf16[16,48,256]{2,1,0:T(8,128)(2,1)S(1)} async-done(((bf16[16,48,256]{2,1,0:T(8,128)(2,1)}), bf16[16,48,256]{2,1,0:T(8,128)(2,1)S(1)}, u32[]{:S(2)}, u32[]{:S(2)}) %all-to-all-start.1) | async-done | bytes 393248 | tf_op jit(solution)/shard_map/all_to_all | solution.py:700
  34.2 0.7 copy-done.16
  34.9 31.5 %shard_map.308 = (bf16[2,32,32,256]{3,2,1,0:T(8,128)(2,1)}, bf16[8,272,256]{2,1,0:T(8,128)(2,1)}, bf16[34,64,256]{2,1,0:T(8,128)(2,1)}) custom-call(bf16[2,32,32,256]{3,2,1,0:T(8,128)(2,1)} %bitcast.25, bf16[32,64,256]{2,1,0:T(8,128)(2,1)} %copy-done.7, bf16[32,64,256]{2,1,0:T(8,128)(2,1)} %copy-done.8, bf16[16,48,256]{2,1,0:T(8,128)(2,1)} %copy-done.16, ...), custom_call_target="tpu_custom_call" | custom-call | flops 40000000000 | bytes 10000000 | tf_op jit(solution)/shard_map/pallas_call | solution.py:772
  66.4 0.0 copy-start.1
  66.4 0.0 copy-start.3
  66.5 0.0 copy-start.5
  66.5 7.9 %all-to-all-start.2 = ((bf16[8,272,256]{2,1,0:T(8,128)(2,1)}), bf16[8,272,256]{2,1,0:T(8,128)(2,1)S(1)}, u32[]{:S(2)}, u32[]{:S(2)}) async-start(bf16[8,272,256]{2,1,0:T(8,128)(2,1)} %get-tuple-element.28), calls=%async_computation.2 | async-start | bytes 2228224 | tf_op jit(solution)/shard_map/all_to_all | solution.py:700
  74.4 1.2 copy-done.11
  75.7 6.4 %shard_map.310 = (bf16[16,48,256]{2,1,0:T(8,128)(2,1)S(1)}, f32[2,3,32,256]{3,2,1,0:T(8,128)S(1)}) custom-call(bf16[34,64,256]{2,1,0:T(8,128)(2,1)S(1)} %copy-done.11, f32[7,8,256]{2,1,0:T(8,128)S(1)} %copy-done.1, s32[1,1024]{1,0:T(1,128)S(1)} %bitcast.27, bf16[768,192]{1,0:T(8,128)(2,1)S(1)} %copy-done.3, bf16[128,128]{1,0:T(8,128)(2,1)S(1)} %copy-done.5), custom_call_target="tpu_custom_call" | custom-call | flops 12000000000 | bytes 10000000 | tf_op jit(solution)/shard_map/pallas_call | solution.py:829
  82.1 8.1 %all-to-all-done.2.wide_ref = bf16[8,272,256]{2,1,0:T(8,128)(2,1)S(1)} async-done(((bf16[8,272,256]{2,1,0:T(8,128)(2,1)}), bf16[8,272,256]{2,1,0:T(8,128)(2,1)S(1)}, u32[]{:S(2)}, u32[]{:S(2)}) %all-to-all-start.2) | async-done | bytes 1114144 | tf_op jit(solution)/shard_map/all_to_all | solution.py:700
  90.2 1.0 shard_map.311
  91.2 3.6 %all-to-all-start.3 = ((bf16[16,80,256]{2,1,0:T(8,128)(2,1)}), bf16[16,80,256]{2,1,0:T(8,128)(2,1)S(1)}, u32[]{:S(2)}, u32[]{:S(2)}) async-start(bf16[16,80,256]{2,1,0:T(8,128)(2,1)} %shard_map.311), calls=%async_computation.3 | async-start | bytes 1310720 | tf_op jit(solution)/shard_map/all_to_all | solution.py:700
  94.8 1.2 copy-done.12
  96.0 6.4 %shard_map.312.inner1_ref = f32[2,32,32,128]{3,2,1,0:T(8,128)S(1)} custom-call(bf16[34,64,256]{2,1,0:T(8,128)(2,1)S(1)} %copy-done.12, f32[7,8,256]{2,1,0:T(8,128)S(1)} %copy-done.1, bf16[768,192]{1,0:T(8,128)(2,1)S(1)} %copy-done.3), custom_call_target="tpu_custom_call" | custom-call | flops 8999999488 | bytes 10000000 | tf_op jit(solution)/shard_map/pallas_call | solution.py:842
  102.4 0.0 copy-start.9
  102.4 1.0 copy-done.9
  103.4 3.0 %all-to-all-done.3.got_ref = bf16[16,80,256]{2,1,0:T(8,128)(2,1)S(1)} async-done(((bf16[16,80,256]{2,1,0:T(8,128)(2,1)}), bf16[16,80,256]{2,1,0:T(8,128)(2,1)S(1)}, u32[]{:S(2)}, u32[]{:S(2)}) %all-to-all-start.3) | async-done | bytes 655392 | tf_op jit(solution)/shard_map/all_to_all | solution.py:700
  106.4 0.5 shard_map.313
  106.9 12.6 %all_to_all.30.recv_ref.got_ref = bf16[16,64,256]{2,1,0:T(8,128)(2,1)S(1)} all-to-all(bf16[16,64,256]{2,1,0:T(8,128)(2,1)S(1)} %get-tuple-element.32), channel_id=1, replica_groups=mesh['face'=16,'rep'=8] {'face'}, dimensions={0} | all-to-all | bytes 1048576 | tf_op jit(solution)/shard_map/all_to_all | solution.py:700
  119.5 1.1 shard_map.315
  120.6 6.7 %all-to-all-start.5 = ((bf16[8,272,256]{2,1,0:T(8,128)(2,1)}), bf16[8,272,256]{2,1,0:T(8,128)(2,1)S(1)}, u32[]{:S(2)}, u32[]{:S(2)}) async-start(bf16[8,272,256]{2,1,0:T(8,128)(2,1)} %shard_map.315), calls=%async_computation.5 | async-start | bytes 2228224 | tf_op jit(solution)/shard_map/all_to_all | solution.py:700
  127.3 1.2 copy-done.13
  128.5 6.4 %shard_map.309.inner0_ref = f32[2,32,32,128]{3,2,1,0:T(8,128)S(1)} custom-call(bf16[34,64,256]{2,1,0:T(8,128)(2,1)S(1)} %copy-done.13, f32[7,8,256]{2,1,0:T(8,128)S(1)} %copy-done.1, bf16[768,192]{1,0:T(8,128)(2,1)S(1)} %copy-done.3), custom_call_target="tpu_custom_call" | custom-call | flops 8999999488 | bytes 10000000 | tf_op jit(solution)/shard_map/pallas_call | solution.py:842
  134.9 2.0 %shard_map.314 = bf16[2,32,32,256]{3,2,1,0:T(8,128)(2,1)} custom-call(f32[2,32,32,128]{3,2,1,0:T(8,128)S(1)} %shard_map.309.inner0_ref, f32[2,32,32,128]{3,2,1,0:T(8,128)S(1)} %copy-done.10, f32[2,3,32,256]{3,2,1,0:T(8,128)S(1)} %get-tuple-element.30.near_ref, bf16[2,32,32,256]{3,2,1,0:T(8,128)(2,1)S(1)} %bitcast.29, ...), custom_call_target="tpu_custom_call" | custom-call | flops 5000000000 | bytes 10000000 | tf_op jit(solution)/shard_map/pallas_call | solution.py:867
  136.9 6.2 %all-to-all-done.5.got_ref = bf16[8,272,256]{2,1,0:T(8,128)(2,1)S(1)} async-done(((bf16[8,272,256]{2,1,0:T(8,128)(2,1)}), bf16[8,272,256]{2,1,0:T(8,128)(2,1)S(1)}, u32[]{:S(2)}, u32[]{:S(2)}) %all-to-all-start.5) | async-done | bytes 1114144 | tf_op jit(solution)/shard_map/all_to_all | solution.py:700
  143.1 1.7 %shard_map.316 = (f32[1024,256]{1,0:T(8,128)}, f32[256,1024]{1,0:T(8,128)}, f32[7,7,256]{2,1,0:T(8,128)}, f32[1,256]{1,0:T(1,128)}, f32[1,256]{1,0:T(1,128)}) custom-call(bf16[8,272,256]{2,1,0:T(8,128)(2,1)S(1)} %all-to-all-done.5.got_ref), custom_call_target="tpu_custom_call" | custom-call | tf_op jit(solution)/shard_map/pallas_call | solution.py:870
  (52 shorter events, 0.2 us)
Async XLA Ops:
  0.6 12.0 %copy-start.21 = (s32[32,4]{0,1:T(4,128)S(1)}, s32[32,4]{0,1:T(4,128)}, u32[]{:S(2)}) copy-start(s32[32,4]{0,1:T(4,128)} %param.35) | copy-start | bytes 1540
  0.6 12.0 %copy-start.27 = (s32[32,4]{0,1:T(4,128)S(1)}, s32[32,4]{0,1:T(4,128)}, u32[]{:S(2)}) copy-start(s32[32,4]{0,1:T(4,128)} %param.34) | copy-start | bytes 1540
  0.7 12.0 %copy-start.20 = (s32[32,4]{0,1:T(4,128)S(1)}, s32[32,4]{0,1:T(4,128)}, u32[]{:S(2)}) copy-start(s32[32,4]{0,1:T(4,128)} %param.37) | copy-start | bytes 1540
  0.7 12.0 %copy-start.26 = (s32[32,4]{0,1:T(4,128)S(1)}, s32[32,4]{0,1:T(4,128)}, u32[]{:S(2)}) copy-start(s32[32,4]{0,1:T(4,128)} %param.36) | copy-start | bytes 1540
  0.7 12.9 %copy-start.18 = (s32[1024,16]{0,1:T(8,128)S(1)}, s32[1024,16]{0,1:T(8,128)}, u32[]{:S(2)}) copy-start(s32[1024,16]{0,1:T(8,128)} %constant.168.clone) | copy-start | bytes 196612
  0.7 13.1 %copy-start.24 = (s32[1024]{0:T(1024)S(1)}, s32[1024]{0:T(1024)}, u32[]{:S(2)}) copy-start(s32[1024]{0:T(1024)} %constant.170.clone) | copy-start | bytes 12292
  0.7 13.1 %copy-start.25 = (s32[1024]{0:T(1024)S(1)}, s32[1024]{0:T(1024)}, u32[]{:S(2)}) copy-start(s32[1024]{0:T(1024)} %constant.169.clone) | copy-start | bytes 12292
  3.9 10.4 %copy-start.14 = (bf16[256,1024]{1,0:T(8,128)(2,1)S(1)}, bf16[256,1024]{1,0:T(8,128)(2,1)}, u32[]{:S(2)}) copy-start(bf16[256,1024]{1,0:T(8,128)(2,1)} %win_in.1) | copy-start | bytes 1572868
  3.9 11.4 %copy-start.15 = (bf16[1024,256]{1,0:T(8,128)(2,1)S(1)}, bf16[1024,256]{1,0:T(8,128)(2,1)}, u32[]{:S(2)}) copy-start(bf16[1024,256]{1,0:T(8,128)(2,1)} %wout_in.1) | copy-start | bytes 1572868
  3.9 16.8 %all-to-all-start = ((bf16[16,48,256]{2,1,0:T(8,128)(2,1)}), bf16[16,48,256]{2,1,0:T(8,128)(2,1)S(1)}, u32[]{:S(2)}, u32[]{:S(2)}) async-start(bf16[16,48,256]{2,1,0:T(8,128)(2,1)} %shard_map.307), calls=%async_computation | async-start | bytes 786432 | tf_op jit(solution)/shard_map/all_to_all | solution.py:700
  13.9 2.4 %copy-start.17 = (s32[992,16]{0,1:T(8,128)S(1)}, s32[992,16]{0,1:T(8,128)}, u32[]{:S(2)}) copy-start(s32[992,16]{0,1:T(8,128)} %constant.165.clone) | copy-start | bytes 190468
  14.0 2.4 %copy-start.22 = (s32[992]{0:T(1024)S(1)}, s32[992]{0:T(1024)}, u32[]{:S(2)}) copy-start(s32[992]{0:T(1024)} %constant.167.clone) | copy-start | bytes 11908
  14.1 2.4 %copy-start.23 = (s32[992]{0:T(1024)S(1)}, s32[992]{0:T(1024)}, u32[]{:S(2)}) copy-start(s32[992]{0:T(1024)} %constant.166.clone) | copy-start | bytes 11908
  20.8 5.4 %copy-start.19 = (bf16[7,7,256]{2,1,0:T(8,128)(2,1)S(1)}, bf16[7,7,256]{2,1,0:T(8,128)(2,1)}, u32[]{:S(2)}) copy-start(bf16[7,7,256]{2,1,0:T(8,128)(2,1)} %param.29) | copy-start | bytes 75268
  20.8 6.1 %copy-start = (bf16[1,2,32,32,256]{4,3,2,1,0:T(8,128)(2,1)S(1)}, bf16[1,2,32,32,256]{4,3,2,1,0:T(8,128)(2,1)}, u32[]{:S(2)}) copy-start(bf16[1,2,32,32,256]{4,3,2,1,0:T(8,128)(2,1)} %param.27) | copy-start | bytes 3145732
  20.8 6.1 %copy-start.2 = (bf16[1,2,32,32,256]{4,3,2,1,0:T(8,128)(2,1)S(1)}, bf16[1,2,32,32,256]{4,3,2,1,0:T(8,128)(2,1)}, u32[]{:S(2)}) copy-start(bf16[1,2,32,32,256]{4,3,2,1,0:T(8,128)(2,1)} %param.28) | copy-start | bytes 3145732
  20.8 6.1 %copy-start.4 = (bf16[256,256]{1,0:T(8,128)(2,1)S(1)}, bf16[256,256]{1,0:T(8,128)(2,1)}, u32[]{:S(2)}) copy-start(bf16[256,256]{1,0:T(8,128)(2,1)} %constant.172.clone.split_ref) | copy-start | bytes 393220
  22.1 12.1 %all-to-all-start.1 = ((bf16[16,48,256]{2,1,0:T(8,128)(2,1)}), bf16[16,48,256]{2,1,0:T(8,128)(2,1)S(1)}, u32[]{:S(2)}, u32[]{:S(2)}) async-start(bf16[16,48,256]{2,1,0:T(8,128)(2,1)} %bitcast.6), calls=%async_computation.1 | async-start | bytes 786432 | tf_op jit(solution)/shard_map/all_to_all | solution.py:700
  27.6 1.0 copy-start.7
  28.5 1.0 copy-start.8
  34.2 0.7 copy-start.16
  66.4 8.0 %copy-start.1 = (f32[7,8,256]{2,1,0:T(8,128)S(1)}, f32[7,8,256]{2,1,0:T(8,128)}, u32[]{:S(2)}) copy-start(f32[7,8,256]{2,1,0:T(8,128)} %pad_convert_fusion.kern_ref) | copy-start | bytes 172036
  66.4 7.9 %copy-start.3 = (bf16[768,192]{1,0:T(8,128)(2,1)S(1)}, bf16[768,192]{1,0:T(8,128)(2,1)}, u32[]{:S(2)}) copy-start(bf16[768,192]{1,0:T(8,128)(2,1)} %constant.175.clone.gsel_ref) | copy-start | bytes 884740
  66.5 7.9 %copy-start.5 = (bf16[128,128]{1,0:T(8,128)(2,1)S(1)}, bf16[128,128]{1,0:T(8,128)(2,1)}, u32[]{:S(2)}) copy-start(bf16[128,128]{1,0:T(8,128)(2,1)} %constant.176.clone.rsel_ref) | copy-start | bytes 98308
  66.5 23.7 %all-to-all-start.2 = ((bf16[8,272,256]{2,1,0:T(8,128)(2,1)}), bf16[8,272,256]{2,1,0:T(8,128)(2,1)S(1)}, u32[]{:S(2)}, u32[]{:S(2)}) async-start(bf16[8,272,256]{2,1,0:T(8,128)(2,1)} %get-tuple-element.28), calls=%async_computation.2 | async-start | bytes 2228224 | tf_op jit(solution)/shard_map/all_to_all | solution.py:700
  74.4 1.2 copy-start.11
  91.2 15.2 %all-to-all-start.3 = ((bf16[16,80,256]{2,1,0:T(8,128)(2,1)}), bf16[16,80,256]{2,1,0:T(8,128)(2,1)S(1)}, u32[]{:S(2)}, u32[]{:S(2)}) async-start(bf16[16,80,256]{2,1,0:T(8,128)(2,1)} %shard_map.311), calls=%async_computation.3 | async-start | bytes 1310720 | tf_op jit(solution)/shard_map/all_to_all | solution.py:700
  94.8 1.2 copy-start.12
  102.4 1.0 copy-start.9
  120.6 22.5 %all-to-all-start.5 = ((bf16[8,272,256]{2,1,0:T(8,128)(2,1)}), bf16[8,272,256]{2,1,0:T(8,128)(2,1)S(1)}, u32[]{:S(2)}, u32[]{:S(2)}) async-start(bf16[8,272,256]{2,1,0:T(8,128)(2,1)} %shard_map.315), calls=%async_computation.5 | async-start | bytes 2228224 | tf_op jit(solution)/shard_map/all_to_all | solution.py:700
  127.3 1.2 copy-start.13
  128.5 6.4 %copy-start.6 = (s32[1,768]{1,0:T(1,128)S(1)}, s32[1,768]{1,0:T(1,128)}, u32[]{:S(2)}) copy-start(s32[1,768]{1,0:T(1,128)} %constant.177.clone.pixel_ref) | copy-start | bytes 9220
  128.5 6.4 %copy-start.10 = (f32[2,32,32,128]{3,2,1,0:T(8,128)S(1)}, f32[2,32,32,128]{3,2,1,0:T(8,128)}, u32[]{:S(2)}) copy-start(f32[2,32,32,128]{3,2,1,0:T(8,128)} %copy-done.9) | copy-start | bytes 3145732
